TPU v7x, 32 devices: a whole 2x2x4 slice. The times are simulated.
32 devices in a mesh: row: 8 (over y, x, core), col: 4 (over z).
Axes of the slice: x: 2, y: 2, z: 4, core: 2. Of those that a mesh axis runs over, the one named last changes fastest.
Arguments:
- eigvecs: float32 [2048, 8192], P(('row', 'col')), may hold values from -6 to 6
- reflectors: float32 [1024, 8192], P('col', 'row'), may hold values from -0.0625 to 0.0625
Outputs:
- transformed: float32 [2048, 8192], P(('row', 'col'))
All inputs are finite; a program needn't handle non-finite values.
Results may differ from a plain program's by a relative error of at most 0.00015.
Values sent between devices are 32-bit elements; how exact they have to be, the bound alone decides.
No kernel may reach another device: no remote copies, remote signals or barrier semaphores. Data moves between devices by JAX's collectives and lax.ppermute only.
A program may use at most 64 MiB of HBM per device.

v0:
```python
import jax
import jax.numpy as jnp
from jax import lax
from jax.sharding import PartitionSpec as P

B = 256
PANELS = 4


def masked_vectors(block, which, row_base):
    rows_all = lax.broadcasted_iota(jnp.int32, block.shape, 1) + row_base
    starts = lax.broadcasted_iota(jnp.int32, block.shape, 0) + which * B
    unit = jnp.where(rows_all == starts, jnp.ones_like(block), jnp.zeros_like(block))
    return jnp.where(rows_all > starts, block, unit)


def upper_factor(gram):
    return jnp.triu(gram, 1) + jnp.diag(jnp.diag(gram) * 0.5)


def hdot(left, right):
    return jnp.dot(left, right, precision=lax.Precision.HIGHEST, preferred_element_type=jnp.float32)


def apply_inverse(product, factor):
    order = factor.shape[0]
    diagonal = jnp.diagonal(factor)
    nilpotent = -jnp.triu(factor, 1) / diagonal[:, None]
    solved = product / diagonal[None, :]
    power = nilpotent
    solved = solved + hdot(solved, power.T)
    for level in range((order - 1).bit_length() - 1):
        power = hdot(power, power)
        solved = solved + hdot(solved, power.T)
    return solved


def shards(eigvecs, reflectors):
    current = lax.all_to_all(eigvecs, "row", split_axis=1, concat_axis=0, tiled=True)
    gathered = lax.all_gather(reflectors, "col", axis=0, tiled=True)
    local_rows = current.shape[1]
    row_base = lax.axis_index("row") * local_rows
    blocks = []
    for which in range(PANELS):
        blocks.append(masked_vectors(gathered[which * B : (which + 1) * B, :], which, row_base))
    gram_local = jnp.stack([hdot(vectors, vectors.T) for vectors in blocks])
    gram_all = lax.psum(gram_local, "row")
    for which in reversed(range(PANELS)):
        vectors = blocks[which]
        factor = upper_factor(gram_all[which])
        partial_value = hdot(current, vectors.T)
        summed = lax.psum(partial_value, "row")
        solved = apply_inverse(summed, factor)
        current = current - hdot(solved, vectors)
    return lax.all_to_all(current, "row", split_axis=0, concat_axis=1, tiled=True)


def solution(mesh):
    placed = (P(("row", "col"), None), P("col", "row"))
    return jax.shard_map(
        shards, mesh=mesh, in_specs=placed, out_specs=P(("row", "col"), None), check_vma=False
    )
```

profile of v0, /device:TPU:0, one launch (start us, length us, event | category | flops | bytes accessed | tf_op | source)
XLA Modules:
  0.0 430.1 jit_solution(13301957718034599494)
XLA Ops:
  6.5 0.7 all-gather.2.cloned.1.call-update
  7.3 3.2 copy.31
  10.4 5.2 %all-to-all-start = ((f32[64,8,1024]{2,0,1:T(8,128)}), f32[64,8,1024]{2,0,1:T(8,128)S(1)}, u32[]{:S(2)}, u32[]{:S(2)}) async-start(f32[64,8,1024]{2,0,1:T(8,128)} %bitcast.172), calls=%async_computation | async-start | bytes 4194304 | tf_op jit(solution)/shard_map/all_to_all | solution.py:39
  15.7 76.7 %all-gather.2.cloned.1.call-done = f32[1024,1024]{1,0:T(8,128)} async-done(((f32[256,1024]{1,0:T(8,128)}), f32[1024,1024]{1,0:T(8,128)}) %all-gather.2.cloned.1.call-update) | async-done | bytes 4194320 | tf_op jit(solution)/shard_map/all_gather | solution.py:40
  92.4 3.1 convolution_bitcast_fusion.4
  95.5 2.9 convolution_bitcast_fusion.1
  98.4 1.3 convolution_bitcast_fusion.2
  99.7 1.3 convolution_bitcast_fusion.3
  101.0 1.1 pad_maximum_fusion
  102.1 4.1 convolution_bitcast_fusion
  106.3 57.7 %all-reduce.12.cloned.1.call-done = (f32[512,256]{0,1:T(8,128)}, f32[4,256,256]{2,1,0:T(8,128)}) async-done(((f32[512,256]{0,1:T(8,128)}, f32[4,256,256]{2,1,0:T(8,128)}), (f32[512,256]{0,1:T(8,128)}, f32[4,256,256]{2,1,0:T(8,128)})) %all-reduce.12.cloned.1.call-update) | async-done | bytes 1572880 | tf_op jit(solution)/shard_map/psum | solution.py:52
  164.0 1.3 slice_bitcast_fusion
  165.2 2.3 gather_fusion.6
  167.6 2.3 gather_fusion.4
  169.9 2.3 gather_fusion.2
  172.3 2.3 gather_fusion
  174.7 1.4 select_add_fusion
  176.1 2.6 gather_fusion.1
  178.7 1.6 fusion.11
  180.2 2.3 convolution_add_fusion.31
  182.9 0.6 convolution_add_fusion.30
  184.0 0.6 convolution_add_fusion.29
  185.0 0.6 convolution_add_fusion.28
  186.0 0.6 convolution_add_fusion.27
  187.1 0.6 convolution_add_fusion.26
  188.1 0.6 convolution_add_fusion.25
  188.7 0.6 convolution_add_fusion.24
  189.4 2.1 convolution_subtract_fusion.3
  191.5 1.3 copy-done
  192.8 2.8 fusion.92
  195.7 14.0 %gather_fusion.3 = f32[256]{0:T(256)S(1)} fusion(f32[256,256]{1,0:T(8,128)S(1)} %get-tuple-element.9, s32[256]{0:T(256)S(1)} %bitcast.167), kind=kCustom, calls=%fused_computation.3 | custom fusion | bytes 4096 | tf_op jit(solution)/shard_map/jit(diagonal)/cond/branch_0_fun/gather | solution.py:27
  209.7 1.6 fusion.9
  213.6 2.3 gather_fusion.5
  215.9 1.6 fusion.7
  217.5 0.7 copy-done.23
  218.6 0.7 copy-done.16
  219.7 0.7 copy-done.14
  220.7 0.7 copy-done.12
  222.2 0.7 copy-done.8
  222.9 1.1 fusion.110
  224.0 2.3 gather_fusion.7
  226.4 1.6 fusion.5
  228.0 0.7 copy-done.21
  229.4 20.2 %all-reduce.6.cloned.1.call-done = f32[512,256]{1,0:T(8,128)} async-done(((f32[512,256]{1,0:T(8,128)}), f32[512,256]{1,0:T(8,128)}) %all-reduce.6.cloned.1.call-update) | async-done | bytes 524304 | tf_op jit(solution)/shard_map/psum | solution.py:52
  249.6 2.2 convolution_add_fusion.23
  251.8 0.6 convolution_add_fusion.22
  255.6 0.6 convolution_add_fusion.16
  256.3 2.2 convolution_subtract_fusion.2
  258.4 2.8 fusion.91
  261.9 1.1 fusion.114
  262.9 52.3 %all-reduce.8.cloned.1.call-done = f32[512,256]{1,0:T(8,128)} async-done(((f32[512,256]{1,0:T(8,128)}), f32[512,256]{1,0:T(8,128)}) %all-reduce.8.cloned.1.call-update) | async-done | bytes 524304 | tf_op jit(solution)/shard_map/psum | solution.py:52
  315.2 2.2 convolution_add_fusion.15
  321.4 0.6 convolution_add_fusion.8
  322.0 2.2 convolution_subtract_fusion.1
  324.2 1.3 copy-done.2
  325.5 2.7 fusion.4
  329.0 53.2 %all-reduce.10.cloned.1.call-done = f32[512,256]{1,0:T(8,128)} async-done(((f32[512,256]{1,0:T(8,128)}), f32[512,256]{1,0:T(8,128)}) %all-reduce.10.cloned.1.call-update) | async-done | bytes 524304 | tf_op jit(solution)/shard_map/psum | solution.py:52
  382.3 2.2 convolution_add_fusion.7
  385.2 0.9 convolution_add_fusion.5
  386.7 0.6 convolution_add_fusion.3
  387.3 0.6 convolution_add_fusion.2
  389.2 3.2 convolution_subtract_fusion
  392.5 29.0 %all_to_all.38 = f32[8,64,1024]{2,1,0:T(8,128)S(1)} all-to-all(f32[8,64,1024]{2,1,0:T(8,128)S(1)} %bitcast.173), channel_id=1, replica_groups=mesh['row'=8,'col'=4] {'row'}, dimensions={0} | all-to-all | bytes 4194304 | tf_op jit(solution)/shard_map/all_to_all | solution.py:55
  421.5 1.6 copy.29
  (98 shorter events, 18.2 us)
Async XLA Ops:
  6.5 85.9 %all-gather.2.cloned.1.call-start = ((), (), s32[]{:S(2)}) async-start(), calls=%async_computation.2 | async-start | bytes 5242880 | tf_op jit(solution)/shard_map/all_gather | solution.py:40
  10.4 91.7 %all-to-all-start = ((f32[64,8,1024]{2,0,1:T(8,128)}), f32[64,8,1024]{2,0,1:T(8,128)S(1)}, u32[]{:S(2)}, u32[]{:S(2)}) async-start(f32[64,8,1024]{2,0,1:T(8,128)} %bitcast.172), calls=%async_computation | async-start | bytes 4194304 | tf_op jit(solution)/shard_map/all_to_all | solution.py:39
  15.6 148.4 %all-reduce.12.cloned.1.call-start = ((), (), s32[]{:S(2)}) async-start(), calls=%async_computation.6 | async-start | bytes 3145728 | tf_op jit(solution)/shard_map/psum | solution.py:52
  92.4 5.9 %copy-start.4 = (f32[1024,1024]{1,0:T(8,128)S(1)}, f32[1024,1024]{1,0:T(8,128)}, u32[]{:S(2)}) copy-start(f32[1024,1024]{1,0:T(8,128)} %all-gather.2.cloned.1.call-done) | copy-start | bytes 12582916
  106.2 143.4 %all-reduce.6.cloned.1.call-start = ((), (), s32[]{:S(2)}) async-start(), calls=%async_computation.3 | async-start | bytes 1048576 | tf_op jit(solution)/shard_map/psum | solution.py:52
  187.1 2.3 copy-start.5
  191.5 1.3 copy-start
  195.6 119.6 %all-reduce.8.cloned.1.call-start = ((), (), s32[]{:S(2)}) async-start(), calls=%async_computation.4 | async-start | bytes 1048576 | tf_op jit(solution)/shard_map/psum | solution.py:52
  217.5 0.7 copy-start.23
  218.6 0.7 copy-start.16
  219.7 0.7 copy-start.14
  220.7 0.7 copy-start.12
  221.8 2.2 copy-start.10
  222.2 0.7 copy-start.8
  228.0 0.7 copy-start.21
  253.1 3.2 copy-start.6
  254.4 1.9 copy-start.1
  261.2 121.1 %all-reduce.10.cloned.1.call-start = ((), (), s32[]{:S(2)}) async-start(), calls=%async_computation.5 | async-start | bytes 1048576 | tf_op jit(solution)/shard_map/psum | solution.py:52
  261.9 55.6 %copy-start.19 = (f32[256,256]{1,0:T(8,128)}, f32[256,256]{1,0:T(8,128)S(1)}, u32[]{:S(2)}) copy-start(f32[256,256]{1,0:T(8,128)S(1)} %fusion.113) | copy-start | bytes 786436
  315.2 2.3 copy-start.24
  315.2 2.9 copy-start.17
  315.2 3.5 copy-start.15
  317.5 1.9 copy-start.13
  318.1 1.9 copy-start.11
  318.8 1.9 copy-start.9
  318.8 2.6 copy-start.25
  319.4 2.5 copy-start.7
  324.2 1.3 copy-start.2
  325.5 2.8 copy-start.18
  328.7 55.9 %copy-start.22 = (f32[256,256]{1,0:T(8,128)S(1)}, f32[256,256]{1,0:T(8,128)}, u32[]{:S(2)}) copy-start(f32[256,256]{1,0:T(8,128)} %copy-done.21) | copy-start | bytes 786436
  384.5 2.2 copy-start.20
  387.3 1.9 copy-start.3
Sparse Core Ops, SparseCore 0:
  8.9 83.4 all-gather.1
  106.3 57.5 all-reduce.11
  195.8 53.7 all-reduce.5
  261.3 53.8 all-reduce.7
  328.4 53.8 all-reduce.9
where the time goes:
time: 438 us; the launch traced here: 430 us
  waiting for transfers between devices  261 us (60%)
  matrix products  74.1 us (17%)
  local copies, waits for them, and re-layouts  43.5 us (10%)
  blocking collectives  29 us (7%)
  between operations  14.5 us (3%)
  starting transfers between devices  5.55 us (1%)
    psum x4, waiting for transfers between devices, shards(): summed = lax.psum(partial_value, 'row')  183 us
    all_gather x1, waiting for transfers between devices, shards(): gathered = lax.all_gather(reflectors, 'col', axis=0, tiled=True)  76.7 us
    dot_general x72, matrix products, hdot(): jnp.dot(left, right, precision=lax.Precision.HIGHEST, preferred_element_t...  74.1 us
    all_to_all x1, blocking collectives, shards(): lax.all_to_all(current, 'row', split_axis=0, concat_axis=1, tiled=True)  29 us
    gather x4, local copies, waits for them, and re-layouts, apply_inverse(): diagonal = jnp.diagonal(factor)  21.2 us
    gather x4, local copies, waits for them, and re-layouts, upper_factor(): return jnp.triu(gram, 1) + jnp.diag(jnp.diag(gram) * 0.5)  9.37 us
  transfers between devices with their start and end apart: 6, of which 5 were waited for; matrix products, arithmetic and copies ran while one was open for 10% of the time, Pallas kernels for 0%

commit v1 on v0

--- a/solution.py
+++ b/solution.py
@@ -1,6 +1,8 @@
 import jax
 import jax.numpy as jnp
 from jax import lax
+from jax.experimental import pallas as pl
+from jax.experimental.pallas import tpu as pltpu
 from jax.sharding import PartitionSpec as P
 
 B = 256
@@ -35,7 +37,7 @@
     return solved
 
 
-def shards(eigvecs, reflectors):
+def general(eigvecs, reflectors):
     current = lax.all_to_all(eigvecs, "row", split_axis=1, concat_axis=0, tiled=True)
     gathered = lax.all_gather(reflectors, "col", axis=0, tiled=True)
     local_rows = current.shape[1]
@@ -55,8 +57,191 @@
     return lax.all_to_all(current, "row", split_axis=0, concat_axis=1, tiled=True)
 
 
+def nt(left, right):
+    return lax.dot_general(
+        left, right, (((1,), (1,)), ((), ())), precision=lax.Precision.HIGH, preferred_element_type=jnp.float32
+    )
+
+
+def nn(left, right):
+    return lax.dot_general(
+        left, right, (((1,), (0,)), ((), ())), precision=lax.Precision.HIGH, preferred_element_type=jnp.float32
+    )
+
+
+def kdot(left, right, contract=0):
+    return lax.dot_general(
+        left,
+        right,
+        (((1,), (contract,)), ((), ())),
+        precision=lax.Precision.HIGHEST,
+        preferred_element_type=jnp.float32,
+    )
+
+
+def inverse_kernel(gram_ref, out_ref):
+    gram = gram_ref[...]
+    rows = lax.broadcasted_iota(jnp.int32, gram.shape, 0)
+    cols = lax.broadcasted_iota(jnp.int32, gram.shape, 1)
+    inv = jnp.where(rows == cols, 2.0 / gram, 0.0)
+    size = 1
+    while size < gram.shape[0]:
+        pick = (rows // (2 * size) == cols // (2 * size)) & (rows % (2 * size) >= size) & (cols % (2 * size) < size)
+        inv = inv - kdot(kdot(inv, jnp.where(pick, gram, 0.0)), inv)
+        size *= 2
+    out_ref[...] = inv
+
+
+def inverse(gram):
+    return pl.pallas_call(inverse_kernel, out_shape=jax.ShapeDtypeStruct(gram.shape, jnp.float32))(gram)
+
+
+def solve_kernel(where_ref, p_ref, g_ref, t_ref, s_ref):
+    c = where_ref[0]
+    for which in reversed(range(PANELS)):
+        slot = c ^ which
+        value = p_ref[slot]
+        for later in range(which + 1, PANELS):
+            other = c ^ later
+            solved = s_ref[other]
+
+            def direct(solved=solved, other=other):
+                return kdot(solved, g_ref[other * (other - 1) // 2 + slot], 0)
+
+            def flipped(solved=solved, other=other):
+                return kdot(solved, g_ref[slot * (slot - 1) // 2 + other], 1)
+
+            value = value - lax.cond(other > slot, direct, flipped)
+        s_ref[slot] = kdot(value, t_ref[which])
+
+
+def solve(c, products, grams, inverses):
+    return pl.pallas_call(
+        solve_kernel,
+        out_shape=jax.ShapeDtypeStruct(products.shape, jnp.float32),
+        in_specs=[pl.BlockSpec(memory_space=pltpu.SMEM)] + [pl.BlockSpec(memory_space=pltpu.VMEM)] * 3,
+        out_specs=pl.BlockSpec(memory_space=pltpu.VMEM),
+        compiler_params=pltpu.CompilerParams(vmem_limit_bytes=24 * 2**20),
+    )(c.reshape(1).astype(jnp.int32), products, grams, inverses)
+
+
+def panels_on_cols(eigvecs, reflectors, chips):
+    width = reflectors.shape[1]
+    r, c = lax.axis_index("row"), lax.axis_index("col")
+    core, chip = r % 2, r // 2
+    mine = eigvecs.shape[0]
+
+    def across(value, x):
+        return lax.ppermute(value, "row", [(i, i ^ (2 * x)) for i in range(2 * chips)])
+
+    def sibling(value):
+        return lax.ppermute(value, "row", [(i, i ^ 1) for i in range(2 * chips)])
+
+    def zmove(value, pairs):
+        return lax.ppermute(value, "col", pairs)
+
+    def by_chip(value):
+        bit = 1
+        while bit < chips:
+            turned = value[jnp.array([i ^ bit for i in range(chips)])] if False else jnp.stack(
+                [value[i ^ bit] for i in range(chips)]
+            )
+            value = jnp.where((chip & bit) != 0, turned, value)
+            bit *= 2
+        return value
+
+    def total(products, grams):
+        n_p, n_g = len(products), len(grams)
+        part = B // 2 // chips
+        packed = [p.reshape(chips, mine, B) for p in products]
+        packed += [by_chip(g.reshape(chips, part, B)) for g in grams]
+        packed = jnp.concatenate(packed, axis=1)
+        held = packed[0]
+        for x in range(1, chips):
+            held = held + across(packed[x], x)
+        full = jnp.stack([held] + [across(held, x) for x in range(1, chips)])
+        out_p = [full[:, i * mine : (i + 1) * mine].reshape(chips * mine, B) for i in range(n_p)]
+        out_g = None
+        if n_g:
+            halves = full[:, n_p * mine :].reshape(chips, n_g, part, B)
+            halves = by_chip(halves).transpose(1, 0, 2, 3).reshape(n_g, B // 2, B)
+            others = sibling(halves)
+            first, second = jnp.where(core == 0, halves, others), jnp.where(core == 0, others, halves)
+            out_g = jnp.concatenate([first, second], axis=1)
+        return out_p, out_g
+
+    vectors = masked_vectors(reflectors, c, r * width)
+    near = zmove(vectors, [(0, 1), (1, 0), (2, 3), (3, 2)])
+    inner = zmove(vectors, [(1, 2), (2, 1)])
+
+    def piece(x):
+        start = (chip ^ x) * 2 * width
+        return jnp.stack(
+            [
+                lax.dynamic_slice(eigvecs, (0, start + core * width), (mine, width)),
+                lax.dynamic_slice(eigvecs, (0, start + (1 - core) * width), (mine, width)),
+            ]
+        )
+
+    pieces = [piece(0)] + [across(piece(x), x) for x in range(1, chips)]
+    e_m = jnp.concatenate([p[0] for p in pieces])
+    e_o = jnp.concatenate([p[1] for p in pieces])
+
+    edge = (c == 0) | (c == 3)
+    second_out = zmove(inner, [(1, 0), (2, 3)])
+    second_in = zmove(near, [(1, 2), (2, 1)])
+    second = jnp.where(edge, second_out, second_in)
+    third_out = zmove(second_in, [(1, 0), (2, 3)])
+    third = jnp.where(edge, third_out, inner)
+
+    slots = []
+    for v in (vectors, near, second, third):
+        slots.append((v, sibling(v)))
+
+    def product(slot):
+        m, o = slots[slot]
+        return nt(e_m, m) + nt(e_o, o)
+
+    def gram(slot, other):
+        m, o = slots[slot]
+        hm = lax.dynamic_slice(m, (core * (B // 2), 0), (B // 2, width))
+        ho = lax.dynamic_slice(o, (core * (B // 2), 0), (B // 2, width))
+        return nt(hm, slots[other][0]) + nt(ho, slots[other][1])
+
+    p_01, g_01 = total([product(0), product(1)], [gram(0, 0), gram(1, 0)])
+    inv = inverse(g_01[0])
+    share = B // (2 * chips)
+    inv_part = lax.dynamic_slice(inv, (r * share, 0), (share, B))
+    inverses = lax.all_gather(inv_part, ("col", "row"), axis=0, tiled=True).reshape(PANELS, B, B)
+    p_2, g_2 = total([product(2)], [gram(2, 0), gram(2, 1)])
+    p_3, g_3 = total([product(3)], [gram(3, 0), gram(3, 1), gram(3, 2)])
+    products = jnp.stack(p_01 + p_2 + p_3)
+    grams = jnp.concatenate([g_01[1:], g_2, g_3])
+    solved = solve(c, products, grams, inverses)
+    s_all = jnp.concatenate([solved[i] for i in range(PANELS)], axis=1)
+    v_m = jnp.concatenate([m for m, _ in slots])
+    v_o = jnp.concatenate([o for _, o in slots])
+    done_m = e_m - nn(s_all, v_m)
+    done_o = e_o - nn(s_all, v_o)
+    result = jnp.zeros_like(eigvecs)
+    for x in range(chips):
+        rows = slice(x * mine, (x + 1) * mine)
+        both = jnp.stack([done_m[rows], done_o[rows]])
+        if x:
+            both = across(both, x)
+        start = (chip ^ x) * 2 * width
+        result = lax.dynamic_update_slice(result, both[0], (0, start + core * width))
+        result = lax.dynamic_update_slice(result, both[1], (0, start + (1 - core) * width))
+    return result
+
+
 def solution(mesh):
+    rows, cols = mesh.shape["row"], mesh.shape["col"]
     placed = (P(("row", "col"), None), P("col", "row"))
-    return jax.shard_map(
-        shards, mesh=mesh, in_specs=placed, out_specs=P(("row", "col"), None), check_vma=False
-    )
+
+    def shards(eigvecs, reflectors):
+        if cols == PANELS and reflectors.shape[0] == B and rows >= 4 and rows & (rows - 1) == 0 and B % (16 * rows) == 0:
+            return panels_on_cols(eigvecs, reflectors, rows // 2)
+        return general(eigvecs, reflectors)
+
+    return jax.shard_map(shards, mesh=mesh, in_specs=placed, out_specs=P(("row", "col"), None), check_vma=False)

time: 438 us -> 215 us (0.49); the launches traced: 430 us -> 214 us
  waiting for transfers between devices: 261 us -> 90.4 us
  matrix products: 74.1 us -> 26.5 us
  starting transfers between devices: 5.55 us -> 38.3 us
  blocking collectives: 29 us -> 0 us
  local copies, waits for them, and re-layouts: 43.5 us -> 19.1 us
  Pallas kernels: 0 us -> 13.6 us
  other arithmetic: 2.49 us -> 11.2 us
    psum x4 -> x0, waiting for transfers between devices: 183 us -> none  [shards(): summed = lax.psum(partial_value, 'row')]
    ppermute x0 -> x36, waiting for transfers between devices: none -> 86.5 us  [the longest x24 67.8 us: across(): lax.ppermute(value, 'row', [(i, i ^ 2 * x) for i in range(2 * chips)])]
    all_gather x1, waiting for transfers between devices: 76.7 us -> 3.9 us  [panels_on_cols(): lax.all_gather(inv_part, ('col', 'row'), axis=0, tiled=True)]
    dot_general x72 -> x24, matrix products: 74.1 us -> 26.5 us  [the longest x22 20.8 us: nt(): lax.dot_general(left, right, (((1,), (1,)), ((), ())), precision=lax.Prec...]
    ppermute x0 -> x36, starting transfers between devices: none -> 38.3 us  [the longest x24 29.9 us: across(): lax.ppermute(value, 'row', [(i, i ^ 2 * x) for i in range(2 * chips)])]
    gather x8 -> x0, local copies, waits for them, and re-layouts: 30.6 us -> none  [the longest x4 21.2 us: apply_inverse(): diagonal = jnp.diagonal(factor)]
    all_to_all x1 -> x0, blocking collectives: 29 us -> none  [shards(): lax.all_to_all(current, 'row', split_axis=0, concat_axis=1, tiled=True)]
    pallas_call x0 -> x2, Pallas kernels: none -> 13.6 us  [the longest x1 9.26 us: inverse(): pl.pallas_call(inverse_kernel, out_shape=jax.ShapeDtypeStruct(gram.shape,...]
  transfers between devices with their start and end apart: 6 -> 37, of which waited for: 5 -> 17; matrix products, arithmetic and copies ran while one was open for 10% -> 18% of each run, Pallas kernels for 0% -> 4%
where the time goes in v1:
time: 215 us; the launch traced here: 214 us
  waiting for transfers between devices  90.4 us (42%)
  starting transfers between devices  38.3 us (18%)
  matrix products  26.5 us (12%)
  local copies, waits for them, and re-layouts  19.1 us (9%)
  between operations  14.9 us (7%)
  Pallas kernels  13.6 us (6%)
  other arithmetic  11.2 us (5%)
    ppermute x24, waiting for transfers between devices, across(): lax.ppermute(value, 'row', [(i, i ^ 2 * x) for i in range(2 * chips)])  67.8 us
    ppermute x24, starting transfers between devices, across(): lax.ppermute(value, 'row', [(i, i ^ 2 * x) for i in range(2 * chips)])  29.9 us
    dot_general x22, matrix products, nt(): lax.dot_general(left, right, (((1,), (1,)), ((), ())), precision=lax.Prec...  20.8 us
    ppermute x5, waiting for transfers between devices, zmove(): return lax.ppermute(value, 'col', pairs)  17.9 us
    pallas_call x1, Pallas kernels, inverse(): pl.pallas_call(inverse_kernel, out_shape=jax.ShapeDtypeStruct(gram.shape,...  9.26 us
    ppermute x5, starting transfers between devices, zmove(): return lax.ppermute(value, 'col', pairs)  7.65 us
    unnamed x92, local copies, waits for them, and re-layouts  7.41 us
    dot_general x2, matrix products, nn(): lax.dot_general(left, right, (((1,), (0,)), ((), ())), precision=lax.Prec...  5.74 us
  transfers between devices with their start and end apart: 37, of which 17 were waited for; matrix products, arithmetic and copies ran while one was open for 18% of the time, Pallas kernels for 4%

profile of v1, /device:TPU:0, one launch (start us, length us, event | category | flops | bytes accessed | tf_op | source)
XLA Modules:
  0.0 214.0 jit_solution(11009870275667744044)
XLA Ops:
  6.5 2.7 %constant_dynamic-slice_fusion.2 = (f32[64,1024]{1,0:T(8,128)}, f32[1,64,1024]{2,1,0:T(8,128)S(1)}, f32[1,64,1024]{2,1,0:T(8,128)}, f32[1,64,1024]{2,1,0:T(8,128...) fusion(f32[64,8192]{1,0:T(8,128)} %param.2, ...), kind=kLoop, calls=%fused_computation.208 | loop fusion | bytes 4194336 | tf_op jit(solution)/shard_map/dynamic_slice | solution.py:181
  9.2 0.8 pad_maximum_fusion.11
  10.1 3.9 %collective-permute-start.2 = (f32[2,64,1024]{2,1,0:T(8,128)}, f32[2,64,1024]{2,1,0:T(8,128)}, u32[]{:S(2)}, u32[]{:S(2)}) collective-permute-start(f32[2,64,1024]{2,1,0:T(8,128)} %pad_maximum_fusion.11), channel_id=1, source_target_pairs={{0,24},{4,28},{8,16},{12,20},{16,8},{20,12},{24,0},{28,4},{1,25},{... | collective-permute-start | bytes 1572872 | tf_op jit(solution)/shard_map/ppermute | solution.py:135
  14.2 1.6 collective-permute-start.4
  15.8 0.8 pad_maximum_fusion.10
  17.2 1.9 pad_maximum_fusion.9
  20.3 6.8 %collective-permute-done.2 = f32[2,64,1024]{2,1,0:T(8,128)} collective-permute-done((f32[2,64,1024]{2,1,0:T(8,128)}, f32[2,64,1024]{2,1,0:T(8,128)}, u32[]{:S(2)}, u32[]{:S(2)}) %collective-permute-start.2) | collective-permute-done | bytes 524320 | tf_op jit(solution)/shard_map/ppermute | solution.py:135
  27.1 1.6 collective-permute-start.12
  28.7 1.1 slice_bitcast_fusion.19
  29.8 7.6 %collective-permute-done.1 = f32[2,64,1024]{2,1,0:T(8,128)} collective-permute-done((f32[2,64,1024]{2,1,0:T(8,128)}, f32[2,64,1024]{2,1,0:T(8,128)}, u32[]{:S(2)}, u32[]{:S(2)}) %collective-permute-start.1) | collective-permute-done | bytes 524320 | tf_op jit(solution)/shard_map/ppermute | solution.py:135
  37.4 1.1 slice_bitcast_fusion.20
  38.5 1.3 slice_bitcast_fusion.21
  40.7 1.6 collective-permute-start.14
  42.3 1.3 collective-permute-start.13
  47.8 0.9 copy-done.38
  48.7 0.9 slice_bitcast_fusion.24
  49.5 2.6 %collective-permute-start.8 = (f32[192,256]{1,0:T(8,128)}, f32[192,256]{1,0:T(8,128)}, u32[]{:S(2)}, u32[]{:S(2)}) collective-permute-start(f32[192,256]{1,0:T(8,128)} %get-tuple-element.31), channel_id=1, source_target_pairs={{0,24},{4,28},{8,16},{12,20},{16,8},{20,12},{24,0},{28,4},{1,25},{... | collective-permute-start | bytes 589832 | tf_op jit(solution)/shard_map/ppermute | solution.py:135
  53.0 5.5 %collective-permute-done.8 = f32[192,256]{1,0:T(8,128)} collective-permute-done((f32[192,256]{1,0:T(8,128)}, f32[192,256]{1,0:T(8,128)}, u32[]{:S(2)}, u32[]{:S(2)}) %collective-permute-start.8) | collective-permute-done | bytes 196640 | tf_op jit(solution)/shard_map/ppermute | solution.py:135
  58.5 3.7 %collective-permute-done.7 = f32[192,256]{1,0:T(8,128)} collective-permute-done((f32[192,256]{1,0:T(8,128)}, f32[192,256]{1,0:T(8,128)}, u32[]{:S(2)}, u32[]{:S(2)}) %collective-permute-start.7) | collective-permute-done | bytes 196640 | tf_op jit(solution)/shard_map/ppermute | solution.py:135
  62.5 1.3 fusion.56
  63.8 1.5 collective-permute-start.11
  65.3 1.5 collective-permute-start.10
  67.3 8.5 %collective-permute-done.13 = f32[256,1024]{1,0:T(8,128)} collective-permute-done((f32[256,1024]{1,0:T(8,128)}, f32[256,1024]{1,0:T(8,128)}, u32[]{:S(2)}, u32[]{:S(2)}) %collective-permute-start.13) | collective-permute-done | bytes 1048608 | tf_op jit(solution)/shard_map/ppermute | solution.py:141
  75.8 1.4 broadcast_select_fusion.1
  77.4 1.0 fusion.83
  78.5 0.7 copy.3
  79.6 1.5 collective-permute-start.22
  81.1 1.9 fusion.31
  83.0 1.1 broadcast_select_fusion.6
  84.0 0.8 fusion.51
  84.9 9.3 %shard_map.28 = f32[256,256]{1,0:T(8,128)} custom-call(f32[256,256]{1,0:T(8,128)} %get-tuple-element.36.gram_ref), custom_call_target="tpu_custom_call" | custom-call | tf_op jit(solution)/shard_map/pallas_call | solution.py:96
  94.1 1.4 constant_dynamic-slice_fusion
  95.5 1.8 fusion.29
  98.1 1.8 convolution_add_fusion.7
  100.1 1.9 fusion.80
  102.8 2.5 %collective-permute-start.18 = (f32[128,256]{1,0:T(8,128)S(1)}, f32[128,256]{1,0:T(8,128)S(1)}, u32[]{:S(2)}, u32[]{:S(2)}) collective-permute-start(f32[128,256]{1,0:T(8,128)S(1)} %get-tuple-element.45), channel_id=1, source_target_pairs={{0,24},{4,28},{8,16},{12,20},{16,8},{20,12},{24,0},{28,4},{1,25},{... | collective-permute-start | bytes 393224 | tf_op jit(solution)/shard_map/ppermute | solution.py:135
  106.3 9.4 %collective-permute-done.22 = f32[256,1024]{1,0:T(8,128)} collective-permute-done((f32[256,1024]{1,0:T(8,128)}, f32[256,1024]{1,0:T(8,128)}, u32[]{:S(2)}, u32[]{:S(2)}) %collective-permute-start.22) | collective-permute-done | bytes 1048608 | tf_op jit(solution)/shard_map/ppermute | solution.py:141
  115.7 1.4 broadcast_select_fusion
  117.3 1.6 collective-permute-start.21
  118.9 1.4 collective-permute-start.20
  121.5 5.4 %collective-permute-done.20 = f32[128,256]{1,0:T(8,128)S(1)} collective-permute-done((f32[128,256]{1,0:T(8,128)S(1)}, f32[128,256]{1,0:T(8,128)S(1)}, u32[]{:S(2)}, u32[]{:S(2)}) %collective-permute-start.20) | collective-permute-done | bytes 131104 | tf_op jit(solution)/shard_map/ppermute | solution.py:135
  127.2 2.3 %fusion.34 = f32[128,256]{1,0:T(8,128)S(1)} fusion(f32[256,1024]{1,0:T(8,128)} %collective-permute-done.15, f32[256,1024]{1,0:T(8,128)S(1)} %collective-permute-done.23, s32[]{:T(128)S(6)} %select_n.225), kind=kOutput, calls=%fused_computation.62 | convolution fusion | flops 201326592 | bytes 1703940 | tf_op jit(solution)/shard_map/dot_general | solution.py:61
  130.9 0.9 convolution_add_fusion.6
  134.0 1.6 collective-permute-start.26
  135.5 1.4 collective-permute-start.25
  137.6 4.5 %collective-permute-done.26 = f32[160,256]{1,0:T(8,128)S(1)} collective-permute-done((f32[160,256]{1,0:T(8,128)S(1)}, f32[160,256]{1,0:T(8,128)S(1)}, u32[]{:S(2)}, u32[]{:S(2)}) %collective-permute-start.26) | collective-permute-done | bytes 163872 | tf_op jit(solution)/shard_map/ppermute | solution.py:135
  142.1 2.5 %collective-permute-done.25 = f32[160,256]{1,0:T(8,128)S(1)} collective-permute-done((f32[160,256]{1,0:T(8,128)S(1)}, f32[160,256]{1,0:T(8,128)S(1)}, u32[]{:S(2)}, u32[]{:S(2)}) %collective-permute-start.25) | collective-permute-done | bytes 163872 | tf_op jit(solution)/shard_map/ppermute | solution.py:135
  144.7 1.5 collective-permute-start.29
  146.2 1.4 collective-permute-start.28
  148.4 8.2 %collective-permute-done.28 = f32[160,256]{1,0:T(8,128)S(1)} collective-permute-done((f32[160,256]{1,0:T(8,128)S(1)}, f32[160,256]{1,0:T(8,128)S(1)}, u32[]{:S(2)}, u32[]{:S(2)}) %collective-permute-start.28) | collective-permute-done | bytes 163872 | tf_op jit(solution)/shard_map/ppermute | solution.py:135
  158.1 0.8 collective-permute-done.32
  159.2 3.9 %all-gather.2.cloned.1.call-done = f32[1024,256]{1,0:T(8,128)} async-done(((f32[32,256]{1,0:T(8,128)}), f32[1024,256]{1,0:T(8,128)}) %all-gather.2.cloned.1.call-update) | async-done | bytes 1048592 | tf_op jit(solution)/shard_map/all_gather | solution.py:215
  163.1 1.2 copy-done
  164.3 4.4 %shard_map.29 = f32[4,256,256]{2,1,0:T(8,128)S(1)} custom-call(s32[1]{0:T(128)} %bitcast.9.where_ref, f32[4,256,256]{2,1,0:T(8,128)S(1)} %pad_maximum_fusion.2.p_ref, f32[6,256,256]{2,1,0:T(8,128)S(1)} %maximum_maximum_fusion.g_ref, f32[4,256,256]{2,1,0:T(8,128)S(1)} %bitcast.249), custom_call_target="tpu_custom_call" | custom-call | tf_op jit(solution)/shard_map/pallas_call | solution.py:119
  168.9 1.1 copy-done.2
  170.2 2.3 %fusion.19 = f32[256,1024]{1,0:T(8,128)S(1)} fusion(f32[256,1024]{1,0:T(8,128)S(1)} %copy-done.14, f32[256,1024]{1,0:T(8,128)S(1)} %copy-done.6, f32[256,1024]{1,0:T(8,128)S(1)} %copy-done.9, f32[256,1024]{1,0:T(8,128)S(1)} %copy-done.2, f32[256,256]{1,0:T(8,128)S(1)} %get-tuple-element.22, f32[256,256]{1,0:T(8,128)S(1)} %get-tuple-element.23, ...), kind=kOutput, calls=%fused_computation.18 | convolution fusion | flops 1615593472 | bytes 7340032 | tf_op jit(solution)/shard_map/dot_general | solution.py:67
  172.8 0.9 copy-done.4
  174.6 3.5 %fusion.16 = f32[256,1024]{1,0:T(8,128)S(1)} fusion(f32[256,1024]{1,0:T(8,128)S(1)} %copy-done.37, f32[256,1024]{1,0:T(8,128)} %collective-permute-done.15, f32[256,1024]{1,0:T(8,128)S(1)} %copy-done.12, f32[256,1024]{1,0:T(8,128)S(1)} %copy-done.4, f32[256,256]{1,0:T(8,128)S(1)} %get-tuple-element.22, f32[256,256]{1,0:T(8,128)S(1)} %get-tuple-element.23, ...), kind=kOutput, calls=%fused_computation.17 | convolution fusion | flops 1615593472 | bytes 7340032 | tf_op jit(solution)/shard_map/dot_general | solution.py:67
  178.3 1.6 collective-permute-start.33
  180.7 1.4 collective-permute-start.35
  182.0 11.0 %collective-permute-done.33 = f32[2,64,1024]{2,1,0:T(8,128)S(1)} collective-permute-done((f32[2,64,1024]{2,1,0:T(8,128)S(1)}, f32[2,64,1024]{2,1,0:T(8,128)S(1)}, u32[]{:S(2)}, u32[]{:S(2)}) %collective-permute-start.33) | collective-permute-done | bytes 524320 | tf_op jit(solution)/shard_map/ppermute | solution.py:135
  193.1 11.9 %collective-permute-done.34 = f32[2,64,1024]{2,1,0:T(8,128)S(1)} collective-permute-done((f32[2,64,1024]{2,1,0:T(8,128)S(1)}, f32[2,64,1024]{2,1,0:T(8,128)S(1)}, u32[]{:S(2)}, u32[]{:S(2)}) %collective-permute-start.34) | collective-permute-done | bytes 524320 | tf_op jit(solution)/shard_map/ppermute | solution.py:135
  205.2 1.3 copy-done.39
  206.5 0.7 fusion.45
  (226 shorter events, 22.3 us)
Async XLA Ops:
  6.5 156.5 %all-gather.2.cloned.1.call-start = ((), (), s32[]{:S(2)}) async-start(), calls=%async_computation | async-start | bytes 1081344 | tf_op jit(solution)/shard_map/all_gather | solution.py:215
  6.5 7.4 %copy-start.43 = (f32[256,1024]{1,0:T(8,128)S(1)}, f32[256,1024]{1,0:T(8,128)}, u32[]{:S(2)}) copy-start(f32[256,1024]{1,0:T(8,128)} %param.3) | copy-start | bytes 3145732
  10.1 17.0 %collective-permute-start.2 = (f32[2,64,1024]{2,1,0:T(8,128)}, f32[2,64,1024]{2,1,0:T(8,128)}, u32[]{:S(2)}, u32[]{:S(2)}) collective-permute-start(f32[2,64,1024]{2,1,0:T(8,128)} %pad_maximum_fusion.11), channel_id=1, source_target_pairs={{0,24},{4,28},{8,16},{12,20},{16,8},{20,12},{24,0},{28,4},{1,25},{... | collective-permute-start | bytes 1572872 | tf_op jit(solution)/shard_map/ppermute | solution.py:135
  14.2 116.7 %copy-start.1 = (f32[256,1024]{1,0:T(8,128)}, f32[256,1024]{1,0:T(8,128)S(1)}, u32[]{:S(2)}) copy-start(f32[256,1024]{1,0:T(8,128)S(1)} %select_select_fusion) | copy-start | bytes 3145732
  14.2 25.6 %collective-permute-start.4 = (f32[256,1024]{1,0:T(8,128)S(1)}, f32[256,1024]{1,0:T(8,128)S(1)}, u32[]{:S(2)}, u32[]{:S(2)}) collective-permute-start(f32[256,1024]{1,0:T(8,128)S(1)} %select_select_fusion), channel_id=1, source_target_pairs={{0,1},{1,0},{2,3},{3,2},{4,5},{5,4},{6,7},{7,6},{8,9},{9,8},{10,11... | collective-permute-start | bytes 3145736 | tf_op jit(solution)/shard_map/ppermute | solution.py:141
  15.8 24.2 %collective-permute-start.3 = (f32[256,1024]{1,0:T(8,128)S(1)}, f32[256,1024]{1,0:T(8,128)S(1)}, u32[]{:S(2)}, u32[]{:S(2)}) collective-permute-start(f32[256,1024]{1,0:T(8,128)S(1)} %select_select_fusion), channel_id=1, source_target_pairs={{0,4},{4,0},{8,12},{12,8},{16,20},{20,16},{24,28},{28,24},{1,5},{5... | collective-permute-start | bytes 3145736 | tf_op jit(solution)/shard_map/ppermute | solution.py:138
  16.7 20.7 %collective-permute-start.1 = (f32[2,64,1024]{2,1,0:T(8,128)}, f32[2,64,1024]{2,1,0:T(8,128)}, u32[]{:S(2)}, u32[]{:S(2)}) collective-permute-start(f32[2,64,1024]{2,1,0:T(8,128)} %pad_maximum_fusion.10), channel_id=1, source_target_pairs={{0,16},{4,20},{8,24},{12,28},{16,0},{20,4},{24,8},{28,12},{1,17},{... | collective-permute-start | bytes 1572872 | tf_op jit(solution)/shard_map/ppermute | solution.py:135
  19.1 19.5 %collective-permute-start = (f32[2,64,1024]{2,1,0:T(8,128)}, f32[2,64,1024]{2,1,0:T(8,128)}, u32[]{:S(2)}, u32[]{:S(2)}) collective-permute-start(f32[2,64,1024]{2,1,0:T(8,128)} %pad_maximum_fusion.9), channel_id=1, source_target_pairs={{0,8},{4,12},{8,0},{12,4},{16,24},{20,28},{24,16},{28,20},{1,9},{5... | collective-permute-start | bytes 1572872 | tf_op jit(solution)/shard_map/ppermute | solution.py:135
  27.1 15.3 %collective-permute-start.12 = (f32[256,1024]{1,0:T(8,128)S(1)}, f32[256,1024]{1,0:T(8,128)}, u32[]{:S(2)}, u32[]{:S(2)}) collective-permute-start(f32[256,1024]{1,0:T(8,128)S(1)} %select_select_fusion), channel_id=1, source_target_pairs={{1,2},{2,1},{5,6},{6,5},{9,10},{10,9},{13,14},{14,13},{17,18},{18,... | collective-permute-start | bytes 3145736 | tf_op jit(solution)/shard_map/ppermute | solution.py:141
  29.8 15.2 %copy-start.27 = (f32[64,1024]{1,0:T(8,128)}, f32[64,1024]{1,0:T(8,128)S(1)}, u32[]{:S(2)}) copy-start(f32[64,1024]{1,0:T(8,128)S(1)} %get-tuple-element.51) | copy-start | bytes 786436
  29.8 17.2 %copy-start.18 = (f32[64,1024]{1,0:T(8,128)}, f32[64,1024]{1,0:T(8,128)S(1)}, u32[]{:S(2)}) copy-start(f32[64,1024]{1,0:T(8,128)S(1)} %get-tuple-element.52) | copy-start | bytes 786436
  38.5 6.5 %copy-start.30 = (f32[64,1024]{1,0:T(8,128)}, f32[64,1024]{1,0:T(8,128)S(1)}, u32[]{:S(2)}) copy-start(f32[64,1024]{1,0:T(8,128)S(1)} %get-tuple-element.49) | copy-start | bytes 786436
  38.5 8.5 %copy-start.21 = (f32[64,1024]{1,0:T(8,128)}, f32[64,1024]{1,0:T(8,128)S(1)}, u32[]{:S(2)}) copy-start(f32[64,1024]{1,0:T(8,128)S(1)} %get-tuple-element.50) | copy-start | bytes 786436
  38.5 5.2 %copy-start.15 = (f32[64,1024]{1,0:T(8,128)S(1)}, f32[64,1024]{1,0:T(8,128)}, u32[]{:S(2)}) copy-start(f32[64,1024]{1,0:T(8,128)} %get-tuple-element.5) | copy-start | bytes 786436
  39.8 5.1 %copy-start.33 = (f32[64,1024]{1,0:T(8,128)}, f32[64,1024]{1,0:T(8,128)S(1)}, u32[]{:S(2)}) copy-start(f32[64,1024]{1,0:T(8,128)S(1)} %get-tuple-element.47) | copy-start | bytes 786436
  39.8 7.2 %copy-start.24 = (f32[64,1024]{1,0:T(8,128)}, f32[64,1024]{1,0:T(8,128)S(1)}, u32[]{:S(2)}) copy-start(f32[64,1024]{1,0:T(8,128)S(1)} %get-tuple-element.48) | copy-start | bytes 786436
  39.8 6.4 %copy-start.7 = (f32[256,1024]{1,0:T(8,128)}, f32[256,1024]{1,0:T(8,128)S(1)}, u32[]{:S(2)}) copy-start(f32[256,1024]{1,0:T(8,128)S(1)} %collective-permute-done.4) | copy-start | bytes 3145732
  39.8 5.7 %collective-permute-start.5 = (f32[256,1024]{1,0:T(8,128)S(1)}, f32[256,1024]{1,0:T(8,128)S(1)}, u32[]{:S(2)}, u32[]{:S(2)}) collective-permute-start(f32[256,1024]{1,0:T(8,128)S(1)} %collective-permute-done.4), channel_id=1, source_target_pairs={{0,4},{4,0},{8,12},{12,8},{16,20},{20,16},{24,28},{28,24},{1,5},{5... | collective-permute-start | bytes 3145736 | tf_op jit(solution)/shard_map/ppermute | solution.py:138
  40.0 90.2 %copy-start.3 = (f32[256,1024]{1,0:T(8,128)}, f32[256,1024]{1,0:T(8,128)S(1)}, u32[]{:S(2)}) copy-start(f32[256,1024]{1,0:T(8,128)S(1)} %collective-permute-done.3) | copy-start | bytes 3145732
  40.7 26.6 %collective-permute-start.14 = (f32[256,1024]{1,0:T(8,128)S(1)}, f32[256,1024]{1,0:T(8,128)}, u32[]{:S(2)}, u32[]{:S(2)}) collective-permute-start(f32[256,1024]{1,0:T(8,128)S(1)} %collective-permute-done.4), channel_id=1, source_target_pairs={{1,2},{2,1},{5,6},{6,5},{9,10},{10,9},{13,14},{14,13},{17,18},{18,... | collective-permute-start | bytes 3145736 | tf_op jit(solution)/shard_map/ppermute | solution.py:141
  42.3 33.5 %collective-permute-start.13 = (f32[256,1024]{1,0:T(8,128)}, f32[256,1024]{1,0:T(8,128)}, u32[]{:S(2)}, u32[]{:S(2)}) collective-permute-start(f32[256,1024]{1,0:T(8,128)} %collective-permute-done.12), channel_id=1, source_target_pairs={{1,0},{2,3},{5,4},{6,7},{9,8},{10,11},{13,12},{14,15},{17,16},{18,... | collective-permute-start | bytes 3145736 | tf_op jit(solution)/shard_map/ppermute | solution.py:141
  49.5 9.0 %collective-permute-start.8 = (f32[192,256]{1,0:T(8,128)}, f32[192,256]{1,0:T(8,128)}, u32[]{:S(2)}, u32[]{:S(2)}) collective-permute-start(f32[192,256]{1,0:T(8,128)} %get-tuple-element.31), channel_id=1, source_target_pairs={{0,24},{4,28},{8,16},{12,20},{16,8},{20,12},{24,0},{28,4},{1,25},{... | collective-permute-start | bytes 589832 | tf_op jit(solution)/shard_map/ppermute | solution.py:135
  52.2 10.0 %collective-permute-start.7 = (f32[192,256]{1,0:T(8,128)}, f32[192,256]{1,0:T(8,128)}, u32[]{:S(2)}, u32[]{:S(2)}) collective-permute-start(f32[192,256]{1,0:T(8,128)} %get-tuple-element.32), channel_id=1, source_target_pairs={{0,16},{4,20},{8,24},{12,28},{16,0},{20,4},{24,8},{28,12},{1,17},{... | collective-permute-start | bytes 589832 | tf_op jit(solution)/shard_map/ppermute | solution.py:135
  52.7 9.8 %collective-permute-start.6 = (f32[192,256]{1,0:T(8,128)}, f32[192,256]{1,0:T(8,128)}, u32[]{:S(2)}, u32[]{:S(2)}) collective-permute-start(f32[192,256]{1,0:T(8,128)} %get-tuple-element.30), channel_id=1, source_target_pairs={{0,8},{4,12},{8,0},{12,4},{16,24},{20,28},{24,16},{28,20},{1,9},{5... | collective-permute-start | bytes 589832 | tf_op jit(solution)/shard_map/ppermute | solution.py:135
  63.8 13.5 %collective-permute-start.11 = (f32[192,256]{1,0:T(8,128)S(1)}, f32[192,256]{1,0:T(8,128)S(1)}, u32[]{:S(2)}, u32[]{:S(2)}) collective-permute-start(f32[192,256]{1,0:T(8,128)S(1)} %fusion.56), channel_id=1, source_target_pairs={{0,24},{4,28},{8,16},{12,20},{16,8},{20,12},{24,0},{28,4},{1,25},{... | collective-permute-start | bytes 589832 | tf_op jit(solution)/shard_map/ppermute | solution.py:135
  65.3 12.0 %collective-permute-start.10 = (f32[192,256]{1,0:T(8,128)S(1)}, f32[192,256]{1,0:T(8,128)S(1)}, u32[]{:S(2)}, u32[]{:S(2)}) collective-permute-start(f32[192,256]{1,0:T(8,128)S(1)} %fusion.56), channel_id=1, source_target_pairs={{0,16},{4,20},{8,24},{12,28},{16,0},{20,4},{24,8},{28,12},{1,17},{... | collective-permute-start | bytes 589832 | tf_op jit(solution)/shard_map/ppermute | solution.py:135
  66.8 10.5 %collective-permute-start.9 = (f32[192,256]{1,0:T(8,128)S(1)}, f32[192,256]{1,0:T(8,128)S(1)}, u32[]{:S(2)}, u32[]{:S(2)}) collective-permute-start(f32[192,256]{1,0:T(8,128)S(1)} %fusion.56), channel_id=1, source_target_pairs={{0,8},{4,12},{8,0},{12,4},{16,24},{20,28},{24,16},{28,20},{1,9},{5... | collective-permute-start | bytes 589832 | tf_op jit(solution)/shard_map/ppermute | solution.py:135
  77.2 52.3 %copy-start.5 = (f32[256,1024]{1,0:T(8,128)}, f32[256,1024]{1,0:T(8,128)S(1)}, u32[]{:S(2)}) copy-start(f32[256,1024]{1,0:T(8,128)S(1)} %broadcast_select_fusion.1) | copy-start | bytes 3145732
  77.2 18.3 %collective-permute-start.15 = (f32[256,1024]{1,0:T(8,128)S(1)}, f32[256,1024]{1,0:T(8,128)}, u32[]{:S(2)}, u32[]{:S(2)}) collective-permute-start(f32[256,1024]{1,0:T(8,128)S(1)} %broadcast_select_fusion.1), channel_id=1, source_target_pairs={{0,4},{4,0},{8,12},{12,8},{16,20},{20,16},{24,28},{28,24},{1,5},{5... | collective-permute-start | bytes 3145736 | tf_op jit(solution)/shard_map/ppermute | solution.py:138
  79.2 3.7 %collective-permute-start.30 = (f32[2,128,256]{2,1,0:T(8,128)}, f32[2,128,256]{2,1,0:T(8,128)}, u32[]{:S(2)}, u32[]{:S(2)}) collective-permute-start(f32[2,128,256]{2,1,0:T(8,128)} %bitcast.86), channel_id=1, source_target_pairs={{0,4},{4,0},{8,12},{12,8},{16,20},{20,16},{24,28},{28,24},{1,5},{5... | collective-permute-start | bytes 786440 | tf_op jit(solution)/shard_map/ppermute | solution.py:138
  79.6 36.2 %collective-permute-start.22 = (f32[256,1024]{1,0:T(8,128)}, f32[256,1024]{1,0:T(8,128)}, u32[]{:S(2)}, u32[]{:S(2)}) collective-permute-start(f32[256,1024]{1,0:T(8,128)} %collective-permute-done.14), channel_id=1, source_target_pairs={{1,0},{2,3},{5,4},{6,7},{9,8},{10,11},{13,12},{14,15},{17,16},{18,... | collective-permute-start | bytes 3145736 | tf_op jit(solution)/shard_map/ppermute | solution.py:141
  95.5 2.5 %copy-start.11 = (f32[256,1024]{1,0:T(8,128)S(1)}, f32[256,1024]{1,0:T(8,128)}, u32[]{:S(2)}) copy-start(f32[256,1024]{1,0:T(8,128)} %copy-done.10) | copy-start | bytes 3145732
  99.9 2.2 %copy-start.16 = (f32[64,1024]{1,0:T(8,128)S(1)}, f32[64,1024]{1,0:T(8,128)}, u32[]{:S(2)}) copy-start(f32[64,1024]{1,0:T(8,128)} %get-tuple-element.5) | copy-start | bytes 786436
  99.9 2.2 %copy-start.28 = (f32[64,1024]{1,0:T(8,128)S(1)}, f32[64,1024]{1,0:T(8,128)}, u32[]{:S(2)}) copy-start(f32[64,1024]{1,0:T(8,128)} %copy-done.27) | copy-start | bytes 786436
  99.9 2.2 %copy-start.31 = (f32[64,1024]{1,0:T(8,128)S(1)}, f32[64,1024]{1,0:T(8,128)}, u32[]{:S(2)}) copy-start(f32[64,1024]{1,0:T(8,128)} %copy-done.30) | copy-start | bytes 786436
  99.9 2.2 %copy-start.34 = (f32[64,1024]{1,0:T(8,128)S(1)}, f32[64,1024]{1,0:T(8,128)}, u32[]{:S(2)}) copy-start(f32[64,1024]{1,0:T(8,128)} %copy-done.33) | copy-start | bytes 786436
  102.8 18.1 %copy-start.8 = (f32[256,1024]{1,0:T(8,128)S(1)}, f32[256,1024]{1,0:T(8,128)}, u32[]{:S(2)}) copy-start(f32[256,1024]{1,0:T(8,128)} %copy-done.7) | copy-start | bytes 3145732
  102.8 14.4 %collective-permute-start.18 = (f32[128,256]{1,0:T(8,128)S(1)}, f32[128,256]{1,0:T(8,128)S(1)}, u32[]{:S(2)}, u32[]{:S(2)}) collective-permute-start(f32[128,256]{1,0:T(8,128)S(1)} %get-tuple-element.45), channel_id=1, source_target_pairs={{0,24},{4,28},{8,16},{12,20},{16,8},{20,12},{24,0},{28,4},{1,25},{... | collective-permute-start | bytes 393224 | tf_op jit(solution)/shard_map/ppermute | solution.py:135
  105.3 11.9 %collective-permute-start.17 = (f32[128,256]{1,0:T(8,128)S(1)}, f32[128,256]{1,0:T(8,128)S(1)}, u32[]{:S(2)}, u32[]{:S(2)}) collective-permute-start(f32[128,256]{1,0:T(8,128)S(1)} %get-tuple-element.46), channel_id=1, source_target_pairs={{0,16},{4,20},{8,24},{12,28},{16,0},{20,4},{24,8},{28,12},{1,17},{... | collective-permute-start | bytes 393224 | tf_op jit(solution)/shard_map/ppermute | solution.py:135
  105.8 11.4 %collective-permute-start.16 = (f32[128,256]{1,0:T(8,128)S(1)}, f32[128,256]{1,0:T(8,128)S(1)}, u32[]{:S(2)}, u32[]{:S(2)}) collective-permute-start(f32[128,256]{1,0:T(8,128)S(1)} %get-tuple-element.44), channel_id=1, source_target_pairs={{0,8},{4,12},{8,0},{12,4},{16,24},{20,28},{24,16},{28,20},{1,9},{5... | collective-permute-start | bytes 393224 | tf_op jit(solution)/shard_map/ppermute | solution.py:135
  117.1 16.1 %copy-start.13 = (f32[256,1024]{1,0:T(8,128)}, f32[256,1024]{1,0:T(8,128)S(1)}, u32[]{:S(2)}) copy-start(f32[256,1024]{1,0:T(8,128)S(1)} %broadcast_select_fusion) | copy-start | bytes 3145732
  117.1 10.0 %collective-permute-start.23 = (f32[256,1024]{1,0:T(8,128)S(1)}, f32[256,1024]{1,0:T(8,128)S(1)}, u32[]{:S(2)}, u32[]{:S(2)}) collective-permute-start(f32[256,1024]{1,0:T(8,128)S(1)} %broadcast_select_fusion), channel_id=1, source_target_pairs={{0,4},{4,0},{8,12},{12,8},{16,20},{20,16},{24,28},{28,24},{1,5},{5... | collective-permute-start | bytes 3145736 | tf_op jit(solution)/shard_map/ppermute | solution.py:138
  117.3 9.7 %collective-permute-start.21 = (f32[128,256]{1,0:T(8,128)S(1)}, f32[128,256]{1,0:T(8,128)S(1)}, u32[]{:S(2)}, u32[]{:S(2)}) collective-permute-start(f32[128,256]{1,0:T(8,128)S(1)} %fusion.62), channel_id=1, source_target_pairs={{0,24},{4,28},{8,16},{12,20},{16,8},{20,12},{24,0},{28,4},{1,25},{... | collective-permute-start | bytes 393224 | tf_op jit(solution)/shard_map/ppermute | solution.py:135
  118.9 8.1 %collective-permute-start.20 = (f32[128,256]{1,0:T(8,128)S(1)}, f32[128,256]{1,0:T(8,128)S(1)}, u32[]{:S(2)}, u32[]{:S(2)}) collective-permute-start(f32[128,256]{1,0:T(8,128)S(1)} %fusion.62), channel_id=1, source_target_pairs={{0,16},{4,20},{8,24},{12,28},{16,0},{20,4},{24,8},{28,12},{1,17},{... | collective-permute-start | bytes 393224 | tf_op jit(solution)/shard_map/ppermute | solution.py:135
  120.3 6.7 %collective-permute-start.19 = (f32[128,256]{1,0:T(8,128)S(1)}, f32[128,256]{1,0:T(8,128)S(1)}, u32[]{:S(2)}, u32[]{:S(2)}) collective-permute-start(f32[128,256]{1,0:T(8,128)S(1)} %fusion.62), channel_id=1, source_target_pairs={{0,8},{4,12},{8,0},{12,4},{16,24},{20,28},{24,16},{28,20},{1,9},{5... | collective-permute-start | bytes 393224 | tf_op jit(solution)/shard_map/ppermute | solution.py:135
  127.2 5.4 %copy-start.36 = (f32[256,1024]{1,0:T(8,128)}, f32[256,1024]{1,0:T(8,128)S(1)}, u32[]{:S(2)}) copy-start(f32[256,1024]{1,0:T(8,128)S(1)} %collective-permute-done.23) | copy-start | bytes 3145732
  134.0 8.1 %collective-permute-start.26 = (f32[160,256]{1,0:T(8,128)S(1)}, f32[160,256]{1,0:T(8,128)S(1)}, u32[]{:S(2)}, u32[]{:S(2)}) collective-permute-start(f32[160,256]{1,0:T(8,128)S(1)} %get-tuple-element.34), channel_id=1, source_target_pairs={{0,24},{4,28},{8,16},{12,20},{16,8},{20,12},{24,0},{28,4},{1,25},{... | collective-permute-start | bytes 491528 | tf_op jit(solution)/shard_map/ppermute | solution.py:135
  135.5 9.0 %collective-permute-start.25 = (f32[160,256]{1,0:T(8,128)S(1)}, f32[160,256]{1,0:T(8,128)S(1)}, u32[]{:S(2)}, u32[]{:S(2)}) collective-permute-start(f32[160,256]{1,0:T(8,128)S(1)} %get-tuple-element.35), channel_id=1, source_target_pairs={{0,16},{4,20},{8,24},{12,28},{16,0},{20,4},{24,8},{28,12},{1,17},{... | collective-permute-start | bytes 491528 | tf_op jit(solution)/shard_map/ppermute | solution.py:135
  136.9 7.7 %collective-permute-start.24 = (f32[160,256]{1,0:T(8,128)S(1)}, f32[160,256]{1,0:T(8,128)S(1)}, u32[]{:S(2)}, u32[]{:S(2)}) collective-permute-start(f32[160,256]{1,0:T(8,128)S(1)} %get-tuple-element.33), channel_id=1, source_target_pairs={{0,8},{4,12},{8,0},{12,4},{16,24},{20,28},{24,16},{28,20},{1,9},{5... | collective-permute-start | bytes 491528 | tf_op jit(solution)/shard_map/ppermute | solution.py:135
  144.7 12.0 %collective-permute-start.29 = (f32[160,256]{1,0:T(8,128)S(1)}, f32[160,256]{1,0:T(8,128)S(1)}, u32[]{:S(2)}, u32[]{:S(2)}) collective-permute-start(f32[160,256]{1,0:T(8,128)S(1)} %fusion.59), channel_id=1, source_target_pairs={{0,24},{4,28},{8,16},{12,20},{16,8},{20,12},{24,0},{28,4},{1,25},{... | collective-permute-start | bytes 491528 | tf_op jit(solution)/shard_map/ppermute | solution.py:135
  146.2 10.4 %collective-permute-start.28 = (f32[160,256]{1,0:T(8,128)S(1)}, f32[160,256]{1,0:T(8,128)S(1)}, u32[]{:S(2)}, u32[]{:S(2)}) collective-permute-start(f32[160,256]{1,0:T(8,128)S(1)} %fusion.59), channel_id=1, source_target_pairs={{0,16},{4,20},{8,24},{12,28},{16,0},{20,4},{24,8},{28,12},{1,17},{... | collective-permute-start | bytes 491528 | tf_op jit(solution)/shard_map/ppermute | solution.py:135
  147.6 9.2 %collective-permute-start.27 = (f32[160,256]{1,0:T(8,128)S(1)}, f32[160,256]{1,0:T(8,128)S(1)}, u32[]{:S(2)}, u32[]{:S(2)}) collective-permute-start(f32[160,256]{1,0:T(8,128)S(1)} %fusion.59), channel_id=1, source_target_pairs={{0,8},{4,12},{8,0},{12,4},{16,24},{20,28},{24,16},{28,20},{1,9},{5... | collective-permute-start | bytes 491528 | tf_op jit(solution)/shard_map/ppermute | solution.py:135
  148.3 8.9 %collective-permute-start.31 = (f32[2,128,256]{2,1,0:T(8,128)S(1)}, f32[2,128,256]{2,1,0:T(8,128)S(1)}, u32[]{:S(2)}, u32[]{:S(2)}) collective-permute-start(f32[2,128,256]{2,1,0:T(8,128)S(1)} %bitcast.285), channel_id=1, source_target_pairs={{0,4},{4,0},{8,12},{12,8},{16,20},{20,16},{24,28},{28,24},{1,5},{5... | collective-permute-start | bytes 786440 | tf_op jit(solution)/shard_map/ppermute | solution.py:138
  157.1 1.8 collective-permute-start.32
  164.3 4.5 %copy-start.9 = (f32[256,1024]{1,0:T(8,128)S(1)}, f32[256,1024]{1,0:T(8,128)}, u32[]{:S(2)}) copy-start(f32[256,1024]{1,0:T(8,128)} %copy-done.7) | copy-start | bytes 3145732
  164.3 4.5 %copy-start.14 = (f32[256,1024]{1,0:T(8,128)S(1)}, f32[256,1024]{1,0:T(8,128)}, u32[]{:S(2)}) copy-start(f32[256,1024]{1,0:T(8,128)} %copy-done.13) | copy-start | bytes 3145732
  164.3 4.5 %copy-start.17 = (f32[64,1024]{1,0:T(8,128)S(1)}, f32[64,1024]{1,0:T(8,128)}, u32[]{:S(2)}) copy-start(f32[64,1024]{1,0:T(8,128)} %get-tuple-element.5) | copy-start | bytes 786436
  164.3 4.5 %copy-start.29 = (f32[64,1024]{1,0:T(8,128)S(1)}, f32[64,1024]{1,0:T(8,128)}, u32[]{:S(2)}) copy-start(f32[64,1024]{1,0:T(8,128)} %copy-done.27) | copy-start | bytes 786436
  164.3 4.5 %copy-start.32 = (f32[64,1024]{1,0:T(8,128)S(1)}, f32[64,1024]{1,0:T(8,128)}, u32[]{:S(2)}) copy-start(f32[64,1024]{1,0:T(8,128)} %copy-done.30) | copy-start | bytes 786436
  164.3 4.5 %copy-start.35 = (f32[64,1024]{1,0:T(8,128)S(1)}, f32[64,1024]{1,0:T(8,128)}, u32[]{:S(2)}) copy-start(f32[64,1024]{1,0:T(8,128)} %copy-done.33) | copy-start | bytes 786436
  172.6 2.1 copy-start.37
  178.3 14.8 %collective-permute-start.33 = (f32[2,64,1024]{2,1,0:T(8,128)S(1)}, f32[2,64,1024]{2,1,0:T(8,128)S(1)}, u32[]{:S(2)}, u32[]{:S(2)}) collective-permute-start(f32[2,64,1024]{2,1,0:T(8,128)S(1)} %pad_maximum_fusion.14), channel_id=1, source_target_pairs={{0,8},{4,12},{8,0},{12,4},{16,24},{20,28},{24,16},{28,20},{1,9},{5... | collective-permute-start | bytes 1572872 | tf_op jit(solution)/shard_map/ppermute | solution.py:135
  179.9 25.1 %collective-permute-start.34 = (f32[2,64,1024]{2,1,0:T(8,128)S(1)}, f32[2,64,1024]{2,1,0:T(8,128)S(1)}, u32[]{:S(2)}, u32[]{:S(2)}) collective-permute-start(f32[2,64,1024]{2,1,0:T(8,128)S(1)} %pad_maximum_fusion.15), channel_id=1, source_target_pairs={{0,16},{4,20},{8,24},{12,28},{16,0},{20,4},{24,8},{28,12},{1,17},{... | collective-permute-start | bytes 1572872 | tf_op jit(solution)/shard_map/ppermute | solution.py:135
  180.7 24.4 %collective-permute-start.35 = (f32[2,64,1024]{2,1,0:T(8,128)S(1)}, f32[2,64,1024]{2,1,0:T(8,128)S(1)}, u32[]{:S(2)}, u32[]{:S(2)}) collective-permute-start(f32[2,64,1024]{2,1,0:T(8,128)S(1)} %pad_maximum_fusion.16), channel_id=1, source_target_pairs={{0,24},{4,28},{8,16},{12,20},{16,8},{20,12},{24,0},{28,4},{1,25},{... | collective-permute-start | bytes 1572872 | tf_op jit(solution)/shard_map/ppermute | solution.py:135
  (19 other events, 28.8 us)
Sparse Core Ops, SparseCore 0:
  95.6 67.3 all-gather.1

commit v2 on v1

--- a/solution.py
+++ b/solution.py
@@ -80,16 +80,21 @@
 
 
 def inverse_kernel(gram_ref, out_ref):
-    gram = gram_ref[...]
-    rows = lax.broadcasted_iota(jnp.int32, gram.shape, 0)
-    cols = lax.broadcasted_iota(jnp.int32, gram.shape, 1)
-    inv = jnp.where(rows == cols, 2.0 / gram, 0.0)
+    half = gram_ref.shape[0] // 2
+    rows = lax.broadcasted_iota(jnp.int32, (half, half), 0)
+    cols = lax.broadcasted_iota(jnp.int32, (half, half), 1)
+    grams = [gram_ref[:half, :half], gram_ref[half:, half:]]
+    inv = [jnp.where(rows == cols, 2.0 / gram, 0.0) for gram in grams]
     size = 1
-    while size < gram.shape[0]:
+    while size < half:
         pick = (rows // (2 * size) == cols // (2 * size)) & (rows % (2 * size) >= size) & (cols % (2 * size) < size)
-        inv = inv - kdot(kdot(inv, jnp.where(pick, gram, 0.0)), inv)
+        inner = [kdot(i, jnp.where(pick, gram, 0.0)) for i, gram in zip(inv, grams)]
+        inv = [i - kdot(t, i) for i, t in zip(inv, inner)]
         size *= 2
-    out_ref[...] = inv
+    out_ref[:half, :half] = inv[0]
+    out_ref[:half, half:] = jnp.zeros((half, half), jnp.float32)
+    out_ref[half:, :half] = -kdot(kdot(inv[1], gram_ref[half:, :half]), inv[0])
+    out_ref[half:, half:] = inv[1]
 
 
 def inverse(gram):
@@ -130,6 +135,11 @@
     r, c = lax.axis_index("row"), lax.axis_index("col")
     core, chip = r % 2, r // 2
     mine = eigvecs.shape[0]
+    part = B // 2 // chips
+    groups = [[2 * i + k for i in range(chips)] for k in range(2)]
+
+    def exchange(value):
+        return lax.all_to_all(value, "row", split_axis=0, concat_axis=0, tiled=True, axis_index_groups=groups)
 
     def across(value, x):
         return lax.ppermute(value, "row", [(i, i ^ (2 * x)) for i in range(2 * chips)])
@@ -139,99 +149,101 @@
 
     def zmove(value, pairs):
         return lax.ppermute(value, "col", pairs)
+
+    def paired(value, axis):
+        other = sibling(value)
+        return jnp.where(
+            core == 0, jnp.concatenate([value, other], axis=axis), jnp.concatenate([other, value], axis=axis)
+        )
 
     def by_chip(value):
         bit = 1
         while bit < chips:
-            turned = value[jnp.array([i ^ bit for i in range(chips)])] if False else jnp.stack(
-                [value[i ^ bit] for i in range(chips)]
-            )
+            turned = jnp.stack([value[i ^ bit] for i in range(chips)])
             value = jnp.where((chip & bit) != 0, turned, value)
             bit *= 2
         return value
 
-    def total(products, grams):
-        n_p, n_g = len(products), len(grams)
-        part = B // 2 // chips
+    def pack(products, grams):
         packed = [p.reshape(chips, mine, B) for p in products]
         packed += [by_chip(g.reshape(chips, part, B)) for g in grams]
-        packed = jnp.concatenate(packed, axis=1)
+        return jnp.concatenate(packed, axis=1)
+
+    def scatter(packed):
         held = packed[0]
         for x in range(1, chips):
             held = held + across(packed[x], x)
-        full = jnp.stack([held] + [across(held, x) for x in range(1, chips)])
+        return held
+
+    def collect(held):
+        return jnp.stack([held] + [across(held, x) for x in range(1, chips)])
+
+    def unpack(full, n_p, n_g):
         out_p = [full[:, i * mine : (i + 1) * mine].reshape(chips * mine, B) for i in range(n_p)]
-        out_g = None
-        if n_g:
-            halves = full[:, n_p * mine :].reshape(chips, n_g, part, B)
-            halves = by_chip(halves).transpose(1, 0, 2, 3).reshape(n_g, B // 2, B)
-            others = sibling(halves)
-            first, second = jnp.where(core == 0, halves, others), jnp.where(core == 0, others, halves)
-            out_g = jnp.concatenate([first, second], axis=1)
-        return out_p, out_g
+        halves = by_chip(full[:, n_p * mine :]).reshape(chips, n_g, part, B).transpose(1, 0, 2, 3)
+        return out_p, paired(halves.reshape(n_g, B // 2, B), 1)
 
     vectors = masked_vectors(reflectors, c, r * width)
     near = zmove(vectors, [(0, 1), (1, 0), (2, 3), (3, 2)])
     inner = zmove(vectors, [(1, 2), (2, 1)])
-
-    def piece(x):
-        start = (chip ^ x) * 2 * width
-        return jnp.stack(
-            [
-                lax.dynamic_slice(eigvecs, (0, start + core * width), (mine, width)),
-                lax.dynamic_slice(eigvecs, (0, start + (1 - core) * width), (mine, width)),
-            ]
-        )
-
-    pieces = [piece(0)] + [across(piece(x), x) for x in range(1, chips)]
-    e_m = jnp.concatenate([p[0] for p in pieces])
-    e_o = jnp.concatenate([p[1] for p in pieces])
+    slots = [paired(vectors, 1)]
+
+    def product(slot):
+        return nt(grid, slots[slot])
+
+    def gram(slot, other):
+        half = lax.dynamic_slice(slots[slot], (core * (B // 2), 0), (B // 2, 2 * width))
+        return nt(half, slots[other])
+
+    own = gram(0, 0)
+    own, eigvecs = lax.optimization_barrier((own, eigvecs))
+    g_own = own
+    for x in range(1, chips):
+        g_own = g_own + across(own, x)
+    g_own = paired(g_own, 0)
+    pieces = [lax.dynamic_slice(eigvecs, (0, (chip ^ x) * 2 * width), (mine, 2 * width)) for x in range(chips)]
+    pieces = pieces[:1] + [across(pieces[x], x) for x in range(1, chips)]
+    grid = jnp.concatenate(pieces)
 
     edge = (c == 0) | (c == 3)
+    g_own, near, inner = lax.optimization_barrier((g_own, near, inner))
     second_out = zmove(inner, [(1, 0), (2, 3)])
     second_in = zmove(near, [(1, 2), (2, 1)])
-    second = jnp.where(edge, second_out, second_in)
+    inv = inverse(g_own)
+    inv_part = lax.dynamic_slice(inv, (core * (B // 2) + chip * part, 0), (part, B))
+    grid, inv_part = lax.optimization_barrier((grid, inv_part))
+    parts = lax.all_to_all(
+        jnp.broadcast_to(inv_part, (PANELS, part, B)), "col", split_axis=0, concat_axis=0, tiled=True
+    ).reshape(PANELS * part, B)
+
+    slots.append(paired(near, 1))
+    packed_01 = pack([product(0), product(1)], [gram(1, 0)])
+    second_out, second_in, packed_01 = lax.optimization_barrier((second_out, second_in, packed_01))
     third_out = zmove(second_in, [(1, 0), (2, 3)])
-    third = jnp.where(edge, third_out, inner)
-
-    slots = []
-    for v in (vectors, near, second, third):
-        slots.append((v, sibling(v)))
-
-    def product(slot):
-        m, o = slots[slot]
-        return nt(e_m, m) + nt(e_o, o)
-
-    def gram(slot, other):
-        m, o = slots[slot]
-        hm = lax.dynamic_slice(m, (core * (B // 2), 0), (B // 2, width))
-        ho = lax.dynamic_slice(o, (core * (B // 2), 0), (B // 2, width))
-        return nt(hm, slots[other][0]) + nt(ho, slots[other][1])
-
-    p_01, g_01 = total([product(0), product(1)], [gram(0, 0), gram(1, 0)])
-    inv = inverse(g_01[0])
-    share = B // (2 * chips)
-    inv_part = lax.dynamic_slice(inv, (r * share, 0), (share, B))
-    inverses = lax.all_gather(inv_part, ("col", "row"), axis=0, tiled=True).reshape(PANELS, B, B)
-    p_2, g_2 = total([product(2)], [gram(2, 0), gram(2, 1)])
-    p_3, g_3 = total([product(3)], [gram(3, 0), gram(3, 1), gram(3, 2)])
+    full_01 = collect(jnp.concatenate([scatter(packed_01), parts]))
+
+    slots.append(paired(jnp.where(edge, second_out, second_in), 1))
+    held_2 = scatter(pack([product(2)], [gram(2, 0), gram(2, 1)]))
+    third_out, full_01, held_2 = lax.optimization_barrier((third_out, full_01, held_2))
+    full_2 = collect(held_2)
+
+    slots.append(paired(jnp.where(edge, third_out, inner), 1))
+    held_3 = scatter(pack([product(3)], [gram(3, 0), gram(3, 1), gram(3, 2)]))
+    full_2, held_3 = lax.optimization_barrier((full_2, held_3))
+    p_01, g_01 = unpack(full_01, 2, 1 + PANELS)
+    p_2, g_2 = unpack(full_2, 1, 2)
+    p_3, g_3 = unpack(collect(held_3), 1, 3)
+    g_01, inverses = g_01[:1], g_01[1:]
     products = jnp.stack(p_01 + p_2 + p_3)
-    grams = jnp.concatenate([g_01[1:], g_2, g_3])
+    grams = jnp.concatenate([g_01, g_2, g_3])
     solved = solve(c, products, grams, inverses)
     s_all = jnp.concatenate([solved[i] for i in range(PANELS)], axis=1)
-    v_m = jnp.concatenate([m for m, _ in slots])
-    v_o = jnp.concatenate([o for _, o in slots])
-    done_m = e_m - nn(s_all, v_m)
-    done_o = e_o - nn(s_all, v_o)
+    done = grid - nn(s_all, jnp.concatenate(slots))
+    done = done.reshape(chips, mine, 2 * width)
     result = jnp.zeros_like(eigvecs)
     for x in range(chips):
-        rows = slice(x * mine, (x + 1) * mine)
-        both = jnp.stack([done_m[rows], done_o[rows]])
-        if x:
-            both = across(both, x)
-        start = (chip ^ x) * 2 * width
-        result = lax.dynamic_update_slice(result, both[0], (0, start + core * width))
-        result = lax.dynamic_update_slice(result, both[1], (0, start + (1 - core) * width))
+        piece = across(done[x], x) if x else done[x]
+        result = lax.dynamic_update_slice(result, piece, (0, (chip ^ x) * 2 * width))
     return result
 
 

time: 215 us -> 178 us (0.83)
  between operations: 14.9 us -> 0.9 us
  waiting for transfers between devices: 90.4 us -> 77.8 us
  matrix products: 26.5 us -> 17.1 us
  local copies, waits for them, and re-layouts: 19.1 us -> 11.4 us
  starting transfers between devices: 38.3 us -> 45.8 us
  Pallas kernels: 13.6 us -> 9.62 us
  other arithmetic: 11.2 us -> 14.9 us
    dot_general x22 -> x11, matrix products: 20.8 us -> 12.8 us  [nt(): lax.dot_general(left, right, (((1,), (1,)), ((), ())), precision=lax.Prec...]
    ppermute x5, waiting for transfers between devices: 17.9 us -> 13 us  [zmove(): return lax.ppermute(value, 'col', pairs)]
    ppermute x24 -> x27, waiting for transfers between devices: 67.8 us -> 63.3 us  [across(): lax.ppermute(value, 'row', [(i, i ^ 2 * x) for i in range(2 * chips)])]
    select_n x5 -> x10, other arithmetic: 3.92 us -> 8.29 us  [the longest x8 6.75 us: paired(): jnp.where(core == 0, jnp.concatenate([value, other], axis=axis), jnp.conc...]
    pallas_call x1, Pallas kernels: 9.26 us -> 5.29 us  [inverse(): pl.pallas_call(inverse_kernel, out_shape=jax.ShapeDtypeStruct(gram.shape,...]
    all_gather x1 -> x0, waiting for transfers between devices: 3.9 us -> none  [panels_on_cols(): lax.all_gather(inv_part, ('col', 'row'), axis=0, tiled=True)]
    another operation x9 -> x3, other arithmetic: 3.78 us -> 0.15 us  [collect(): return jnp.stack([held] + [across(held, x) for x in range(1, chips)])]
    unnamed x92 -> x16, local copies, waits for them, and re-layouts: 7.41 us -> 3.96 us
  transfers between devices with their start and end apart: 37 -> 41, of which waited for: 17 -> 21; matrix products, arithmetic and copies ran while one was open for 18% -> 17% of each run, Pallas kernels for 4% -> 3%
where the time goes in v2:
time: 178 us
  waiting for transfers between devices  77.8 us (44%)
  starting transfers between devices  45.8 us (26%)
  matrix products  17.1 us (10%)
  other arithmetic  14.9 us (8%)
  local copies, waits for them, and re-layouts  11.4 us (6%)
  Pallas kernels  9.62 us (5%)
    ppermute x27, waiting for transfers between devices, across(): lax.ppermute(value, 'row', [(i, i ^ 2 * x) for i in range(2 * chips)])  63.3 us
    ppermute x27, starting transfers between devices, across(): lax.ppermute(value, 'row', [(i, i ^ 2 * x) for i in range(2 * chips)])  32.8 us
    ppermute x5, waiting for transfers between devices, zmove(): return lax.ppermute(value, 'col', pairs)  13 us
    dot_general x11, matrix products, nt(): lax.dot_general(left, right, (((1,), (1,)), ((), ())), precision=lax.Prec...  12.8 us
    ppermute x5, starting transfers between devices, zmove(): return lax.ppermute(value, 'col', pairs)  8.68 us
    select_n x8, other arithmetic, paired(): jnp.where(core == 0, jnp.concatenate([value, other], axis=axis), jnp.conc...  6.75 us
    pallas_call x1, Pallas kernels, inverse(): pl.pallas_call(inverse_kernel, out_shape=jax.ShapeDtypeStruct(gram.shape,...  5.29 us
    dot_general x1, matrix products, nn(): lax.dot_general(left, right, (((1,), (0,)), ((), ())), precision=lax.Prec...  4.35 us
  transfers between devices with their start and end apart: 41, of which 21 were waited for; matrix products, arithmetic and copies ran while one was open for 17% of the time, Pallas kernels for 3%

profile of v2, /device:TPU:0, one launch (start us, length us, event | category | flops | bytes accessed | tf_op | source)
XLA Modules:
  0.0 177.5 jit_solution(4409593938636953024)
XLA Ops:
  0.0 1.4 select_select_fusion
  2.0 2.7 %collective-permute-start.8 = (f32[256,1024]{1,0:T(8,128)S(1)}, f32[256,1024]{1,0:T(8,128)}, u32[]{:S(2)}, u32[]{:S(2)}) collective-permute-start(f32[256,1024]{1,0:T(8,128)S(1)} %select_select_fusion), channel_id=1, source_target_pairs={{0,1},{1,0},{2,3},{3,2},{4,5},{5,4},{6,7},{7,6},{8,9},{9,8},{10,11... | collective-permute-start | bytes 3145736 | tf_op jit(solution)/shard_map/ppermute | solution.py:151
  4.6 1.6 collective-permute-start.9
  6.3 1.8 %maximum_select_fusion = f32[256,2048]{1,0:T(8,128)S(1)} fusion(f32[256,1024]{1,0:T(8,128)} %collective-permute-done, f32[256,1024]{1,0:T(8,128)S(1)} %select_select_fusion, pred[]{:T(512)S(6)} %eq.10), kind=kLoop, calls=%fused_computation.9 | loop fusion | flops 1572864 | bytes 4194305 | tf_op jit(solution)/shard_map/jit(_where)/select_n | solution.py:155
  8.1 1.2 fusion.20
  9.3 2.5 %collective-permute-start.6 = (f32[128,256]{1,0:T(8,128)S(1)}, f32[128,256]{1,0:T(8,128)S(1)}, u32[]{:S(2)}, u32[]{:S(2)}) collective-permute-start(f32[128,256]{1,0:T(8,128)S(1)} %fusion.20), channel_id=1, source_target_pairs={{0,24},{4,28},{8,16},{12,20},{16,8},{20,12},{24,0},{28,4},{1,25},{... | collective-permute-start | bytes 393224 | tf_op jit(solution)/shard_map/ppermute | solution.py:145
  12.8 3.3 %collective-permute-done.6 = f32[128,256]{1,0:T(8,128)S(1)} collective-permute-done((f32[128,256]{1,0:T(8,128)S(1)}, f32[128,256]{1,0:T(8,128)S(1)}, u32[]{:S(2)}, u32[]{:S(2)}) %collective-permute-start.6) | collective-permute-done | bytes 131104 | tf_op jit(solution)/shard_map/ppermute | solution.py:145
  16.1 2.5 %collective-permute-done.5 = f32[128,256]{1,0:T(8,128)S(1)} collective-permute-done((f32[128,256]{1,0:T(8,128)S(1)}, f32[128,256]{1,0:T(8,128)S(1)}, u32[]{:S(2)}, u32[]{:S(2)}) %collective-permute-start.5) | collective-permute-done | bytes 131104 | tf_op jit(solution)/shard_map/ppermute | solution.py:145
  18.8 0.9 add_add_fusion
  19.8 2.9 %constant_dynamic-slice_fusion.4 = (f32[64,2048]{1,0:T(8,128)}, f32[64,2048]{1,0:T(8,128)}, f32[64,2048]{1,0:T(8,128)}, f32[64,2048]{1,0:T(8,128)}) fusion(f32[64,8192]{1,0:T(8,128)} %param.2, s32[]{:T(128)S(6)} %select_n.213, s32[]{:T(128)S(6)} %select_n.216, s32[]{:T(128)S(6)} %select_n.215, s32[]{:T(128)S(6)} %select_n.214), kind=kLoop, calls=%fused_computation.136 | loop fusion | bytes 4194320 | tf_op jit(solution)/shard_map/dynamic_slice | solution.py:204
  22.7 1.6 collective-permute-start.3
  24.3 1.4 collective-permute-start.2
  26.9 1.5 collective-permute-done.8
  28.5 1.6 collective-permute-start.11
  30.1 5.3 %shard_map.28 = f32[256,256]{1,0:T(8,128)} custom-call(f32[256,256]{1,0:T(8,128)} %maximum_select_fusion.10.gram_ref), custom_call_target="tpu_custom_call" | custom-call | tf_op jit(solution)/shard_map/pallas_call | solution.py:101
  36.2 2.5 %collective-permute-done.3 = f32[64,2048]{1,0:T(8,128)} collective-permute-done((f32[64,2048]{1,0:T(8,128)}, f32[64,2048]{1,0:T(8,128)}, u32[]{:S(2)}, u32[]{:S(2)}) %collective-permute-start.3) | collective-permute-done | bytes 524320 | tf_op jit(solution)/shard_map/ppermute | solution.py:145
  38.7 1.3 collective-permute-start.10
  40.0 9.5 %collective-permute-done.2 = f32[64,2048]{1,0:T(8,128)} collective-permute-done((f32[64,2048]{1,0:T(8,128)}, f32[64,2048]{1,0:T(8,128)}, u32[]{:S(2)}, u32[]{:S(2)}) %collective-permute-start.2) | collective-permute-done | bytes 524320 | tf_op jit(solution)/shard_map/ppermute | solution.py:145
  49.5 1.7 pad_maximum_fusion
  51.1 1.1 fusion.63
  52.2 1.8 %maximum_select_fusion.1 = f32[256,2048]{1,0:T(8,128)S(1)} fusion(f32[256,1024]{1,0:T(8,128)S(1)} %collective-permute-done.12, f32[256,1024]{1,0:T(8,128)} %collective-permute-done.8, pred[]{:T(512)S(6)} %eq.10), kind=kLoop, calls=%fused_computation.11 | loop fusion | flops 1572864 | bytes 4194305 | tf_op jit(solution)/shard_map/jit(_where)/select_n | solution.py:155
  54.1 1.2 fusion.18
  55.4 1.1 fusion.64
  56.5 11.5 %collective-permute-done.10 = f32[256,1024]{1,0:T(8,128)S(1)} collective-permute-done((f32[256,1024]{1,0:T(8,128)}, f32[256,1024]{1,0:T(8,128)S(1)}, u32[]{:S(2)}, u32[]{:S(2)}) %collective-permute-start.10) | collective-permute-done | bytes 1048608 | tf_op jit(solution)/shard_map/ppermute | solution.py:151
  68.2 0.8 slice_bitcast_fusion.10
  69.1 2.4 %collective-permute-start.16 = (f32[160,256]{1,0:T(8,128)}, f32[160,256]{1,0:T(8,128)S(1)}, u32[]{:S(2)}, u32[]{:S(2)}) collective-permute-start(f32[160,256]{1,0:T(8,128)} %get-tuple-element.59), channel_id=1, source_target_pairs={{0,24},{4,28},{8,16},{12,20},{16,8},{20,12},{24,0},{28,4},{1,25},{... | collective-permute-start | bytes 491528 | tf_op jit(solution)/shard_map/ppermute | solution.py:145
  73.2 3.3 %all-to-all-start = ((f32[4,32,256]{2,1,0:T(8,128)}), f32[4,32,256]{2,1,0:T(8,128)S(1)}, u32[]{:S(2)}, u32[]{:S(2)}) async-start(f32[4,32,256]{2,1,0:T(8,128)} %broadcast_in_dim.15), calls=%async_computation | async-start | bytes 262144 | tf_op jit(solution)/shard_map/all_to_all | solution.py:215
  76.5 1.5 collective-permute-start.13
  78.0 2.3 %collective-permute-done.15 = f32[160,256]{1,0:T(8,128)} collective-permute-done((f32[160,256]{1,0:T(8,128)}, f32[160,256]{1,0:T(8,128)}, u32[]{:S(2)}, u32[]{:S(2)}) %collective-permute-start.15) | collective-permute-done | bytes 163872 | tf_op jit(solution)/shard_map/ppermute | solution.py:145
  80.5 1.2 fusion.37
  81.7 1.0 all-to-all-done
  82.7 2.5 %collective-permute-start.19 = (f32[288,256]{1,0:T(8,128)S(1)}, f32[288,256]{1,0:T(8,128)S(1)}, u32[]{:S(2)}, u32[]{:S(2)}) collective-permute-start(f32[288,256]{1,0:T(8,128)S(1)} %get-tuple-element.73), channel_id=1, source_target_pairs={{0,24},{4,28},{8,16},{12,20},{16,8},{20,12},{24,0},{28,4},{1,25},{... | collective-permute-start | bytes 884744 | tf_op jit(solution)/shard_map/ppermute | solution.py:145
  86.2 1.8 %maximum_select_fusion.2 = f32[256,2048]{1,0:T(8,128)S(1)} fusion(f32[256,1024]{1,0:T(8,128)} %collective-permute-done.20, f32[256,1024]{1,0:T(8,128)S(1)} %broadcast_select_fusion.1, pred[]{:T(512)S(6)} %eq.10), kind=kLoop, calls=%fused_computation.12 | loop fusion | flops 1572864 | bytes 4194305 | tf_op jit(solution)/shard_map/jit(_where)/select_n | solution.py:155
  88.1 1.2 fusion.24
  89.7 1.2 fusion.22
  91.1 1.4 copy-done.1
  92.5 1.2 fusion.65
  93.7 2.5 %collective-permute-start.23 = (f32[128,256]{1,0:T(8,128)S(1)}, f32[128,256]{1,0:T(8,128)S(1)}, u32[]{:S(2)}, u32[]{:S(2)}) collective-permute-start(f32[128,256]{1,0:T(8,128)S(1)} %get-tuple-element.68), channel_id=1, source_target_pairs={{0,24},{4,28},{8,16},{12,20},{16,8},{20,12},{24,0},{28,4},{1,25},{... | collective-permute-start | bytes 393224 | tf_op jit(solution)/shard_map/ppermute | solution.py:145
  96.7 2.6 %collective-permute-done.18 = f32[288,256]{1,0:T(8,128)S(1)} collective-permute-done((f32[288,256]{1,0:T(8,128)S(1)}, f32[288,256]{1,0:T(8,128)S(1)}, u32[]{:S(2)}, u32[]{:S(2)}) %collective-permute-start.18) | collective-permute-done | bytes 294944 | tf_op jit(solution)/shard_map/ppermute | solution.py:145
  99.4 1.5 collective-permute-start.21
  101.0 2.5 %collective-permute-done.22 = f32[128,256]{1,0:T(8,128)S(1)} collective-permute-done((f32[128,256]{1,0:T(8,128)S(1)}, f32[128,256]{1,0:T(8,128)S(1)}, u32[]{:S(2)}, u32[]{:S(2)}) %collective-permute-start.22) | collective-permute-done | bytes 131104 | tf_op jit(solution)/shard_map/ppermute | solution.py:145
  103.5 1.3 collective-permute-done.21
  104.9 1.4 broadcast_select_fusion
  106.3 2.2 %collective-permute-start.26 = (f32[128,256]{1,0:T(8,128)S(1)}, f32[128,256]{1,0:T(8,128)S(1)}, u32[]{:S(2)}, u32[]{:S(2)}) collective-permute-start(f32[128,256]{1,0:T(8,128)S(1)} %fusion.40), channel_id=1, source_target_pairs={{0,24},{4,28},{8,16},{12,20},{16,8},{20,12},{24,0},{28,4},{1,25},{... | collective-permute-start | bytes 393224 | tf_op jit(solution)/shard_map/ppermute | solution.py:145
  108.5 0.9 collective-permute-start.25
  110.6 1.2 fusion.26
  111.8 1.2 fusion.28
  113.0 1.2 fusion.30
  114.2 1.2 fusion.66
  115.8 2.2 %collective-permute-start.30 = (f32[160,256]{1,0:T(8,128)S(1)}, f32[160,256]{1,0:T(8,128)S(1)}, u32[]{:S(2)}, u32[]{:S(2)}) collective-permute-start(f32[160,256]{1,0:T(8,128)S(1)} %get-tuple-element.56), channel_id=1, source_target_pairs={{0,24},{4,28},{8,16},{12,20},{16,8},{20,12},{24,0},{28,4},{1,25},{... | collective-permute-start | bytes 491528 | tf_op jit(solution)/shard_map/ppermute | solution.py:145
  118.0 0.9 collective-permute-start.29
  119.6 4.3 %collective-permute-done.30 = f32[160,256]{1,0:T(8,128)S(1)} collective-permute-done((f32[160,256]{1,0:T(8,128)S(1)}, f32[160,256]{1,0:T(8,128)S(1)}, u32[]{:S(2)}, u32[]{:S(2)}) %collective-permute-start.30) | collective-permute-done | bytes 163872 | tf_op jit(solution)/shard_map/ppermute | solution.py:145
  123.9 2.1 %collective-permute-done.29 = f32[160,256]{1,0:T(8,128)S(1)} collective-permute-done((f32[160,256]{1,0:T(8,128)S(1)}, f32[160,256]{1,0:T(8,128)S(1)}, u32[]{:S(2)}, u32[]{:S(2)}) %collective-permute-start.29) | collective-permute-done | bytes 163872 | tf_op jit(solution)/shard_map/ppermute | solution.py:145
  126.1 1.7 collective-permute-start.33
  127.8 1.2 collective-permute-start.32
  130.0 6.5 %collective-permute-done.32 = f32[160,256]{1,0:T(8,128)S(1)} collective-permute-done((f32[160,256]{1,0:T(8,128)S(1)}, f32[160,256]{1,0:T(8,128)S(1)}, u32[]{:S(2)}, u32[]{:S(2)}) %collective-permute-start.32) | collective-permute-done | bytes 163872 | tf_op jit(solution)/shard_map/ppermute | solution.py:145
  137.4 0.8 copy-done.4
  139.4 4.3 %shard_map.29 = f32[4,256,256]{2,1,0:T(8,128)S(1)} custom-call(s32[1]{0:T(128)} %bitcast.where_ref, f32[4,256,256]{2,1,0:T(8,128)S(1)} %pad_maximum_fusion.3.p_ref, f32[6,256,256]{2,1,0:T(8,128)S(1)} %pad_maximum_fusion.1.g_ref, f32[4,256,256]{2,1,0:T(8,128)S(1)} %slice.539.t_ref), custom_call_target="tpu_custom_call" | custom-call | tf_op jit(solution)/shard_map/pallas_call | solution.py:124
  143.8 4.4 %fusion.8 = f32[256,2048]{1,0:T(8,128)S(1)} fusion(f32[256,2048]{1,0:T(8,128)S(1)} %copy-done.1, f32[256,2048]{1,0:T(8,128)S(1)} %maximum_select_fusion.3, f32[256,2048]{1,0:T(8,128)S(1)} %maximum_select_fusion.2, f32[256,2048]{1,0:T(8,128)S(1)} %copy-done.3, f32[256,2048]{1,0:T(8,128)S(1)} %maximum_select_fusion, f32[256,256]{1,0:T(8,128)S(1)} %get-tuple-element.50, ...), kind=kOutput, calls=%fused_computation.8 | convolution fusion | flops 3228827648 | bytes 13631488 | tf_op jit(solution)/shard_map/dot_general | solution.py:67
  148.5 1.5 collective-permute-start.37
  150.6 1.5 collective-permute-start.39
  152.1 11.2 %collective-permute-done.37 = f32[64,2048]{1,0:T(8,128)S(1)} collective-permute-done((f32[64,2048]{1,0:T(8,128)S(1)}, f32[64,2048]{1,0:T(8,128)S(1)}, u32[]{:S(2)}, u32[]{:S(2)}) %collective-permute-start.37) | collective-permute-done | bytes 524320 | tf_op jit(solution)/shard_map/ppermute | solution.py:145
  163.4 11.9 %collective-permute-done.38 = f32[64,2048]{1,0:T(8,128)S(1)} collective-permute-done((f32[64,2048]{1,0:T(8,128)S(1)}, f32[64,2048]{1,0:T(8,128)S(1)}, u32[]{:S(2)}, u32[]{:S(2)}) %collective-permute-start.38) | collective-permute-done | bytes 524320 | tf_op jit(solution)/shard_map/ppermute | solution.py:145
  175.4 1.3 copy-done.6
  (132 shorter events, 15.5 us)
Async XLA Ops:
  1.4 4.8 %collective-permute-start = (f32[256,1024]{1,0:T(8,128)S(1)}, f32[256,1024]{1,0:T(8,128)}, u32[]{:S(2)}, u32[]{:S(2)}) collective-permute-start(f32[256,1024]{1,0:T(8,128)S(1)} %select_select_fusion), channel_id=1, source_target_pairs={{0,4},{4,0},{8,12},{12,8},{16,20},{20,16},{24,28},{28,24},{1,5},{5... | collective-permute-start | bytes 3145736 | tf_op jit(solution)/shard_map/ppermute | solution.py:148
  2.0 26.5 %collective-permute-start.8 = (f32[256,1024]{1,0:T(8,128)S(1)}, f32[256,1024]{1,0:T(8,128)}, u32[]{:S(2)}, u32[]{:S(2)}) collective-permute-start(f32[256,1024]{1,0:T(8,128)S(1)} %select_select_fusion), channel_id=1, source_target_pairs={{0,1},{1,0},{2,3},{3,2},{4,5},{5,4},{6,7},{7,6},{8,9},{9,8},{10,11... | collective-permute-start | bytes 3145736 | tf_op jit(solution)/shard_map/ppermute | solution.py:151
  4.6 23.9 %collective-permute-start.9 = (f32[256,1024]{1,0:T(8,128)S(1)}, f32[256,1024]{1,0:T(8,128)}, u32[]{:S(2)}, u32[]{:S(2)}) collective-permute-start(f32[256,1024]{1,0:T(8,128)S(1)} %select_select_fusion), channel_id=1, source_target_pairs={{1,2},{2,1},{5,6},{6,5},{9,10},{10,9},{13,14},{14,13},{17,18},{18,... | collective-permute-start | bytes 3145736 | tf_op jit(solution)/shard_map/ppermute | solution.py:151
  9.3 6.8 %collective-permute-start.6 = (f32[128,256]{1,0:T(8,128)S(1)}, f32[128,256]{1,0:T(8,128)S(1)}, u32[]{:S(2)}, u32[]{:S(2)}) collective-permute-start(f32[128,256]{1,0:T(8,128)S(1)} %fusion.20), channel_id=1, source_target_pairs={{0,24},{4,28},{8,16},{12,20},{16,8},{20,12},{24,0},{28,4},{1,25},{... | collective-permute-start | bytes 393224 | tf_op jit(solution)/shard_map/ppermute | solution.py:145
  11.8 6.8 %collective-permute-start.5 = (f32[128,256]{1,0:T(8,128)S(1)}, f32[128,256]{1,0:T(8,128)S(1)}, u32[]{:S(2)}, u32[]{:S(2)}) collective-permute-start(f32[128,256]{1,0:T(8,128)S(1)} %fusion.20), channel_id=1, source_target_pairs={{0,16},{4,20},{8,24},{12,28},{16,0},{20,4},{24,8},{28,12},{1,17},{... | collective-permute-start | bytes 393224 | tf_op jit(solution)/shard_map/ppermute | solution.py:145
  12.3 6.5 %collective-permute-start.4 = (f32[128,256]{1,0:T(8,128)S(1)}, f32[128,256]{1,0:T(8,128)}, u32[]{:S(2)}, u32[]{:S(2)}) collective-permute-start(f32[128,256]{1,0:T(8,128)S(1)} %fusion.20), channel_id=1, source_target_pairs={{0,8},{4,12},{8,0},{12,4},{16,24},{20,28},{24,16},{28,20},{1,9},{5... | collective-permute-start | bytes 393224 | tf_op jit(solution)/shard_map/ppermute | solution.py:145
  19.7 5.9 %collective-permute-start.7 = (f32[128,256]{1,0:T(8,128)S(1)}, f32[128,256]{1,0:T(8,128)S(1)}, u32[]{:S(2)}, u32[]{:S(2)}) collective-permute-start(f32[128,256]{1,0:T(8,128)S(1)} %add_add_fusion), channel_id=1, source_target_pairs={{0,4},{4,0},{8,12},{12,8},{16,20},{20,16},{24,28},{28,24},{1,5},{5... | collective-permute-start | bytes 393224 | tf_op jit(solution)/shard_map/ppermute | solution.py:148
  22.7 16.0 %collective-permute-start.3 = (f32[64,2048]{1,0:T(8,128)}, f32[64,2048]{1,0:T(8,128)}, u32[]{:S(2)}, u32[]{:S(2)}) collective-permute-start(f32[64,2048]{1,0:T(8,128)} %get-tuple-element.40), channel_id=1, source_target_pairs={{0,24},{4,28},{8,16},{12,20},{16,8},{20,12},{24,0},{28,4},{1,25},{... | collective-permute-start | bytes 1572872 | tf_op jit(solution)/shard_map/ppermute | solution.py:145
  24.3 25.2 %collective-permute-start.2 = (f32[64,2048]{1,0:T(8,128)}, f32[64,2048]{1,0:T(8,128)}, u32[]{:S(2)}, u32[]{:S(2)}) collective-permute-start(f32[64,2048]{1,0:T(8,128)} %get-tuple-element.41), channel_id=1, source_target_pairs={{0,16},{4,20},{8,24},{12,28},{16,0},{20,4},{24,8},{28,12},{1,17},{... | collective-permute-start | bytes 1572872 | tf_op jit(solution)/shard_map/ppermute | solution.py:145
  25.7 23.8 %collective-permute-start.1 = (f32[64,2048]{1,0:T(8,128)}, f32[64,2048]{1,0:T(8,128)}, u32[]{:S(2)}, u32[]{:S(2)}) collective-permute-start(f32[64,2048]{1,0:T(8,128)} %get-tuple-element.42), channel_id=1, source_target_pairs={{0,8},{4,12},{8,0},{12,4},{16,24},{20,28},{24,16},{28,20},{1,9},{5... | collective-permute-start | bytes 1572872 | tf_op jit(solution)/shard_map/ppermute | solution.py:145
  28.5 23.7 %collective-permute-start.12 = (f32[256,1024]{1,0:T(8,128)}, f32[256,1024]{1,0:T(8,128)S(1)}, u32[]{:S(2)}, u32[]{:S(2)}) collective-permute-start(f32[256,1024]{1,0:T(8,128)} %collective-permute-done.8), channel_id=1, source_target_pairs={{0,4},{4,0},{8,12},{12,8},{16,20},{20,16},{24,28},{28,24},{1,5},{5... | collective-permute-start | bytes 3145736 | tf_op jit(solution)/shard_map/ppermute | solution.py:148
  28.5 39.5 %collective-permute-start.11 = (f32[256,1024]{1,0:T(8,128)}, f32[256,1024]{1,0:T(8,128)}, u32[]{:S(2)}, u32[]{:S(2)}) collective-permute-start(f32[256,1024]{1,0:T(8,128)} %collective-permute-done.8), channel_id=1, source_target_pairs={{1,2},{2,1},{5,6},{6,5},{9,10},{10,9},{13,14},{14,13},{17,18},{18,... | collective-permute-start | bytes 3145736 | tf_op jit(solution)/shard_map/ppermute | solution.py:151
  38.7 29.3 %collective-permute-start.10 = (f32[256,1024]{1,0:T(8,128)}, f32[256,1024]{1,0:T(8,128)S(1)}, u32[]{:S(2)}, u32[]{:S(2)}) collective-permute-start(f32[256,1024]{1,0:T(8,128)} %collective-permute-done.9), channel_id=1, source_target_pairs={{1,0},{2,3},{5,4},{6,7},{9,8},{10,11},{13,12},{14,15},{17,16},{18,... | collective-permute-start | bytes 3145736 | tf_op jit(solution)/shard_map/ppermute | solution.py:151
  51.1 4.2 %copy-start = (f32[256,2048]{1,0:T(8,128)}, f32[256,2048]{1,0:T(8,128)S(1)}, u32[]{:S(2)}) copy-start(f32[256,2048]{1,0:T(8,128)S(1)} %pad_maximum_fusion) | copy-start | bytes 6291460
  54.1 1.3 copy-start.2
  56.5 11.7 %copy-start.5 = (f32[4,160,256]{2,1,0:T(8,128)}, f32[4,160,256]{2,1,0:T(8,128)S(1)}, u32[]{:S(2)}) copy-start(f32[4,160,256]{2,1,0:T(8,128)S(1)} %pad_maximum_fusion.4) | copy-start | bytes 1966084
  68.1 18.1 %collective-permute-start.20 = (f32[256,1024]{1,0:T(8,128)S(1)}, f32[256,1024]{1,0:T(8,128)}, u32[]{:S(2)}, u32[]{:S(2)}) collective-permute-start(f32[256,1024]{1,0:T(8,128)S(1)} %broadcast_select_fusion.1), channel_id=1, source_target_pairs={{0,4},{4,0},{8,12},{12,8},{16,20},{20,16},{24,28},{28,24},{1,5},{5... | collective-permute-start | bytes 3145736 | tf_op jit(solution)/shard_map/ppermute | solution.py:148
  69.1 9.0 %collective-permute-start.16 = (f32[160,256]{1,0:T(8,128)}, f32[160,256]{1,0:T(8,128)S(1)}, u32[]{:S(2)}, u32[]{:S(2)}) collective-permute-start(f32[160,256]{1,0:T(8,128)} %get-tuple-element.59), channel_id=1, source_target_pairs={{0,24},{4,28},{8,16},{12,20},{16,8},{20,12},{24,0},{28,4},{1,25},{... | collective-permute-start | bytes 491528 | tf_op jit(solution)/shard_map/ppermute | solution.py:145
  71.5 8.9 %collective-permute-start.15 = (f32[160,256]{1,0:T(8,128)}, f32[160,256]{1,0:T(8,128)}, u32[]{:S(2)}, u32[]{:S(2)}) collective-permute-start(f32[160,256]{1,0:T(8,128)} %get-tuple-element.60), channel_id=1, source_target_pairs={{0,16},{4,20},{8,24},{12,28},{16,0},{20,4},{24,8},{28,12},{1,17},{... | collective-permute-start | bytes 491528 | tf_op jit(solution)/shard_map/ppermute | solution.py:145
  72.0 8.5 %collective-permute-start.14 = (f32[160,256]{1,0:T(8,128)}, f32[160,256]{1,0:T(8,128)}, u32[]{:S(2)}, u32[]{:S(2)}) collective-permute-start(f32[160,256]{1,0:T(8,128)} %get-tuple-element.58), channel_id=1, source_target_pairs={{0,8},{4,12},{8,0},{12,4},{16,24},{20,28},{24,16},{28,20},{1,9},{5... | collective-permute-start | bytes 491528 | tf_op jit(solution)/shard_map/ppermute | solution.py:145
  73.2 9.4 %all-to-all-start = ((f32[4,32,256]{2,1,0:T(8,128)}), f32[4,32,256]{2,1,0:T(8,128)S(1)}, u32[]{:S(2)}, u32[]{:S(2)}) async-start(f32[4,32,256]{2,1,0:T(8,128)} %broadcast_in_dim.15), calls=%async_computation | async-start | bytes 262144 | tf_op jit(solution)/shard_map/all_to_all | solution.py:215
  76.5 28.3 %collective-permute-start.13 = (f32[256,1024]{1,0:T(8,128)}, f32[256,1024]{1,0:T(8,128)}, u32[]{:S(2)}, u32[]{:S(2)}) collective-permute-start(f32[256,1024]{1,0:T(8,128)} %collective-permute-done.11), channel_id=1, source_target_pairs={{1,0},{2,3},{5,4},{6,7},{9,8},{10,11},{13,12},{14,15},{17,16},{18,... | collective-permute-start | bytes 3145736 | tf_op jit(solution)/shard_map/ppermute | solution.py:151
  78.0 2.4 %copy-start.7 = (f32[160,256]{1,0:T(8,128)}, f32[160,256]{1,0:T(8,128)S(1)}, u32[]{:S(2)}) copy-start(f32[160,256]{1,0:T(8,128)S(1)} %collective-permute-done.16) | copy-start | bytes 491524
  82.7 13.6 %collective-permute-start.19 = (f32[288,256]{1,0:T(8,128)S(1)}, f32[288,256]{1,0:T(8,128)S(1)}, u32[]{:S(2)}, u32[]{:S(2)}) collective-permute-start(f32[288,256]{1,0:T(8,128)S(1)} %get-tuple-element.73), channel_id=1, source_target_pairs={{0,24},{4,28},{8,16},{12,20},{16,8},{20,12},{24,0},{28,4},{1,25},{... | collective-permute-start | bytes 884744 | tf_op jit(solution)/shard_map/ppermute | solution.py:145
  85.2 14.2 %collective-permute-start.18 = (f32[288,256]{1,0:T(8,128)S(1)}, f32[288,256]{1,0:T(8,128)S(1)}, u32[]{:S(2)}, u32[]{:S(2)}) collective-permute-start(f32[288,256]{1,0:T(8,128)S(1)} %get-tuple-element.73), channel_id=1, source_target_pairs={{0,16},{4,20},{8,24},{12,28},{16,0},{20,4},{24,8},{28,12},{1,17},{... | collective-permute-start | bytes 884744 | tf_op jit(solution)/shard_map/ppermute | solution.py:145
  85.7 15.2 %collective-permute-start.17 = (f32[288,256]{1,0:T(8,128)S(1)}, f32[288,256]{1,0:T(8,128)S(1)}, u32[]{:S(2)}, u32[]{:S(2)}) collective-permute-start(f32[288,256]{1,0:T(8,128)S(1)} %get-tuple-element.73), channel_id=1, source_target_pairs={{0,8},{4,12},{8,0},{12,4},{16,24},{20,28},{24,16},{28,20},{1,9},{5... | collective-permute-start | bytes 884744 | tf_op jit(solution)/shard_map/ppermute | solution.py:145
  88.1 1.6 copy-start.3
  90.9 1.6 copy-start.1
  93.7 7.2 %collective-permute-start.23 = (f32[128,256]{1,0:T(8,128)S(1)}, f32[128,256]{1,0:T(8,128)S(1)}, u32[]{:S(2)}, u32[]{:S(2)}) collective-permute-start(f32[128,256]{1,0:T(8,128)S(1)} %get-tuple-element.68), channel_id=1, source_target_pairs={{0,24},{4,28},{8,16},{12,20},{16,8},{20,12},{24,0},{28,4},{1,25},{... | collective-permute-start | bytes 393224 | tf_op jit(solution)/shard_map/ppermute | solution.py:145
  96.2 7.3 %collective-permute-start.22 = (f32[128,256]{1,0:T(8,128)S(1)}, f32[128,256]{1,0:T(8,128)S(1)}, u32[]{:S(2)}, u32[]{:S(2)}) collective-permute-start(f32[128,256]{1,0:T(8,128)S(1)} %get-tuple-element.69), channel_id=1, source_target_pairs={{0,16},{4,20},{8,24},{12,28},{16,0},{20,4},{24,8},{28,12},{1,17},{... | collective-permute-start | bytes 393224 | tf_op jit(solution)/shard_map/ppermute | solution.py:145
  99.4 5.4 %collective-permute-start.21 = (f32[128,256]{1,0:T(8,128)S(1)}, f32[128,256]{1,0:T(8,128)S(1)}, u32[]{:S(2)}, u32[]{:S(2)}) collective-permute-start(f32[128,256]{1,0:T(8,128)S(1)} %get-tuple-element.67), channel_id=1, source_target_pairs={{0,8},{4,12},{8,0},{12,4},{16,24},{20,28},{24,16},{28,20},{1,9},{5... | collective-permute-start | bytes 393224 | tf_op jit(solution)/shard_map/ppermute | solution.py:145
  106.3 4.0 %collective-permute-start.27 = (f32[256,1024]{1,0:T(8,128)S(1)}, f32[256,1024]{1,0:T(8,128)S(1)}, u32[]{:S(2)}, u32[]{:S(2)}) collective-permute-start(f32[256,1024]{1,0:T(8,128)S(1)} %broadcast_select_fusion), channel_id=1, source_target_pairs={{0,4},{4,0},{8,12},{12,8},{16,20},{20,16},{24,28},{28,24},{1,5},{5... | collective-permute-start | bytes 3145736 | tf_op jit(solution)/shard_map/ppermute | solution.py:148
  106.3 12.5 %collective-permute-start.26 = (f32[128,256]{1,0:T(8,128)S(1)}, f32[128,256]{1,0:T(8,128)S(1)}, u32[]{:S(2)}, u32[]{:S(2)}) collective-permute-start(f32[128,256]{1,0:T(8,128)S(1)} %fusion.40), channel_id=1, source_target_pairs={{0,24},{4,28},{8,16},{12,20},{16,8},{20,12},{24,0},{28,4},{1,25},{... | collective-permute-start | bytes 393224 | tf_op jit(solution)/shard_map/ppermute | solution.py:145
  108.5 11.0 %collective-permute-start.25 = (f32[128,256]{1,0:T(8,128)S(1)}, f32[128,256]{1,0:T(8,128)S(1)}, u32[]{:S(2)}, u32[]{:S(2)}) collective-permute-start(f32[128,256]{1,0:T(8,128)S(1)} %fusion.40), channel_id=1, source_target_pairs={{0,16},{4,20},{8,24},{12,28},{16,0},{20,4},{24,8},{28,12},{1,17},{... | collective-permute-start | bytes 393224 | tf_op jit(solution)/shard_map/ppermute | solution.py:145
  109.4 10.2 %collective-permute-start.24 = (f32[128,256]{1,0:T(8,128)S(1)}, f32[128,256]{1,0:T(8,128)S(1)}, u32[]{:S(2)}, u32[]{:S(2)}) collective-permute-start(f32[128,256]{1,0:T(8,128)S(1)} %fusion.40), channel_id=1, source_target_pairs={{0,8},{4,12},{8,0},{12,4},{16,24},{20,28},{24,16},{28,20},{1,9},{5... | collective-permute-start | bytes 393224 | tf_op jit(solution)/shard_map/ppermute | solution.py:145
  115.8 8.1 %collective-permute-start.30 = (f32[160,256]{1,0:T(8,128)S(1)}, f32[160,256]{1,0:T(8,128)S(1)}, u32[]{:S(2)}, u32[]{:S(2)}) collective-permute-start(f32[160,256]{1,0:T(8,128)S(1)} %get-tuple-element.56), channel_id=1, source_target_pairs={{0,24},{4,28},{8,16},{12,20},{16,8},{20,12},{24,0},{28,4},{1,25},{... | collective-permute-start | bytes 491528 | tf_op jit(solution)/shard_map/ppermute | solution.py:145
  118.0 8.0 %collective-permute-start.29 = (f32[160,256]{1,0:T(8,128)S(1)}, f32[160,256]{1,0:T(8,128)S(1)}, u32[]{:S(2)}, u32[]{:S(2)}) collective-permute-start(f32[160,256]{1,0:T(8,128)S(1)} %get-tuple-element.57), channel_id=1, source_target_pairs={{0,16},{4,20},{8,24},{12,28},{16,0},{20,4},{24,8},{28,12},{1,17},{... | collective-permute-start | bytes 491528 | tf_op jit(solution)/shard_map/ppermute | solution.py:145
  118.8 7.3 %collective-permute-start.28 = (f32[160,256]{1,0:T(8,128)S(1)}, f32[160,256]{1,0:T(8,128)S(1)}, u32[]{:S(2)}, u32[]{:S(2)}) collective-permute-start(f32[160,256]{1,0:T(8,128)S(1)} %get-tuple-element.55), channel_id=1, source_target_pairs={{0,8},{4,12},{8,0},{12,4},{16,24},{20,28},{24,16},{28,20},{1,9},{5... | collective-permute-start | bytes 491528 | tf_op jit(solution)/shard_map/ppermute | solution.py:145
  119.5 17.6 %collective-permute-start.34 = (f32[5,128,256]{2,1,0:T(8,128)S(1)}, f32[5,128,256]{2,1,0:T(8,128)S(1)}, u32[]{:S(2)}, u32[]{:S(2)}) collective-permute-start(f32[5,128,256]{2,1,0:T(8,128)S(1)} %bitcast.156), channel_id=1, source_target_pairs={{0,4},{4,0},{8,12},{12,8},{16,20},{20,16},{24,28},{28,24},{1,5},{5... | collective-permute-start | bytes 1966088 | tf_op jit(solution)/shard_map/ppermute | solution.py:148
  126.1 10.4 %collective-permute-start.33 = (f32[160,256]{1,0:T(8,128)S(1)}, f32[160,256]{1,0:T(8,128)S(1)}, u32[]{:S(2)}, u32[]{:S(2)}) collective-permute-start(f32[160,256]{1,0:T(8,128)S(1)} %fusion.35), channel_id=1, source_target_pairs={{0,24},{4,28},{8,16},{12,20},{16,8},{20,12},{24,0},{28,4},{1,25},{... | collective-permute-start | bytes 491528 | tf_op jit(solution)/shard_map/ppermute | solution.py:145
  127.8 8.6 %collective-permute-start.32 = (f32[160,256]{1,0:T(8,128)S(1)}, f32[160,256]{1,0:T(8,128)S(1)}, u32[]{:S(2)}, u32[]{:S(2)}) collective-permute-start(f32[160,256]{1,0:T(8,128)S(1)} %fusion.35), channel_id=1, source_target_pairs={{0,16},{4,20},{8,24},{12,28},{16,0},{20,4},{24,8},{28,12},{1,17},{... | collective-permute-start | bytes 491528 | tf_op jit(solution)/shard_map/ppermute | solution.py:145
  129.1 7.7 %collective-permute-start.31 = (f32[160,256]{1,0:T(8,128)S(1)}, f32[160,256]{1,0:T(8,128)S(1)}, u32[]{:S(2)}, u32[]{:S(2)}) collective-permute-start(f32[160,256]{1,0:T(8,128)S(1)} %fusion.35), channel_id=1, source_target_pairs={{0,8},{4,12},{8,0},{12,4},{16,24},{20,28},{24,16},{28,20},{1,9},{5... | collective-permute-start | bytes 491528 | tf_op jit(solution)/shard_map/ppermute | solution.py:145
  129.9 8.3 %collective-permute-start.35 = (f32[2,128,256]{2,1,0:T(8,128)S(1)}, f32[2,128,256]{2,1,0:T(8,128)S(1)}, u32[]{:S(2)}, u32[]{:S(2)}) collective-permute-start(f32[2,128,256]{2,1,0:T(8,128)S(1)} %bitcast.188), channel_id=1, source_target_pairs={{0,4},{4,0},{8,12},{12,8},{16,20},{20,16},{24,28},{28,24},{1,5},{5... | collective-permute-start | bytes 786440 | tf_op jit(solution)/shard_map/ppermute | solution.py:148
  137.0 1.8 %collective-permute-start.36 = (f32[3,128,256]{2,1,0:T(8,128)S(1)}, f32[3,128,256]{2,1,0:T(8,128)S(1)}, u32[]{:S(2)}, u32[]{:S(2)}) collective-permute-start(f32[3,128,256]{2,1,0:T(8,128)S(1)} %bitcast.179), channel_id=1, source_target_pairs={{0,4},{4,0},{8,12},{12,8},{16,20},{20,16},{24,28},{28,24},{1,5},{5... | collective-permute-start | bytes 1179656 | tf_op jit(solution)/shard_map/ppermute | solution.py:148
  137.2 1.1 copy-start.4
  138.2 1.0 slice-start
  148.5 14.8 %collective-permute-start.37 = (f32[64,2048]{1,0:T(8,128)S(1)}, f32[64,2048]{1,0:T(8,128)S(1)}, u32[]{:S(2)}, u32[]{:S(2)}) collective-permute-start(f32[64,2048]{1,0:T(8,128)S(1)} %get-tuple-element.37), channel_id=1, source_target_pairs={{0,8},{4,12},{8,0},{12,4},{16,24},{20,28},{24,16},{28,20},{1,9},{5... | collective-permute-start | bytes 1572872 | tf_op jit(solution)/shard_map/ppermute | solution.py:145
  150.0 25.3 %collective-permute-start.38 = (f32[64,2048]{1,0:T(8,128)S(1)}, f32[64,2048]{1,0:T(8,128)S(1)}, u32[]{:S(2)}, u32[]{:S(2)}) collective-permute-start(f32[64,2048]{1,0:T(8,128)S(1)} %get-tuple-element.36), channel_id=1, source_target_pairs={{0,16},{4,20},{8,24},{12,28},{16,0},{20,4},{24,8},{28,12},{1,17},{... | collective-permute-start | bytes 1572872 | tf_op jit(solution)/shard_map/ppermute | solution.py:145
  150.6 24.8 %collective-permute-start.39 = (f32[64,2048]{1,0:T(8,128)S(1)}, f32[64,2048]{1,0:T(8,128)S(1)}, u32[]{:S(2)}, u32[]{:S(2)}) collective-permute-start(f32[64,2048]{1,0:T(8,128)S(1)} %get-tuple-element.35), channel_id=1, source_target_pairs={{0,24},{4,28},{8,16},{12,20},{16,8},{20,12},{24,0},{28,4},{1,25},{... | collective-permute-start | bytes 1572872 | tf_op jit(solution)/shard_map/ppermute | solution.py:145
  175.3 1.3 copy-start.6

commit v3 on v0

--- a/solution.py
+++ b/solution.py
@@ -1,6 +1,10 @@
+import functools
+
 import jax
 import jax.numpy as jnp
 from jax import lax
+from jax.experimental import pallas as pl
+from jax.experimental.pallas import tpu as pltpu
 from jax.sharding import PartitionSpec as P
 
 B = 256
@@ -35,7 +39,7 @@
     return solved
 
 
-def shards(eigvecs, reflectors):
+def general(eigvecs, reflectors):
     current = lax.all_to_all(eigvecs, "row", split_axis=1, concat_axis=0, tiled=True)
     gathered = lax.all_gather(reflectors, "col", axis=0, tiled=True)
     local_rows = current.shape[1]
@@ -55,8 +59,304 @@
     return lax.all_to_all(current, "row", split_axis=0, concat_axis=1, tiled=True)
 
 
+LITTLE = pl.CostEstimate(flops=1, bytes_accessed=1, transcendentals=0)
+NT = (((1,), (1,)), ((), ()))
+NN = (((1,), (0,)), ((), ()))
+
+
+def split(value):
+    high = value.astype(jnp.bfloat16)
+    return high, (value - high.astype(jnp.float32)).astype(jnp.bfloat16)
+
+
+def dot3(left, right, dims):
+    def part(a, b):
+        return lax.dot_general(a, b, dims, preferred_element_type=jnp.float32)
+
+    return part(left[0], right[0]) + (part(left[0], right[1]) + part(left[1], right[0]))
+
+
+def fdot(left, right, dims=NN):
+    return dot3(split(left), split(right), dims)
+
+
+def call(kernel, out_shape, *operands, scratch=(), limit=16):
+    return pl.pallas_call(
+        kernel,
+        out_shape=out_shape,
+        in_specs=[pl.BlockSpec(memory_space=pltpu.SMEM)]
+        + [pl.BlockSpec(memory_space=pltpu.VMEM)] * (len(operands) - 1),
+        out_specs=jax.tree.map(lambda _: pl.BlockSpec(memory_space=pltpu.VMEM), out_shape),
+        scratch_shapes=list(scratch),
+        cost_estimate=LITTLE,
+        compiler_params=pltpu.CompilerParams(vmem_limit_bytes=limit * 2**20),
+    )(*operands)
+
+
+def own_rows(place, x, part):
+    return pl.multiple_of(place[0] * (B // 2) + (place[1] ^ x) * part, part)
+
+
+def place_rows(chips, place, dest, index, ref, begin, sib, sib_begin):
+    part = B // 2 // chips
+    for x in range(chips):
+        at = pl.multiple_of(place[0] * (B // 2) + (place[1] ^ x) * part, part)
+        dest[index, pl.ds(at, part), :] = ref[x, begin : begin + part]
+        at = pl.multiple_of((1 - place[0]) * (B // 2) + (place[1] ^ x) * part, part)
+        dest[index, pl.ds(at, part), :] = sib[x, sib_begin : sib_begin + part]
+
+
+def product_kernel(chips, plan, choice, lefts, place, *refs):
+    e_ref, out_ref, kept = refs[0], refs[-5], refs[-4:]
+    groups, at = [], 1
+    while at < len(refs) - 5:
+        size = 4 if len(groups) == choice else 2
+        groups.append(refs[at : at + size])
+        at += size
+    edge = place[2] == 1
+    width = e_ref.shape[1] // 2
+    step = min(width, 512)
+    mine = e_ref.shape[0] // chips
+    part = B // 2 // chips
+
+    def read(slot, h, rows, cols):
+        group = groups[slot]
+        if len(group) == 2:
+            return group[h][rows, cols]
+        return jnp.where(edge, group[h][rows, cols], group[2 + h][rows, cols])
+
+    totals = [None] * len(plan)
+    for h in range(2):
+        for k in range(0, width, step):
+            at = pl.multiple_of((place[0] ^ h) * width + k, step)
+            cols = slice(k, k + step)
+            left = [e_ref[:, pl.ds(at, step)]]
+            for j in range(lefts):
+                left += [read(j, h, pl.ds(own_rows(place, x, part), part), cols) for x in range(chips)]
+            both = split(jnp.concatenate(left))
+            for i, (target, used) in enumerate(plan):
+                rows = chips * mine + used * (B // 2)
+                right = split(read(target, h, slice(None), cols))
+                for ref, value in zip(kept[2 * h : 2 * h + 2], right):
+                    ref[i * B : (i + 1) * B, cols] = value
+                value = dot3(tuple(b[:rows] for b in both), right, NT)
+                totals[i] = value if totals[i] is None else totals[i] + value
+    begin = 0
+    for value in totals:
+        for x in range(chips):
+            out_ref[x, begin : begin + mine] = value[x * mine : (x + 1) * mine]
+        begin += mine
+    for (_, used), value in zip(plan, totals):
+        for j in range(used):
+            for x in range(chips):
+                at = chips * mine + j * (B // 2) + x * part
+                out_ref[x, begin : begin + part] = value[at : at + part]
+            begin += part
+
+
+def inverse_kernel(chips, mine, place, f01, f2, fb, s01, s2, sb, out_ref, g_ref, high_ref, low_ref, gram_ref):
+    part = B // 2 // chips
+
+    def stored(dest, index, ref, at, sib):
+        place_rows(chips, place, dest, index, ref, at * part + (2 * mine if ref is f01 else mine if ref is f2 else 0), sib, at * part)
+
+    for slot, (ref, at, sib) in enumerate(((f01, 0, s01), (f01, 2, s01), (f2, 2, s2), (fb, 2, sb))):
+        stored(gram_ref, slot, ref, at, sib)
+    pairs = ((f01, 1, s01), (f2, 0, s2), (f2, 1, s2), (fb, 1, sb), (fb, 0, sb), (fb, 3, sb), (f2, 3, s2))
+    for index, (ref, at, sib) in enumerate(pairs):
+        stored(g_ref, index, ref, at, sib)
+    for slot, value in enumerate((f01[:, :mine], f01[:, mine : 2 * mine], f2[:, :mine])):
+        high, low = split(value.reshape(chips * mine, B))
+        high_ref[:, slot * B : (slot + 1) * B] = high
+        low_ref[:, slot * B : (slot + 1) * B] = low
+    half = B // 2
+    rows = lax.broadcasted_iota(jnp.int32, (half, half), 0)
+    cols = lax.broadcasted_iota(jnp.int32, (half, half), 1)
+    grams = [gram_ref[i, k : k + half, k : k + half] for i in range(PANELS) for k in (0, half)]
+    inv = [jnp.where(rows == cols, 2.0 / gram, 0.0) for gram in grams]
+    size = 1
+    while size < half:
+        pick = (rows // (2 * size) == cols // (2 * size)) & (rows % (2 * size) >= size) & (cols % (2 * size) < size)
+        inner = [fdot(i, jnp.where(pick, gram, 0.0)) for i, gram in zip(inv, grams)]
+        inv = [i - fdot(t, i) for i, t in zip(inv, inner)]
+        size *= 2
+    for i in range(PANELS):
+        first, second = inv[2 * i], inv[2 * i + 1]
+        out_ref[i, :half, :half] = first
+        out_ref[i, :half, half:] = jnp.zeros((half, half), jnp.float32)
+        out_ref[i, half:, :half] = -fdot(fdot(second, gram_ref[i, half:, :half]), first)
+        out_ref[i, half:, half:] = second
+
+
+def combine_kernel(place, t_ref, g_ref, high_ref, low_ref):
+    edge, c = place[2], place[3]
+    lower, inverses, whole = {}, {}, {}
+    for which in range(PANELS):
+        inverses[which] = t_ref[c ^ which]
+        whole[which, which] = split(inverses[which])
+        for later in range(which + 1, PANELS):
+            slot, other = c ^ which, c ^ later
+            low, high = jnp.minimum(slot, other), jnp.maximum(slot, other)
+            turned = jnp.where((low == 2) & (edge == 0), 1, 0)
+            gram = g_ref[high * (high - 1) // 2 + low + turned]
+            row_slot = jnp.where(turned == 1, high, low)
+            lower[later, which] = jnp.where(other == row_slot, gram, gram.T)
+    for which in reversed(range(PANELS - 1)):
+        scaled = [fdot(lower[r, which], inverses[which]) for r in range(which + 1, PANELS)]
+        scaled = [split(s) for s in scaled]
+        for later in range(which + 1, PANELS):
+            value = None
+            for r in range(which + 1, later + 1):
+                term = dot3(whole[later, r], scaled[r - which - 1], NN)
+                value = term if value is None else value + term
+            whole[later, which] = split(-value)
+    zeros = jnp.zeros((B, B), jnp.bfloat16)
+    for q in range(PANELS):
+        for p in range(PANELS):
+            high, low = whole.get((q, p), (zeros, zeros))
+            rows = pl.ds(pl.multiple_of((c ^ q) * B, B), B)
+            cols = pl.ds(pl.multiple_of((c ^ p) * B, B), B)
+            high_ref[rows, cols] = high
+            low_ref[rows, cols] = low
+
+
+def apply_kernel(chips, mine, place, p_high, p_low, f3, m_high, m_low, high_ref, low_ref):
+    early = (PANELS - 1) * B
+    solved = dot3((p_high[...], p_low[...]), (m_high[:early], m_low[:early]), NN)
+    solved = solved + dot3(split(f3[...].reshape(chips * mine, B)), (m_high[early:], m_low[early:]), NN)
+    high_ref[...], low_ref[...] = split(solved)
+
+
+def update_kernel(chips, half, place, e_ref, s_high, s_low, *refs):
+    out_ref = refs[-1]
+    width = out_ref.shape[-1]
+    mine = out_ref.shape[1]
+    step = min(width, 512)
+    for k in range(0, width, step):
+        at = pl.multiple_of((place[0] ^ half) * width + k, step)
+        value = e_ref[:, pl.ds(at, step)]
+        begin = 0
+        for high, low in zip(refs[:-1:2], refs[1:-1:2]):
+            rows = slice(begin, begin + high.shape[0])
+            begin += high.shape[0]
+            cols = slice(k, k + step)
+            value = value - dot3((s_high[:, rows], s_low[:, rows]), (high[:, cols], low[:, cols]), NN)
+        out_ref[:, :, k : k + step] = value.reshape(chips, mine, step)
+
+
+def panels_on_cols(eigvecs, reflectors, chips):
+    width = reflectors.shape[1]
+    r, c = lax.axis_index("row"), lax.axis_index("col")
+    core, chip = r % 2, r // 2
+    edge = (c == 0) | (c == 3)
+    place = jnp.stack([core, chip, edge, c]).astype(jnp.int32)
+    mine = eigvecs.shape[0]
+    part = B // 2 // chips
+    f32 = lambda *shape: jax.ShapeDtypeStruct(shape, jnp.float32)
+    b16 = lambda *shape: jax.ShapeDtypeStruct(shape, jnp.bfloat16)
+
+    def across(value, x):
+        return lax.ppermute(value, "row", [(i, i ^ (2 * x)) for i in range(2 * chips)])
+
+    def sibling(value):
+        return lax.ppermute(value, "row", [(i, i ^ 1) for i in range(2 * chips)])
+
+    def zmove(value, pairs):
+        return lax.ppermute(value, "col", pairs)
+
+    def scatter(packed):
+        held = packed[0]
+        for x in range(1, chips):
+            held = held + across(packed[x], x)
+        return held
+
+    def collect(held):
+        return jnp.stack([held] + [across(held, x) for x in range(1, chips)])
+
+    def products(plan, choice, lefts, *operands):
+        rows = sum(mine + used * part for _, used in plan)
+        kernel = functools.partial(product_kernel, chips, plan, choice, lefts)
+        kept = b16(len(plan) * B, width)
+        return call(kernel, (f32(chips, rows, B), kept, kept, kept, kept), place, grid, *operands, limit=40)
+
+    vectors = masked_vectors(reflectors, c, r * width)
+    vectors, eigvecs = lax.optimization_barrier((vectors, eigvecs))
+    near = zmove(vectors, [(0, 1), (1, 0), (2, 3), (3, 2)])
+    inner = zmove(vectors, [(1, 2), (2, 1)])
+    pieces = [lax.dynamic_slice(eigvecs, (0, (chip ^ x) * 2 * width), (mine, 2 * width)) for x in range(chips)]
+    grid = jnp.concatenate(pieces[:1] + [across(pieces[x], x) for x in range(1, chips)])
+    grid, near, inner, vectors = lax.optimization_barrier((grid, near, inner, vectors))
+
+    second_out = zmove(inner, [(1, 0), (2, 3)])
+    second_in = zmove(near, [(1, 2), (2, 1)])
+    zero, one = (vectors, sibling(vectors)), (near, sibling(near))
+    packed_01, *kept_01 = products(((0, 1), (1, 2)), -1, 2, *zero, *one)
+    held_01 = scatter(packed_01)
+    from_01 = [across(held_01, x) for x in range(1, chips)]
+    second_out, second_in, from_01[0] = lax.optimization_barrier((second_out, second_in, from_01[0]))
+
+    third_out = zmove(second_in, [(1, 0), (2, 3)])
+    two = (second_out, sibling(second_out), second_in, sibling(second_in))
+    full_01 = jnp.stack([held_01] + from_01)
+    inner_o = sibling(inner)
+    packed_2, *kept_2 = products(((2, 4),), 2, 4, *zero, *one, *two, inner, inner_o)
+    held_2 = scatter(packed_2)
+    partner = zmove(held_2[mine:], [(0, 1), (1, 0), (2, 3), (3, 2)])
+    full_2 = collect(held_2)
+    sib_01 = sibling(full_01[:, 2 * mine :])
+    third_out, full_01, sib_01, full_2, partner = lax.optimization_barrier((third_out, full_01, sib_01, full_2, partner))
+
+    third_o, full_2 = lax.optimization_barrier((sibling(third_out), full_2))
+    packed_3, *kept_3 = products(((0, 0),), 0, 0, third_out, third_o, inner, inner_o)
+    from_b = [across(partner, x) for x in range(1, chips)]
+    from_b, _ = lax.optimization_barrier((from_b, packed_3))
+    full_b = jnp.stack([partner] + from_b)
+    sib_2, sib_b = sibling(full_2[:, mine:]), sibling(full_b)
+    early = b16(chips * mine, (PANELS - 1) * B)
+    inverses, grams, *p_early = call(
+        functools.partial(inverse_kernel, chips, mine),
+        (f32(PANELS, B, B), f32(7, B, B), early, early),
+        place,
+        *(full_01, full_2, full_b, sib_01, sib_2, sib_b),
+        scratch=[pltpu.VMEM((PANELS, B, B), jnp.float32)],
+        limit=24,
+    )
+    from_3 = [across(packed_3[x], x) for x in range(1, chips)]
+    from_3, inverses = lax.optimization_barrier((from_3, inverses))
+    held_3 = sum(from_3, packed_3[0])
+    whole = b16(PANELS * B, PANELS * B)
+    inverse = call(combine_kernel, (whole, whole), place, inverses, grams, limit=32)
+    from_3 = [across(held_3, x) for x in range(1, chips)]
+    from_3, inverse = lax.optimization_barrier((from_3, inverse))
+    full_3 = jnp.stack([held_3] + from_3)
+    solved = b16(chips * mine, PANELS * B)
+    solved = call(
+        functools.partial(apply_kernel, chips, mine), (solved, solved), place, *p_early, full_3, *inverse, limit=24
+    )
+    result = jnp.zeros_like(eigvecs)
+    for half in range(2):
+        done = call(
+            functools.partial(update_kernel, chips, half),
+            f32(chips, mine, width),
+            place,
+            *(grid, *solved),
+            *(kept_01[2 * half : 2 * half + 2] + kept_2[2 * half : 2 * half + 2] + kept_3[2 * half : 2 * half + 2]),
+            limit=32,
+        )
+        for x in range(chips):
+            piece = across(done[x], x) if x else done[x]
+            start = (chip ^ x) * 2 * width + (core ^ half) * width
+            result = lax.dynamic_update_slice(result, piece, (0, start))
+    return result
+
+
 def solution(mesh):
+    rows, cols = mesh.shape["row"], mesh.shape["col"]
     placed = (P(("row", "col"), None), P("col", "row"))
-    return jax.shard_map(
-        shards, mesh=mesh, in_specs=placed, out_specs=P(("row", "col"), None), check_vma=False
-    )
+
+    def shards(eigvecs, reflectors):
+        if cols == PANELS and reflectors.shape[0] == B and rows >= 4 and rows & (rows - 1) == 0 and B % (16 * rows) == 0:
+            return panels_on_cols(eigvecs, reflectors, rows // 2)
+        return general(eigvecs, reflectors)
+
+    return jax.shard_map(shards, mesh=mesh, in_specs=placed, out_specs=P(("row", "col"), None), check_vma=False)

time: 438 us -> 163 us (0.37); the launches traced: 430 us -> 163 us
  waiting for transfers between devices: 261 us -> 72.3 us
  matrix products: 74.1 us -> 0 us
  starting transfers between devices: 5.55 us -> 49.9 us
  local copies, waits for them, and re-layouts: 43.5 us -> 8.37 us
  blocking collectives: 29 us -> 0 us
  Pallas kernels: 0 us -> 28.3 us
  between operations: 14.5 us -> 0.71 us
    psum x4 -> x0, waiting for transfers between devices: 183 us -> none  [shards(): summed = lax.psum(partial_value, 'row')]
    all_gather x1 -> x0, waiting for transfers between devices: 76.7 us -> none  [shards(): gathered = lax.all_gather(reflectors, 'col', axis=0, tiled=True)]
    dot_general x72 -> x0, matrix products: 74.1 us -> none  [hdot(): jnp.dot(left, right, precision=lax.Precision.HIGHEST, preferred_element_t...]
    ppermute x0 -> x45, waiting for transfers between devices: none -> 72.3 us  [the longest x30 63.9 us: across(): lax.ppermute(value, 'row', [(i, i ^ 2 * x) for i in range(2 * chips)])]
    ppermute x0 -> x45, starting transfers between devices: none -> 49.9 us  [the longest x30 36.6 us: across(): lax.ppermute(value, 'row', [(i, i ^ 2 * x) for i in range(2 * chips)])]
    gather x8 -> x0, local copies, waits for them, and re-layouts: 30.6 us -> none  [the longest x4 21.2 us: apply_inverse(): diagonal = jnp.diagonal(factor)]
    all_to_all x1 -> x0, blocking collectives: 29 us -> none  [shards(): lax.all_to_all(current, 'row', split_axis=0, concat_axis=1, tiled=True)]
    pallas_call x0 -> x8, Pallas kernels: none -> 28.3 us  [call(): pl.pallas_call(kernel, out_shape=out_shape, in_specs=[pl.BlockSpec(memory...]
  transfers between devices with their start and end apart: 6 -> 45, of which waited for: 5 -> 22; matrix products, arithmetic and copies ran while one was open for 10% -> 1% of each run, Pallas kernels for 0% -> 14%
where the time goes in v3:
time: 163 us
  waiting for transfers between devices  72.3 us (44%)
  starting transfers between devices  49.9 us (31%)
  Pallas kernels  28.3 us (17%)
  local copies, waits for them, and re-layouts  8.37 us (5%)
  other arithmetic  3.65 us (2%)
    ppermute x30, waiting for transfers between devices, across(): lax.ppermute(value, 'row', [(i, i ^ 2 * x) for i in range(2 * chips)])  63.9 us
    ppermute x30, starting transfers between devices, across(): lax.ppermute(value, 'row', [(i, i ^ 2 * x) for i in range(2 * chips)])  36.6 us
    pallas_call x8, Pallas kernels, call(): pl.pallas_call(kernel, out_shape=out_shape, in_specs=[pl.BlockSpec(memory...  28.3 us
    ppermute x6, starting transfers between devices, zmove(): return lax.ppermute(value, 'col', pairs)  11.5 us
    unnamed x64, local copies, waits for them, and re-layouts  6.87 us
    ppermute x6, waiting for transfers between devices, zmove(): return lax.ppermute(value, 'col', pairs)  6.47 us
  transfers between devices with their start and end apart: 45, of which 22 were waited for; matrix products, arithmetic and copies ran while one was open for 1% of the time, Pallas kernels for 14%

profile of v3, /device:TPU:0, one launch (start us, length us, event | category | flops | bytes accessed | tf_op | source)
XLA Modules:
  0.0 163.2 jit_solution(1739626212557094278)
XLA Ops:
  0.0 1.6 select_select_fusion.refs_1_
  1.6 3.1 %collective-permute-start.3 = (f32[256,1024]{1,0:T(8,128)S(1)}, f32[256,1024]{1,0:T(8,128)}, u32[]{:S(2)}, u32[]{:S(2)}) collective-permute-start(f32[256,1024]{1,0:T(8,128)S(1)} %select_select_fusion.refs_1_), channel_id=1, source_target_pairs={{0,1},{1,0},{2,3},{3,2},{4,5},{5,4},{6,7},{7,6},{8,9},{9,8},{10,11... | collective-permute-start | bytes 3145736 | tf_op jit(solution)/shard_map/ppermute | solution.py:265
  4.7 1.6 %collective-permute-start.4 = (f32[256,1024]{1,0:T(8,128)S(1)}, f32[256,1024]{1,0:T(8,128)}, u32[]{:S(2)}, u32[]{:S(2)}) collective-permute-start(f32[256,1024]{1,0:T(8,128)S(1)} %select_select_fusion.refs_1_), channel_id=1, source_target_pairs={{1,2},{2,1},{5,6},{6,5},{9,10},{10,9},{13,14},{14,13},{17,18},{18,... | collective-permute-start | bytes 3145736 | tf_op jit(solution)/shard_map/ppermute | solution.py:265
  6.5 1.6 collective-permute-start
  8.1 1.5 collective-permute-start.1
  10.1 11.4 %collective-permute-done = f32[64,2048]{1,0:T(8,128)S(1)} collective-permute-done((f32[64,2048]{1,0:T(8,128)S(1)}, f32[64,2048]{1,0:T(8,128)S(1)}, u32[]{:S(2)}, u32[]{:S(2)}) %collective-permute-start) | collective-permute-done | bytes 524320 | tf_op jit(solution)/shard_map/ppermute | solution.py:259
  21.4 11.0 %collective-permute-done.1 = f32[64,2048]{1,0:T(8,128)S(1)} collective-permute-done((f32[64,2048]{1,0:T(8,128)S(1)}, f32[64,2048]{1,0:T(8,128)S(1)}, u32[]{:S(2)}, u32[]{:S(2)}) %collective-permute-start.1) | collective-permute-done | bytes 524320 | tf_op jit(solution)/shard_map/ppermute | solution.py:259
  33.9 1.3 collective-permute-start.5
  35.3 0.9 collective-permute-done.7.refs_2_
  36.1 1.0 collective-permute-done.8.refs_4_
  37.2 5.0 %shard_map.28 = (f32[4,224,256]{2,1,0:T(8,128)S(1)}, bf16[512,1024]{1,0:T(8,128)(2,1)S(1)}, bf16[512,1024]{1,0:T(8,128)(2,1)S(1)}, bf16[512,1024]{1,0:T(8,128)(2,1)S(1)}, bf16[512,1024]{1,0:T(8,128)(2,1)S(1)}) custom-call(s32[4]{0:T(128)S(1)} %pad_add_fusion.place, f32[256,2048]{1,0:T(8,128)S(1)} %pad_maximum_fusion.refs_0_.e_ref, ...), custom_call_target="tpu_custom_call" | custom-call | flops 1 | bytes 1 | tf_op jit(solution)/shard_map/pallas_call | solution.py:84
  42.2 1.0 copy-done.8
  43.2 1.0 copy-done.10
  44.3 1.6 collective-permute-start.10
  45.8 1.2 collective-permute-start.11
  47.0 0.8 collective-permute-start.9
  47.8 9.1 %collective-permute-done.10 = f32[224,256]{1,0:T(8,128)S(1)} collective-permute-done((f32[224,256]{1,0:T(8,128)S(1)}, f32[224,256]{1,0:T(8,128)S(1)}, u32[]{:S(2)}, u32[]{:S(2)}) %collective-permute-start.10) | collective-permute-done | bytes 229408 | tf_op jit(solution)/shard_map/ppermute | solution.py:259
  56.9 1.2 collective-permute-done.9
  58.2 1.3 collective-permute-start.12
  59.5 3.7 %collective-permute-done.5.refs_5_ = f32[256,1024]{1,0:T(8,128)S(1)} collective-permute-done((f32[256,1024]{1,0:T(8,128)}, f32[256,1024]{1,0:T(8,128)S(1)}, u32[]{:S(2)}, u32[]{:S(2)}) %collective-permute-start.5) | collective-permute-done | bytes 1048608 | tf_op jit(solution)/shard_map/ppermute | solution.py:265
  63.2 1.6 collective-permute-done.12
  65.3 1.5 collective-permute-start.13
  66.7 1.6 collective-permute-start.14
  68.4 1.2 collective-permute-start.15
  69.5 5.8 %shard_map.29 = (f32[4,192,256]{2,1,0:T(8,128)S(1)}, bf16[256,1024]{1,0:T(8,128)(2,1)S(1)}, bf16[256,1024]{1,0:T(8,128)(2,1)S(1)}, bf16[256,1024]{1,0:T(8,128)(2,1)S(1)}, bf16[256,1024]{1,0:T(8,128)(2,1)S(1)}) custom-call(s32[4]{0:T(128)S(1)} %pad_add_fusion.place, f32[256,2048]{1,0:T(8,128)} %copy-done, f32[256,1024]{1,0:T(8,128)S(1)} %select_select_fusion.refs_1_, ...), custom_call_target="tpu_custom_call" | custom-call | flops 1 | bytes 1 | tf_op jit(solution)/shard_map/pallas_call | solution.py:84
  75.4 0.8 collective-permute-start.20
  76.3 1.5 collective-permute-start.21
  77.8 2.1 %collective-permute-done.14 = f32[224,256]{1,0:T(8,128)S(1)} collective-permute-done((f32[224,256]{1,0:T(8,128)S(1)}, f32[224,256]{1,0:T(8,128)S(1)}, u32[]{:S(2)}, u32[]{:S(2)}) %collective-permute-start.14) | collective-permute-done | bytes 229408 | tf_op jit(solution)/shard_map/ppermute | solution.py:259
  79.8 1.2 collective-permute-start.22
  81.8 5.9 %collective-permute-done.21 = f32[192,256]{1,0:T(8,128)S(1)} collective-permute-done((f32[192,256]{1,0:T(8,128)S(1)}, f32[192,256]{1,0:T(8,128)S(1)}, u32[]{:S(2)}, u32[]{:S(2)}) %collective-permute-start.21) | collective-permute-done | bytes 196640 | tf_op jit(solution)/shard_map/ppermute | solution.py:259
  87.8 1.3 collective-permute-start.23
  89.1 0.8 collective-permute-start.24
  89.9 1.4 collective-permute-start.25
  91.3 3.9 %collective-permute-done.23 = f32[192,256]{1,0:T(8,128)S(1)} collective-permute-done((f32[192,256]{1,0:T(8,128)S(1)}, f32[192,256]{1,0:T(8,128)S(1)}, u32[]{:S(2)}, u32[]{:S(2)}) %collective-permute-start.23) | collective-permute-done | bytes 196640 | tf_op jit(solution)/shard_map/ppermute | solution.py:259
  95.3 3.3 %collective-permute-start.26 = (f32[128,256]{1,0:T(8,128)S(1)}, f32[128,256]{1,0:T(8,128)S(1)}, u32[]{:S(2)}, u32[]{:S(2)}) collective-permute-start(f32[128,256]{1,0:T(8,128)S(1)} %slice.93), channel_id=1, source_target_pairs={{0,1},{1,0},{2,3},{3,2},{4,5},{5,4},{6,7},{7,6},{8,9},{9,8},{10,11... | collective-permute-start | bytes 393224 | tf_op jit(solution)/shard_map/ppermute | solution.py:265
  98.8 2.8 %collective-permute-done.26 = f32[128,256]{1,0:T(8,128)S(1)} collective-permute-done((f32[128,256]{1,0:T(8,128)S(1)}, f32[128,256]{1,0:T(8,128)S(1)}, u32[]{:S(2)}, u32[]{:S(2)}) %collective-permute-start.26) | collective-permute-done | bytes 131104 | tf_op jit(solution)/shard_map/ppermute | solution.py:265
  102.1 1.8 %collective-permute-start.29 = (f32[128,256]{1,0:T(8,128)S(1)}, f32[128,256]{1,0:T(8,128)S(1)}, u32[]{:S(2)}, u32[]{:S(2)}) collective-permute-start(f32[128,256]{1,0:T(8,128)S(1)} %collective-permute-done.26), channel_id=1, source_target_pairs={{0,16},{4,20},{8,24},{12,28},{16,0},{20,4},{24,8},{28,12},{1,17},{... | collective-permute-start | bytes 393224 | tf_op jit(solution)/shard_map/ppermute | solution.py:259
  103.9 1.1 collective-permute-start.30
  105.0 2.6 %shard_map.30 = (f32[4,64,256]{2,1,0:T(8,128)S(1)}, bf16[256,1024]{1,0:T(8,128)(2,1)S(1)}, bf16[256,1024]{1,0:T(8,128)(2,1)S(1)}, bf16[256,1024]{1,0:T(8,128)(2,1)S(1)}, bf16[256,1024]{1,0:T(8,128)(2,1)S(1)}) custom-call(s32[4]{0:T(128)S(1)} %pad_add_fusion.place, f32[256,2048]{1,0:T(8,128)S(1)} %copy-done.1, ...), custom_call_target="tpu_custom_call" | custom-call | flops 1 | bytes 1 | tf_op jit(solution)/shard_map/pallas_call | solution.py:84
  107.8 2.1 %collective-permute-done.29 = f32[128,256]{1,0:T(8,128)S(1)} collective-permute-done((f32[128,256]{1,0:T(8,128)S(1)}, f32[128,256]{1,0:T(8,128)S(1)}, u32[]{:S(2)}, u32[]{:S(2)}) %collective-permute-start.29) | collective-permute-done | bytes 131104 | tf_op jit(solution)/shard_map/ppermute | solution.py:259
  109.9 1.5 collective-permute-done.30
  112.9 1.7 %collective-permute-start.34 = (f32[64,256]{1,0:T(8,128)S(1)}, f32[64,256]{1,0:T(8,128)S(1)}, u32[]{:S(2)}, u32[]{:S(2)}) collective-permute-start(f32[64,256]{1,0:T(8,128)S(1)} %get-tuple-element.124), channel_id=1, source_target_pairs={{0,16},{4,20},{8,24},{12,28},{16,0},{20,4},{24,8},{28,12},{1,17},{... | collective-permute-start | bytes 196616 | tf_op jit(solution)/shard_map/ppermute | solution.py:259
  114.5 1.2 collective-permute-start.35
  115.7 4.5 %shard_map.31 = (f32[4,256,256]{2,1,0:T(8,128)S(1)}, f32[7,256,256]{2,1,0:T(8,128)S(1)}, bf16[256,768]{1,0:T(8,128)(2,1)S(1)}, bf16[256,768]{1,0:T(8,128)(2,1)S(1)}) custom-call(s32[4]{0:T(128)S(1)} %pad_add_fusion.place, f32[4,224,256]{2,1,0:T(8,128)S(1)} %pad_maximum_fusion.1.f01, f32[4,192,256]{2,1,0:T(8,128)S(1)} %pad_maximum_fusion.2.f2, ...), custom_call_target="tpu_custom_call" | custom-call | flops 1 | bytes 1 | tf_op jit(solution)/shard_map/pallas_call | solution.py:84
  120.3 1.2 copy-done.2
  121.5 0.8 copy-done.28
  123.6 1.7 %collective-permute-start.37 = (f32[64,256]{1,0:T(8,128)}, f32[64,256]{1,0:T(8,128)}, u32[]{:S(2)}, u32[]{:S(2)}) collective-permute-start(f32[64,256]{1,0:T(8,128)} %fusion.7), channel_id=1, source_target_pairs={{0,16},{4,20},{8,24},{12,28},{16,0},{20,4},{24,8},{28,12},{1,17},{... | collective-permute-start | bytes 196616 | tf_op jit(solution)/shard_map/ppermute | solution.py:259
  125.2 1.2 collective-permute-start.38
  126.4 1.5 copy-done.3
  127.9 3.0 %shard_map.32 = (bf16[1024,1024]{1,0:T(8,128)(2,1)S(1)}, bf16[1024,1024]{1,0:T(8,128)(2,1)S(1)}) custom-call(s32[4]{0:T(128)S(1)} %pad_add_fusion.place, f32[4,256,256]{2,1,0:T(8,128)S(1)} %get-tuple-element.84.t_ref, f32[7,256,256]{2,1,0:T(8,128)S(1)} %copy-done.3), custom_call_target="tpu_custom_call" | custom-call | flops 1 | bytes 1 | tf_op jit(solution)/shard_map/pallas_call | solution.py:84
  131.0 1.0 pad_maximum_fusion.4.f3
  132.0 2.5 %shard_map.33 = (bf16[256,1024]{1,0:T(8,128)(2,1)S(1)}, bf16[256,1024]{1,0:T(8,128)(2,1)S(1)}) custom-call(s32[4]{0:T(128)S(1)} %pad_add_fusion.place, bf16[256,768]{1,0:T(8,128)(2,1)S(1)} %get-tuple-element.78.p_high, bf16[256,768]{1,0:T(8,128)(2,1)S(1)} %copy-done.29, f32[4,64,256]{2,1,0:T(8,128)S(1)} %pad_maximum_fusion.4.f3, ...), custom_call_target="tpu_custom_call" | custom-call | flops 1 | bytes 1 | tf_op jit(solution)/shard_map/pallas_call | solution.py:84
  134.7 2.4 %shard_map.34 = f32[4,64,1024]{2,1,0:T(8,128)S(1)} custom-call(s32[4]{0:T(128)S(1)} %pad_add_fusion.place, f32[256,2048]{1,0:T(8,128)S(1)} %copy-done.1, bf16[256,1024]{1,0:T(8,128)(2,1)S(1)} %get-tuple-element.93.s_high, bf16[256,1024]{1,0:T(8,128)(2,1)S(1)} %get-tuple-element.94.s_low, bf16[512,1024]{1,0:T(8,128)(2,1)S(1)} %copy-done.9, ...), custom_call_target="tpu_custom_call" | custom-call | flops 1 | bytes 1 | tf_op jit(solution)/shard_map/pallas_call | solution.py:84
  137.9 1.7 %collective-permute-start.40 = (f32[64,1024]{1,0:T(8,128)S(1)}, f32[64,1024]{1,0:T(8,128)S(1)}, u32[]{:S(2)}, u32[]{:S(2)}) collective-permute-start(f32[64,1024]{1,0:T(8,128)S(1)} %get-tuple-element.115), channel_id=1, source_target_pairs={{0,16},{4,20},{8,24},{12,28},{16,0},{20,4},{24,8},{28,12},{1,17},{... | collective-permute-start | bytes 786440 | tf_op jit(solution)/shard_map/ppermute | solution.py:259
  139.6 1.2 collective-permute-start.41
  140.8 2.4 %shard_map.35 = f32[4,64,1024]{2,1,0:T(8,128)S(1)} custom-call(s32[4]{0:T(128)S(1)} %pad_add_fusion.place, f32[256,2048]{1,0:T(8,128)S(1)} %copy-done.1, bf16[256,1024]{1,0:T(8,128)(2,1)S(1)} %get-tuple-element.93.s_high, bf16[256,1024]{1,0:T(8,128)(2,1)S(1)} %get-tuple-element.94.s_low, bf16[512,1024]{1,0:T(8,128)(2,1)S(1)} %copy-done.5, ...), custom_call_target="tpu_custom_call" | custom-call | flops 1 | bytes 1 | tf_op jit(solution)/shard_map/pallas_call | solution.py:84
  143.2 0.7 collective-permute-start.42
  144.0 1.7 %collective-permute-start.43 = (f32[64,1024]{1,0:T(8,128)S(1)}, f32[64,1024]{1,0:T(8,128)S(1)}, u32[]{:S(2)}, u32[]{:S(2)}) collective-permute-start(f32[64,1024]{1,0:T(8,128)S(1)} %get-tuple-element.112), channel_id=1, source_target_pairs={{0,16},{4,20},{8,24},{12,28},{16,0},{20,4},{24,8},{28,12},{1,17},{... | collective-permute-start | bytes 786440 | tf_op jit(solution)/shard_map/ppermute | solution.py:259
  146.5 1.8 %collective-permute-start.44 = (f32[64,1024]{1,0:T(8,128)S(1)}, f32[64,1024]{1,0:T(8,128)S(1)}, u32[]{:S(2)}, u32[]{:S(2)}) collective-permute-start(f32[64,1024]{1,0:T(8,128)S(1)} %get-tuple-element.111), channel_id=1, source_target_pairs={{0,24},{4,28},{8,16},{12,20},{16,8},{20,12},{24,0},{28,4},{1,25},{... | collective-permute-start | bytes 786440 | tf_op jit(solution)/shard_map/ppermute | solution.py:259
  148.3 2.2 %collective-permute-done.40 = f32[64,1024]{1,0:T(8,128)S(1)} collective-permute-done((f32[64,1024]{1,0:T(8,128)S(1)}, f32[64,1024]{1,0:T(8,128)S(1)}, u32[]{:S(2)}, u32[]{:S(2)}) %collective-permute-start.40) | collective-permute-done | bytes 262176 | tf_op jit(solution)/shard_map/ppermute | solution.py:259
  150.5 2.0 %collective-permute-done.41 = f32[64,1024]{1,0:T(8,128)S(1)} collective-permute-done((f32[64,1024]{1,0:T(8,128)S(1)}, f32[64,1024]{1,0:T(8,128)S(1)}, u32[]{:S(2)}, u32[]{:S(2)}) %collective-permute-start.41) | collective-permute-done | bytes 262176 | tf_op jit(solution)/shard_map/ppermute | solution.py:259
  152.5 5.2 %collective-permute-done.42 = f32[64,1024]{1,0:T(8,128)S(1)} collective-permute-done((f32[64,1024]{1,0:T(8,128)S(1)}, f32[64,1024]{1,0:T(8,128)S(1)}, u32[]{:S(2)}, u32[]{:S(2)}) %collective-permute-start.42) | collective-permute-done | bytes 262176 | tf_op jit(solution)/shard_map/ppermute | solution.py:259
  157.7 3.4 %collective-permute-done.43 = f32[64,1024]{1,0:T(8,128)S(1)} collective-permute-done((f32[64,1024]{1,0:T(8,128)S(1)}, f32[64,1024]{1,0:T(8,128)S(1)}, u32[]{:S(2)}, u32[]{:S(2)}) %collective-permute-start.43) | collective-permute-done | bytes 262176 | tf_op jit(solution)/shard_map/ppermute | solution.py:259
  161.2 1.3 copy-done.30
  (128 shorter events, 10.0 us)
Async XLA Ops:
  0.0 6.3 %copy-start.31 = (f32[64,8192]{1,0:T(8,128)S(1)}, f32[64,8192]{1,0:T(8,128)}, u32[]{:S(2)}) copy-start(f32[64,8192]{1,0:T(8,128)} %param.2) | copy-start | bytes 6291460
  1.6 31.0 %collective-permute-start.3 = (f32[256,1024]{1,0:T(8,128)S(1)}, f32[256,1024]{1,0:T(8,128)}, u32[]{:S(2)}, u32[]{:S(2)}) collective-permute-start(f32[256,1024]{1,0:T(8,128)S(1)} %select_select_fusion.refs_1_), channel_id=1, source_target_pairs={{0,1},{1,0},{2,3},{3,2},{4,5},{5,4},{6,7},{7,6},{8,9},{9,8},{10,11... | collective-permute-start | bytes 3145736 | tf_op jit(solution)/shard_map/ppermute | solution.py:265
  4.7 27.9 %collective-permute-start.4 = (f32[256,1024]{1,0:T(8,128)S(1)}, f32[256,1024]{1,0:T(8,128)}, u32[]{:S(2)}, u32[]{:S(2)}) collective-permute-start(f32[256,1024]{1,0:T(8,128)S(1)} %select_select_fusion.refs_1_), channel_id=1, source_target_pairs={{1,2},{2,1},{5,6},{6,5},{9,10},{10,9},{13,14},{14,13},{17,18},{18,... | collective-permute-start | bytes 3145736 | tf_op jit(solution)/shard_map/ppermute | solution.py:265
  6.5 14.9 %collective-permute-start = (f32[64,2048]{1,0:T(8,128)S(1)}, f32[64,2048]{1,0:T(8,128)S(1)}, u32[]{:S(2)}, u32[]{:S(2)}) collective-permute-start(f32[64,2048]{1,0:T(8,128)S(1)} %get-tuple-element.110), channel_id=1, source_target_pairs={{0,8},{4,12},{8,0},{12,4},{16,24},{20,28},{24,16},{28,20},{1,9},{5... | collective-permute-start | bytes 1572872 | tf_op jit(solution)/shard_map/ppermute | solution.py:259
  8.1 24.3 %collective-permute-start.1 = (f32[64,2048]{1,0:T(8,128)S(1)}, f32[64,2048]{1,0:T(8,128)S(1)}, u32[]{:S(2)}, u32[]{:S(2)}) collective-permute-start(f32[64,2048]{1,0:T(8,128)S(1)} %get-tuple-element.109), channel_id=1, source_target_pairs={{0,16},{4,20},{8,24},{12,28},{16,0},{20,4},{24,8},{28,12},{1,17},{... | collective-permute-start | bytes 1572872 | tf_op jit(solution)/shard_map/ppermute | solution.py:259
  9.6 22.8 %collective-permute-start.2 = (f32[64,2048]{1,0:T(8,128)S(1)}, f32[64,2048]{1,0:T(8,128)S(1)}, u32[]{:S(2)}, u32[]{:S(2)}) collective-permute-start(f32[64,2048]{1,0:T(8,128)S(1)} %get-tuple-element.108), channel_id=1, source_target_pairs={{0,24},{4,28},{8,16},{12,20},{16,8},{20,12},{24,0},{28,4},{1,25},{... | collective-permute-start | bytes 1572872 | tf_op jit(solution)/shard_map/ppermute | solution.py:259
  32.6 9.6 %copy-start = (f32[256,2048]{1,0:T(8,128)}, f32[256,2048]{1,0:T(8,128)S(1)}, u32[]{:S(2)}) copy-start(f32[256,2048]{1,0:T(8,128)S(1)} %pad_maximum_fusion.refs_0_.e_ref) | copy-start | bytes 6291460
  32.6 3.6 %collective-permute-start.7 = (f32[256,1024]{1,0:T(8,128)S(1)}, f32[256,1024]{1,0:T(8,128)}, u32[]{:S(2)}, u32[]{:S(2)}) collective-permute-start(f32[256,1024]{1,0:T(8,128)S(1)} %select_select_fusion.refs_1_), channel_id=1, source_target_pairs={{0,4},{4,0},{8,12},{12,8},{16,20},{20,16},{24,28},{28,24},{1,5},{5... | collective-permute-start | bytes 3145736 | tf_op jit(solution)/shard_map/ppermute | solution.py:262
  32.7 4.5 %collective-permute-start.8 = (f32[256,1024]{1,0:T(8,128)}, f32[256,1024]{1,0:T(8,128)}, u32[]{:S(2)}, u32[]{:S(2)}) collective-permute-start(f32[256,1024]{1,0:T(8,128)} %collective-permute-done.3.refs_3_), channel_id=1, source_target_pairs={{0,4},{4,0},{8,12},{12,8},{16,20},{20,16},{24,28},{28,24},{1,5},{5... | collective-permute-start | bytes 3145736 | tf_op jit(solution)/shard_map/ppermute | solution.py:262
  33.2 30.0 %collective-permute-start.6 = (f32[256,1024]{1,0:T(8,128)}, f32[256,1024]{1,0:T(8,128)S(1)}, u32[]{:S(2)}, u32[]{:S(2)}) collective-permute-start(f32[256,1024]{1,0:T(8,128)} %collective-permute-done.3.refs_3_), channel_id=1, source_target_pairs={{1,2},{2,1},{5,6},{6,5},{9,10},{10,9},{13,14},{14,13},{17,18},{18,... | collective-permute-start | bytes 3145736 | tf_op jit(solution)/shard_map/ppermute | solution.py:265
  33.9 29.3 %collective-permute-start.5 = (f32[256,1024]{1,0:T(8,128)}, f32[256,1024]{1,0:T(8,128)S(1)}, u32[]{:S(2)}, u32[]{:S(2)}) collective-permute-start(f32[256,1024]{1,0:T(8,128)} %collective-permute-done.4.refs_9_.refs_3_), channel_id=1, source_target_pairs={{1,0},{2,3},{5,4},{6,7},{9,8},{10,11},{13,12},{14,15},{17,16},{18,... | collective-permute-start | bytes 3145736 | tf_op jit(solution)/shard_map/ppermute | solution.py:265
  44.2 24.2 %copy-start.4 = (bf16[512,1024]{1,0:T(8,128)(2,1)}, bf16[512,1024]{1,0:T(8,128)(2,1)S(1)}, u32[]{:S(2)}) copy-start(bf16[512,1024]{1,0:T(8,128)(2,1)S(1)} %get-tuple-element.101.refs_0_) | copy-start | bytes 3145732
  44.2 31.1 %copy-start.6 = (bf16[512,1024]{1,0:T(8,128)(2,1)}, bf16[512,1024]{1,0:T(8,128)(2,1)S(1)}, u32[]{:S(2)}) copy-start(bf16[512,1024]{1,0:T(8,128)(2,1)S(1)} %get-tuple-element.102.refs_1_) | copy-start | bytes 3145732
  44.3 12.6 %collective-permute-start.10 = (f32[224,256]{1,0:T(8,128)S(1)}, f32[224,256]{1,0:T(8,128)S(1)}, u32[]{:S(2)}, u32[]{:S(2)}) collective-permute-start(f32[224,256]{1,0:T(8,128)S(1)} %get-tuple-element.119), channel_id=1, source_target_pairs={{0,16},{4,20},{8,24},{12,28},{16,0},{20,4},{24,8},{28,12},{1,17},{... | collective-permute-start | bytes 688136 | tf_op jit(solution)/shard_map/ppermute | solution.py:259
  45.8 11.0 %collective-permute-start.11 = (f32[224,256]{1,0:T(8,128)S(1)}, f32[224,256]{1,0:T(8,128)S(1)}, u32[]{:S(2)}, u32[]{:S(2)}) collective-permute-start(f32[224,256]{1,0:T(8,128)S(1)} %get-tuple-element.118), channel_id=1, source_target_pairs={{0,24},{4,28},{8,16},{12,20},{16,8},{20,12},{24,0},{28,4},{1,25},{... | collective-permute-start | bytes 688136 | tf_op jit(solution)/shard_map/ppermute | solution.py:259
  47.0 11.1 %collective-permute-start.9 = (f32[224,256]{1,0:T(8,128)S(1)}, f32[224,256]{1,0:T(8,128)S(1)}, u32[]{:S(2)}, u32[]{:S(2)}) collective-permute-start(f32[224,256]{1,0:T(8,128)S(1)} %get-tuple-element.117), channel_id=1, source_target_pairs={{0,8},{4,12},{8,0},{12,4},{16,24},{20,28},{24,16},{28,20},{1,9},{5... | collective-permute-start | bytes 688136 | tf_op jit(solution)/shard_map/ppermute | solution.py:259
  58.2 6.6 %collective-permute-start.12 = (f32[224,256]{1,0:T(8,128)S(1)}, f32[224,256]{1,0:T(8,128)S(1)}, u32[]{:S(2)}, u32[]{:S(2)}) collective-permute-start(f32[224,256]{1,0:T(8,128)S(1)} %fusion.3), channel_id=1, source_target_pairs={{0,8},{4,12},{8,0},{12,4},{16,24},{20,28},{24,16},{28,20},{1,9},{5... | collective-permute-start | bytes 688136 | tf_op jit(solution)/shard_map/ppermute | solution.py:259
  59.5 8.9 %collective-permute-start.19 = (f32[256,1024]{1,0:T(8,128)}, f32[256,1024]{1,0:T(8,128)S(1)}, u32[]{:S(2)}, u32[]{:S(2)}) collective-permute-start(f32[256,1024]{1,0:T(8,128)} %collective-permute-done.4.refs_9_.refs_3_), channel_id=1, source_target_pairs={{0,4},{4,0},{8,12},{12,8},{16,20},{20,16},{24,28},{28,24},{1,5},{5... | collective-permute-start | bytes 3145736 | tf_op jit(solution)/shard_map/ppermute | solution.py:262
  64.8 4.8 %collective-permute-start.17 = (f32[256,1024]{1,0:T(8,128)S(1)}, f32[256,1024]{1,0:T(8,128)S(1)}, u32[]{:S(2)}, u32[]{:S(2)}) collective-permute-start(f32[256,1024]{1,0:T(8,128)S(1)} %collective-permute-done.5.refs_5_), channel_id=1, source_target_pairs={{0,4},{4,0},{8,12},{12,8},{16,20},{20,16},{24,28},{28,24},{1,5},{5... | collective-permute-start | bytes 3145736 | tf_op jit(solution)/shard_map/ppermute | solution.py:262
  64.8 4.8 %collective-permute-start.18 = (f32[256,1024]{1,0:T(8,128)S(1)}, f32[256,1024]{1,0:T(8,128)S(1)}, u32[]{:S(2)}, u32[]{:S(2)}) collective-permute-start(f32[256,1024]{1,0:T(8,128)S(1)} %collective-permute-done.6.refs_7_), channel_id=1, source_target_pairs={{0,4},{4,0},{8,12},{12,8},{16,20},{20,16},{24,28},{28,24},{1,5},{5... | collective-permute-start | bytes 3145736 | tf_op jit(solution)/shard_map/ppermute | solution.py:262
  65.3 33.5 %collective-permute-start.13 = (f32[256,1024]{1,0:T(8,128)S(1)}, f32[256,1024]{1,0:T(8,128)S(1)}, u32[]{:S(2)}, u32[]{:S(2)}) collective-permute-start(f32[256,1024]{1,0:T(8,128)S(1)} %collective-permute-done.6.refs_7_), channel_id=1, source_target_pairs={{1,0},{2,3},{5,4},{6,7},{9,8},{10,11},{13,12},{14,15},{17,16},{18,... | collective-permute-start | bytes 3145736 | tf_op jit(solution)/shard_map/ppermute | solution.py:265
  66.7 13.1 %collective-permute-start.14 = (f32[224,256]{1,0:T(8,128)S(1)}, f32[224,256]{1,0:T(8,128)S(1)}, u32[]{:S(2)}, u32[]{:S(2)}) collective-permute-start(f32[224,256]{1,0:T(8,128)S(1)} %fusion.3), channel_id=1, source_target_pairs={{0,16},{4,20},{8,24},{12,28},{16,0},{20,4},{24,8},{28,12},{1,17},{... | collective-permute-start | bytes 688136 | tf_op jit(solution)/shard_map/ppermute | solution.py:259
  68.4 12.7 %collective-permute-start.15 = (f32[224,256]{1,0:T(8,128)S(1)}, f32[224,256]{1,0:T(8,128)S(1)}, u32[]{:S(2)}, u32[]{:S(2)}) collective-permute-start(f32[224,256]{1,0:T(8,128)S(1)} %fusion.3), channel_id=1, source_target_pairs={{0,24},{4,28},{8,16},{12,20},{16,8},{20,12},{24,0},{28,4},{1,25},{... | collective-permute-start | bytes 688136 | tf_op jit(solution)/shard_map/ppermute | solution.py:259
  75.3 12.4 %copy-start.12 = (bf16[256,1024]{1,0:T(8,128)(2,1)}, bf16[256,1024]{1,0:T(8,128)(2,1)S(1)}, u32[]{:S(2)}) copy-start(bf16[256,1024]{1,0:T(8,128)(2,1)S(1)} %get-tuple-element.103.refs_2_) | copy-start | bytes 1572868
  75.3 12.4 %copy-start.14 = (bf16[256,1024]{1,0:T(8,128)(2,1)}, bf16[256,1024]{1,0:T(8,128)(2,1)S(1)}, u32[]{:S(2)}) copy-start(bf16[256,1024]{1,0:T(8,128)(2,1)S(1)} %get-tuple-element.104.refs_3_) | copy-start | bytes 1572868
  75.3 12.4 %copy-start.16 = (bf16[256,1024]{1,0:T(8,128)(2,1)}, bf16[256,1024]{1,0:T(8,128)(2,1)S(1)}, u32[]{:S(2)}) copy-start(bf16[256,1024]{1,0:T(8,128)(2,1)S(1)} %get-tuple-element.97.refs_2_) | copy-start | bytes 1572868
  75.3 12.4 %copy-start.18 = (bf16[256,1024]{1,0:T(8,128)(2,1)}, bf16[256,1024]{1,0:T(8,128)(2,1)S(1)}, u32[]{:S(2)}) copy-start(bf16[256,1024]{1,0:T(8,128)(2,1)S(1)} %get-tuple-element.98.refs_3_) | copy-start | bytes 1572868
  75.4 6.4 %collective-permute-start.20 = (f32[192,256]{1,0:T(8,128)S(1)}, f32[192,256]{1,0:T(8,128)S(1)}, u32[]{:S(2)}, u32[]{:S(2)}) collective-permute-start(f32[192,256]{1,0:T(8,128)S(1)} %get-tuple-element.120), channel_id=1, source_target_pairs={{0,8},{4,12},{8,0},{12,4},{16,24},{20,28},{24,16},{28,20},{1,9},{5... | collective-permute-start | bytes 589832 | tf_op jit(solution)/shard_map/ppermute | solution.py:259
  76.3 11.4 %collective-permute-start.21 = (f32[192,256]{1,0:T(8,128)S(1)}, f32[192,256]{1,0:T(8,128)S(1)}, u32[]{:S(2)}, u32[]{:S(2)}) collective-permute-start(f32[192,256]{1,0:T(8,128)S(1)} %get-tuple-element.122), channel_id=1, source_target_pairs={{0,16},{4,20},{8,24},{12,28},{16,0},{20,4},{24,8},{28,12},{1,17},{... | collective-permute-start | bytes 589832 | tf_op jit(solution)/shard_map/ppermute | solution.py:259
  79.8 7.8 %collective-permute-start.22 = (f32[192,256]{1,0:T(8,128)S(1)}, f32[192,256]{1,0:T(8,128)S(1)}, u32[]{:S(2)}, u32[]{:S(2)}) collective-permute-start(f32[192,256]{1,0:T(8,128)S(1)} %get-tuple-element.121), channel_id=1, source_target_pairs={{0,24},{4,28},{8,16},{12,20},{16,8},{20,12},{24,0},{28,4},{1,25},{... | collective-permute-start | bytes 589832 | tf_op jit(solution)/shard_map/ppermute | solution.py:259
  81.1 23.9 %copy-start.1 = (f32[256,2048]{1,0:T(8,128)S(1)}, f32[256,2048]{1,0:T(8,128)}, u32[]{:S(2)}) copy-start(f32[256,2048]{1,0:T(8,128)} %copy-done) | copy-start | bytes 6291460
  81.2 17.5 %collective-permute-start.16 = (f32[4,96,256]{2,1,0:T(8,128)S(1)}, f32[4,96,256]{2,1,0:T(8,128)S(1)}, u32[]{:S(2)}, u32[]{:S(2)}) collective-permute-start(f32[4,96,256]{2,1,0:T(8,128)S(1)} %slice.92), channel_id=1, source_target_pairs={{0,4},{4,0},{8,12},{12,8},{16,20},{20,16},{24,28},{28,24},{1,5},{5... | collective-permute-start | bytes 1179656 | tf_op jit(solution)/shard_map/ppermute | solution.py:262
  87.8 7.5 %collective-permute-start.23 = (f32[192,256]{1,0:T(8,128)S(1)}, f32[192,256]{1,0:T(8,128)S(1)}, u32[]{:S(2)}, u32[]{:S(2)}) collective-permute-start(f32[192,256]{1,0:T(8,128)S(1)} %fusion.5), channel_id=1, source_target_pairs={{0,8},{4,12},{8,0},{12,4},{16,24},{20,28},{24,16},{28,20},{1,9},{5... | collective-permute-start | bytes 589832 | tf_op jit(solution)/shard_map/ppermute | solution.py:259
  89.1 9.6 %collective-permute-start.24 = (f32[192,256]{1,0:T(8,128)S(1)}, f32[192,256]{1,0:T(8,128)S(1)}, u32[]{:S(2)}, u32[]{:S(2)}) collective-permute-start(f32[192,256]{1,0:T(8,128)S(1)} %fusion.5), channel_id=1, source_target_pairs={{0,16},{4,20},{8,24},{12,28},{16,0},{20,4},{24,8},{28,12},{1,17},{... | collective-permute-start | bytes 589832 | tf_op jit(solution)/shard_map/ppermute | solution.py:259
  89.9 8.8 %collective-permute-start.25 = (f32[192,256]{1,0:T(8,128)S(1)}, f32[192,256]{1,0:T(8,128)S(1)}, u32[]{:S(2)}, u32[]{:S(2)}) collective-permute-start(f32[192,256]{1,0:T(8,128)S(1)} %fusion.5), channel_id=1, source_target_pairs={{0,24},{4,28},{8,16},{12,20},{16,8},{20,12},{24,0},{28,4},{1,25},{... | collective-permute-start | bytes 589832 | tf_op jit(solution)/shard_map/ppermute | solution.py:259
  95.3 6.3 %collective-permute-start.26 = (f32[128,256]{1,0:T(8,128)S(1)}, f32[128,256]{1,0:T(8,128)S(1)}, u32[]{:S(2)}, u32[]{:S(2)}) collective-permute-start(f32[128,256]{1,0:T(8,128)S(1)} %slice.93), channel_id=1, source_target_pairs={{0,1},{1,0},{2,3},{3,2},{4,5},{5,4},{6,7},{7,6},{8,9},{9,8},{10,11... | collective-permute-start | bytes 393224 | tf_op jit(solution)/shard_map/ppermute | solution.py:265
  101.5 3.5 %collective-permute-start.27 = (f32[256,1024]{1,0:T(8,128)S(1)}, f32[256,1024]{1,0:T(8,128)S(1)}, u32[]{:S(2)}, u32[]{:S(2)}) collective-permute-start(f32[256,1024]{1,0:T(8,128)S(1)} %collective-permute-done.13.refs_1_), channel_id=1, source_target_pairs={{0,4},{4,0},{8,12},{12,8},{16,20},{20,16},{24,28},{28,24},{1,5},{5... | collective-permute-start | bytes 3145736 | tf_op jit(solution)/shard_map/ppermute | solution.py:262
  101.5 6.3 %collective-permute-start.28 = (f32[128,256]{1,0:T(8,128)S(1)}, f32[128,256]{1,0:T(8,128)S(1)}, u32[]{:S(2)}, u32[]{:S(2)}) collective-permute-start(f32[128,256]{1,0:T(8,128)S(1)} %collective-permute-done.26), channel_id=1, source_target_pairs={{0,8},{4,12},{8,0},{12,4},{16,24},{20,28},{24,16},{28,20},{1,9},{5... | collective-permute-start | bytes 393224 | tf_op jit(solution)/shard_map/ppermute | solution.py:259
  102.1 7.8 %collective-permute-start.29 = (f32[128,256]{1,0:T(8,128)S(1)}, f32[128,256]{1,0:T(8,128)S(1)}, u32[]{:S(2)}, u32[]{:S(2)}) collective-permute-start(f32[128,256]{1,0:T(8,128)S(1)} %collective-permute-done.26), channel_id=1, source_target_pairs={{0,16},{4,20},{8,24},{12,28},{16,0},{20,4},{24,8},{28,12},{1,17},{... | collective-permute-start | bytes 393224 | tf_op jit(solution)/shard_map/ppermute | solution.py:259
  103.9 7.5 %collective-permute-start.30 = (f32[128,256]{1,0:T(8,128)S(1)}, f32[128,256]{1,0:T(8,128)S(1)}, u32[]{:S(2)}, u32[]{:S(2)}) collective-permute-start(f32[128,256]{1,0:T(8,128)S(1)} %collective-permute-done.26), channel_id=1, source_target_pairs={{0,24},{4,28},{8,16},{12,20},{16,8},{20,12},{24,0},{28,4},{1,25},{... | collective-permute-start | bytes 393224 | tf_op jit(solution)/shard_map/ppermute | solution.py:259
  107.6 12.6 %copy-start.20 = (bf16[256,1024]{1,0:T(8,128)(2,1)}, bf16[256,1024]{1,0:T(8,128)(2,1)S(1)}, u32[]{:S(2)}) copy-start(bf16[256,1024]{1,0:T(8,128)(2,1)S(1)} %get-tuple-element.105.refs_4_) | copy-start | bytes 1572868
  107.6 12.6 %copy-start.22 = (bf16[256,1024]{1,0:T(8,128)(2,1)}, bf16[256,1024]{1,0:T(8,128)(2,1)S(1)}, u32[]{:S(2)}) copy-start(bf16[256,1024]{1,0:T(8,128)(2,1)S(1)} %get-tuple-element.106.refs_5_) | copy-start | bytes 1572868
  107.6 12.6 %copy-start.24 = (bf16[256,1024]{1,0:T(8,128)(2,1)}, bf16[256,1024]{1,0:T(8,128)(2,1)S(1)}, u32[]{:S(2)}) copy-start(bf16[256,1024]{1,0:T(8,128)(2,1)S(1)} %get-tuple-element.99.refs_4_) | copy-start | bytes 1572868
  107.7 12.6 %copy-start.26 = (bf16[256,1024]{1,0:T(8,128)(2,1)}, bf16[256,1024]{1,0:T(8,128)(2,1)S(1)}, u32[]{:S(2)}) copy-start(bf16[256,1024]{1,0:T(8,128)(2,1)S(1)} %get-tuple-element.100.refs_5_) | copy-start | bytes 1572868
  111.5 4.3 %collective-permute-start.32 = (f32[4,128,256]{2,1,0:T(8,128)S(1)}, f32[4,128,256]{2,1,0:T(8,128)S(1)}, u32[]{:S(2)}, u32[]{:S(2)}) collective-permute-start(f32[4,128,256]{2,1,0:T(8,128)S(1)} %pad_maximum_fusion.3.fb), channel_id=1, source_target_pairs={{0,4},{4,0},{8,12},{12,8},{16,20},{20,16},{24,28},{28,24},{1,5},{5... | collective-permute-start | bytes 1572872 | tf_op jit(solution)/shard_map/ppermute | solution.py:262
  111.6 4.1 %collective-permute-start.31 = (f32[4,128,256]{2,1,0:T(8,128)S(1)}, f32[4,128,256]{2,1,0:T(8,128)S(1)}, u32[]{:S(2)}, u32[]{:S(2)}) collective-permute-start(f32[4,128,256]{2,1,0:T(8,128)S(1)} %slice.79), channel_id=1, source_target_pairs={{0,4},{4,0},{8,12},{12,8},{16,20},{20,16},{24,28},{28,24},{1,5},{5... | collective-permute-start | bytes 1572872 | tf_op jit(solution)/shard_map/ppermute | solution.py:262
  112.2 10.1 %collective-permute-start.33 = (f32[64,256]{1,0:T(8,128)S(1)}, f32[64,256]{1,0:T(8,128)S(1)}, u32[]{:S(2)}, u32[]{:S(2)}) collective-permute-start(f32[64,256]{1,0:T(8,128)S(1)} %get-tuple-element.125), channel_id=1, source_target_pairs={{0,8},{4,12},{8,0},{12,4},{16,24},{20,28},{24,16},{28,20},{1,9},{5... | collective-permute-start | bytes 196616 | tf_op jit(solution)/shard_map/ppermute | solution.py:259
  112.9 9.4 %collective-permute-start.34 = (f32[64,256]{1,0:T(8,128)S(1)}, f32[64,256]{1,0:T(8,128)S(1)}, u32[]{:S(2)}, u32[]{:S(2)}) collective-permute-start(f32[64,256]{1,0:T(8,128)S(1)} %get-tuple-element.124), channel_id=1, source_target_pairs={{0,16},{4,20},{8,24},{12,28},{16,0},{20,4},{24,8},{28,12},{1,17},{... | collective-permute-start | bytes 196616 | tf_op jit(solution)/shard_map/ppermute | solution.py:259
  114.5 7.7 %collective-permute-start.35 = (f32[64,256]{1,0:T(8,128)S(1)}, f32[64,256]{1,0:T(8,128)S(1)}, u32[]{:S(2)}, u32[]{:S(2)}) collective-permute-start(f32[64,256]{1,0:T(8,128)S(1)} %get-tuple-element.123), channel_id=1, source_target_pairs={{0,24},{4,28},{8,16},{12,20},{16,8},{20,12},{24,0},{28,4},{1,25},{... | collective-permute-start | bytes 196616 | tf_op jit(solution)/shard_map/ppermute | solution.py:259
  122.9 8.0 %collective-permute-start.36 = (f32[64,256]{1,0:T(8,128)}, f32[64,256]{1,0:T(8,128)}, u32[]{:S(2)}, u32[]{:S(2)}) collective-permute-start(f32[64,256]{1,0:T(8,128)} %fusion.7), channel_id=1, source_target_pairs={{0,8},{4,12},{8,0},{12,4},{16,24},{20,28},{24,16},{28,20},{1,9},{5... | collective-permute-start | bytes 196616 | tf_op jit(solution)/shard_map/ppermute | solution.py:259
  123.6 7.4 %collective-permute-start.37 = (f32[64,256]{1,0:T(8,128)}, f32[64,256]{1,0:T(8,128)}, u32[]{:S(2)}, u32[]{:S(2)}) collective-permute-start(f32[64,256]{1,0:T(8,128)} %fusion.7), channel_id=1, source_target_pairs={{0,16},{4,20},{8,24},{12,28},{16,0},{20,4},{24,8},{28,12},{1,17},{... | collective-permute-start | bytes 196616 | tf_op jit(solution)/shard_map/ppermute | solution.py:259
  125.2 5.7 %collective-permute-start.38 = (f32[64,256]{1,0:T(8,128)}, f32[64,256]{1,0:T(8,128)}, u32[]{:S(2)}, u32[]{:S(2)}) collective-permute-start(f32[64,256]{1,0:T(8,128)} %fusion.7), channel_id=1, source_target_pairs={{0,24},{4,28},{8,16},{12,20},{16,8},{20,12},{24,0},{28,4},{1,25},{... | collective-permute-start | bytes 196616 | tf_op jit(solution)/shard_map/ppermute | solution.py:259
  127.9 4.0 %copy-start.29 = (bf16[256,768]{1,0:T(8,128)(2,1)S(1)}, bf16[256,768]{1,0:T(8,128)(2,1)}, u32[]{:S(2)}) copy-start(bf16[256,768]{1,0:T(8,128)(2,1)} %copy-done.28) | copy-start | bytes 1179652
  134.6 6.1 %copy-start.7 = (bf16[512,1024]{1,0:T(8,128)(2,1)S(1)}, bf16[512,1024]{1,0:T(8,128)(2,1)}, u32[]{:S(2)}) copy-start(bf16[512,1024]{1,0:T(8,128)(2,1)} %copy-done.6) | copy-start | bytes 3145732
  134.6 6.1 %copy-start.13 = (bf16[256,1024]{1,0:T(8,128)(2,1)S(1)}, bf16[256,1024]{1,0:T(8,128)(2,1)}, u32[]{:S(2)}) copy-start(bf16[256,1024]{1,0:T(8,128)(2,1)} %copy-done.12) | copy-start | bytes 1572868
  134.7 6.1 %copy-start.15 = (bf16[256,1024]{1,0:T(8,128)(2,1)S(1)}, bf16[256,1024]{1,0:T(8,128)(2,1)}, u32[]{:S(2)}) copy-start(bf16[256,1024]{1,0:T(8,128)(2,1)} %copy-done.14) | copy-start | bytes 1572868
  134.7 6.1 %copy-start.21 = (bf16[256,1024]{1,0:T(8,128)(2,1)S(1)}, bf16[256,1024]{1,0:T(8,128)(2,1)}, u32[]{:S(2)}) copy-start(bf16[256,1024]{1,0:T(8,128)(2,1)} %copy-done.20) | copy-start | bytes 1572868
  134.7 6.1 %copy-start.23 = (bf16[256,1024]{1,0:T(8,128)(2,1)S(1)}, bf16[256,1024]{1,0:T(8,128)(2,1)}, u32[]{:S(2)}) copy-start(bf16[256,1024]{1,0:T(8,128)(2,1)} %copy-done.22) | copy-start | bytes 1572868
  137.2 9.3 %collective-permute-start.39 = (f32[64,1024]{1,0:T(8,128)S(1)}, f32[64,1024]{1,0:T(8,128)S(1)}, u32[]{:S(2)}, u32[]{:S(2)}) collective-permute-start(f32[64,1024]{1,0:T(8,128)S(1)} %get-tuple-element.116), channel_id=1, source_target_pairs={{0,8},{4,12},{8,0},{12,4},{16,24},{20,28},{24,16},{28,20},{1,9},{5... | collective-permute-start | bytes 786440 | tf_op jit(solution)/shard_map/ppermute | solution.py:259
  137.9 12.6 %collective-permute-start.40 = (f32[64,1024]{1,0:T(8,128)S(1)}, f32[64,1024]{1,0:T(8,128)S(1)}, u32[]{:S(2)}, u32[]{:S(2)}) collective-permute-start(f32[64,1024]{1,0:T(8,128)S(1)} %get-tuple-element.115), channel_id=1, source_target_pairs={{0,16},{4,20},{8,24},{12,28},{16,0},{20,4},{24,8},{28,12},{1,17},{... | collective-permute-start | bytes 786440 | tf_op jit(solution)/shard_map/ppermute | solution.py:259
  139.6 12.9 %collective-permute-start.41 = (f32[64,1024]{1,0:T(8,128)S(1)}, f32[64,1024]{1,0:T(8,128)S(1)}, u32[]{:S(2)}, u32[]{:S(2)}) collective-permute-start(f32[64,1024]{1,0:T(8,128)S(1)} %get-tuple-element.114), channel_id=1, source_target_pairs={{0,24},{4,28},{8,16},{12,20},{16,8},{20,12},{24,0},{28,4},{1,25},{... | collective-permute-start | bytes 786440 | tf_op jit(solution)/shard_map/ppermute | solution.py:259
  143.2 14.5 %collective-permute-start.42 = (f32[64,1024]{1,0:T(8,128)S(1)}, f32[64,1024]{1,0:T(8,128)S(1)}, u32[]{:S(2)}, u32[]{:S(2)}) collective-permute-start(f32[64,1024]{1,0:T(8,128)S(1)} %get-tuple-element.113), channel_id=1, source_target_pairs={{0,8},{4,12},{8,0},{12,4},{16,24},{20,28},{24,16},{28,20},{1,9},{5... | collective-permute-start | bytes 786440 | tf_op jit(solution)/shard_map/ppermute | solution.py:259
  144.0 17.2 %collective-permute-start.43 = (f32[64,1024]{1,0:T(8,128)S(1)}, f32[64,1024]{1,0:T(8,128)S(1)}, u32[]{:S(2)}, u32[]{:S(2)}) collective-permute-start(f32[64,1024]{1,0:T(8,128)S(1)} %get-tuple-element.112), channel_id=1, source_target_pairs={{0,16},{4,20},{8,24},{12,28},{16,0},{20,4},{24,8},{28,12},{1,17},{... | collective-permute-start | bytes 786440 | tf_op jit(solution)/shard_map/ppermute | solution.py:259
  146.5 14.7 %collective-permute-start.44 = (f32[64,1024]{1,0:T(8,128)S(1)}, f32[64,1024]{1,0:T(8,128)S(1)}, u32[]{:S(2)}, u32[]{:S(2)}) collective-permute-start(f32[64,1024]{1,0:T(8,128)S(1)} %get-tuple-element.111), channel_id=1, source_target_pairs={{0,24},{4,28},{8,16},{12,20},{16,8},{20,12},{24,0},{28,4},{1,25},{... | collective-permute-start | bytes 786440 | tf_op jit(solution)/shard_map/ppermute | solution.py:259
  (13 other events, 26.2 us)

commit v4 on v3

--- a/solution.py
+++ b/solution.py
@@ -220,11 +220,12 @@
             low_ref[rows, cols] = low
 
 
-def apply_kernel(chips, mine, place, p_high, p_low, f3, m_high, m_low, high_ref, low_ref):
+def apply_kernel(place, p_high, p_low, m_high, m_low, *refs):
     early = (PANELS - 1) * B
     solved = dot3((p_high[...], p_low[...]), (m_high[:early], m_low[:early]), NN)
-    solved = solved + dot3(split(f3[...].reshape(chips * mine, B)), (m_high[early:], m_low[early:]), NN)
-    high_ref[...], low_ref[...] = split(solved)
+    last = jnp.concatenate([ref[...] for ref in refs[:-2]])
+    solved = solved + dot3(split(last), (m_high[early:], m_low[early:]), NN)
+    refs[-2][...], refs[-1][...] = split(solved)
 
 
 def update_kernel(chips, half, place, e_ref, s_high, s_low, *refs):
@@ -277,7 +278,7 @@
         rows = sum(mine + used * part for _, used in plan)
         kernel = functools.partial(product_kernel, chips, plan, choice, lefts)
         kept = b16(len(plan) * B, width)
-        return call(kernel, (f32(chips, rows, B), kept, kept, kept, kept), place, grid, *operands, limit=40)
+        return call(kernel, (f32(chips, rows, B), kept, kept, kept, kept), place, grid, *operands, limit=24)
 
     vectors = masked_vectors(reflectors, c, r * width)
     vectors, eigvecs = lax.optimization_barrier((vectors, eigvecs))
@@ -319,19 +320,18 @@
         place,
         *(full_01, full_2, full_b, sib_01, sib_2, sib_b),
         scratch=[pltpu.VMEM((PANELS, B, B), jnp.float32)],
-        limit=24,
+        limit=16,
     )
     from_3 = [across(packed_3[x], x) for x in range(1, chips)]
     from_3, inverses = lax.optimization_barrier((from_3, inverses))
     held_3 = sum(from_3, packed_3[0])
     whole = b16(PANELS * B, PANELS * B)
-    inverse = call(combine_kernel, (whole, whole), place, inverses, grams, limit=32)
+    inverse = call(combine_kernel, (whole, whole), place, inverses, grams, limit=16)
     from_3 = [across(held_3, x) for x in range(1, chips)]
     from_3, inverse = lax.optimization_barrier((from_3, inverse))
-    full_3 = jnp.stack([held_3] + from_3)
     solved = b16(chips * mine, PANELS * B)
     solved = call(
-        functools.partial(apply_kernel, chips, mine), (solved, solved), place, *p_early, full_3, *inverse, limit=24
+        apply_kernel, (solved, solved), place, *p_early, *inverse, held_3, *from_3, limit=16
     )
     result = jnp.zeros_like(eigvecs)
     for half in range(2):
@@ -341,7 +341,7 @@
             place,
             *(grid, *solved),
             *(kept_01[2 * half : 2 * half + 2] + kept_2[2 * half : 2 * half + 2] + kept_3[2 * half : 2 * half + 2]),
-            limit=32,
+            limit=20,
         )
         for x in range(chips):
             piece = across(done[x], x) if x else done[x]

time: 163 us -> 161 us (0.988)
    unnamed x64 -> x60, local copies, waits for them, and re-layouts: 6.87 us -> 6.83 us
  transfers between devices with their start and end apart: 45 -> 45, of which waited for: 22 -> 20; matrix products, arithmetic and copies ran while one was open for 1% -> 1% of each run, Pallas kernels for 14% -> 14%
where the time goes in v4:
time: 161 us
  waiting for transfers between devices  71.4 us (44%)
  starting transfers between devices  50 us (31%)
  Pallas kernels  28.1 us (17%)
  local copies, waits for them, and re-layouts  8.29 us (5%)
  other arithmetic  2.7 us (2%)
    ppermute x30, waiting for transfers between devices, across(): lax.ppermute(value, 'row', [(i, i ^ 2 * x) for i in range(2 * chips)])  62.9 us
    ppermute x30, starting transfers between devices, across(): lax.ppermute(value, 'row', [(i, i ^ 2 * x) for i in range(2 * chips)])  36.7 us
    pallas_call x8, Pallas kernels, call(): pl.pallas_call(kernel, out_shape=out_shape, in_specs=[pl.BlockSpec(memory...  28.1 us
    ppermute x6, starting transfers between devices, zmove(): return lax.ppermute(value, 'col', pairs)  11.5 us
    unnamed x60, local copies, waits for them, and re-layouts  6.83 us
    ppermute x6, waiting for transfers between devices, zmove(): return lax.ppermute(value, 'col', pairs)  6.63 us
  transfers between devices with their start and end apart: 45, of which 20 were waited for; matrix products, arithmetic and copies ran while one was open for 1% of the time, Pallas kernels for 14%

profile of v4, /device:TPU:0, one launch (start us, length us, event | category | flops | bytes accessed | tf_op | source)
XLA Modules:
  0.0 161.1 jit_solution(14770096140169302668)
XLA Ops:
  0.0 1.6 select_select_fusion.refs_1_
  1.6 3.1 %collective-permute-start.3 = (f32[256,1024]{1,0:T(8,128)S(1)}, f32[256,1024]{1,0:T(8,128)}, u32[]{:S(2)}, u32[]{:S(2)}) collective-permute-start(f32[256,1024]{1,0:T(8,128)S(1)} %select_select_fusion.refs_1_), channel_id=1, source_target_pairs={{0,1},{1,0},{2,3},{3,2},{4,5},{5,4},{6,7},{7,6},{8,9},{9,8},{10,11... | collective-permute-start | bytes 3145736 | tf_op jit(solution)/shard_map/ppermute | solution.py:266
  4.7 1.7 %collective-permute-start.4 = (f32[256,1024]{1,0:T(8,128)S(1)}, f32[256,1024]{1,0:T(8,128)}, u32[]{:S(2)}, u32[]{:S(2)}) collective-permute-start(f32[256,1024]{1,0:T(8,128)S(1)} %select_select_fusion.refs_1_), channel_id=1, source_target_pairs={{1,2},{2,1},{5,6},{6,5},{9,10},{10,9},{13,14},{14,13},{17,18},{18,... | collective-permute-start | bytes 3145736 | tf_op jit(solution)/shard_map/ppermute | solution.py:266
  6.5 1.6 collective-permute-start
  8.0 1.5 collective-permute-start.1
  10.0 11.4 %collective-permute-done = f32[64,2048]{1,0:T(8,128)S(1)} collective-permute-done((f32[64,2048]{1,0:T(8,128)S(1)}, f32[64,2048]{1,0:T(8,128)S(1)}, u32[]{:S(2)}, u32[]{:S(2)}) %collective-permute-start) | collective-permute-done | bytes 524320 | tf_op jit(solution)/shard_map/ppermute | solution.py:260
  21.4 11.0 %collective-permute-done.1 = f32[64,2048]{1,0:T(8,128)S(1)} collective-permute-done((f32[64,2048]{1,0:T(8,128)S(1)}, f32[64,2048]{1,0:T(8,128)S(1)}, u32[]{:S(2)}, u32[]{:S(2)}) %collective-permute-start.1) | collective-permute-done | bytes 524320 | tf_op jit(solution)/shard_map/ppermute | solution.py:260
  33.9 1.3 collective-permute-start.5
  35.2 0.9 collective-permute-done.7.refs_2_
  36.1 1.0 collective-permute-done.8.refs_4_
  37.1 5.0 %shard_map.28 = (f32[4,224,256]{2,1,0:T(8,128)S(1)}, bf16[512,1024]{1,0:T(8,128)(2,1)S(1)}, bf16[512,1024]{1,0:T(8,128)(2,1)S(1)}, bf16[512,1024]{1,0:T(8,128)(2,1)S(1)}, bf16[512,1024]{1,0:T(8,128)(2,1)S(1)}) custom-call(s32[4]{0:T(128)S(1)} %pad_add_fusion.place, f32[256,2048]{1,0:T(8,128)S(1)} %pad_maximum_fusion.refs_0_.e_ref, ...), custom_call_target="tpu_custom_call" | custom-call | flops 1 | bytes 1 | tf_op jit(solution)/shard_map/pallas_call | solution.py:84
  42.1 1.0 copy-done.6
  43.1 1.0 copy-done.8
  44.1 1.6 collective-permute-start.10
  45.7 1.2 collective-permute-start.11
  47.7 9.1 %collective-permute-done.10 = f32[224,256]{1,0:T(8,128)S(1)} collective-permute-done((f32[224,256]{1,0:T(8,128)S(1)}, f32[224,256]{1,0:T(8,128)S(1)}, u32[]{:S(2)}, u32[]{:S(2)}) %collective-permute-start.10) | collective-permute-done | bytes 229408 | tf_op jit(solution)/shard_map/ppermute | solution.py:260
  56.8 1.2 collective-permute-done.9
  58.1 1.3 collective-permute-start.12
  59.4 3.8 %collective-permute-done.5.refs_5_ = f32[256,1024]{1,0:T(8,128)S(1)} collective-permute-done((f32[256,1024]{1,0:T(8,128)}, f32[256,1024]{1,0:T(8,128)S(1)}, u32[]{:S(2)}, u32[]{:S(2)}) %collective-permute-start.5) | collective-permute-done | bytes 1048608 | tf_op jit(solution)/shard_map/ppermute | solution.py:266
  63.1 1.6 collective-permute-done.12
  65.2 1.5 collective-permute-start.13
  66.7 1.6 collective-permute-start.14
  68.2 1.2 collective-permute-start.15
  69.4 5.1 %shard_map.29 = (f32[4,192,256]{2,1,0:T(8,128)S(1)}, bf16[256,1024]{1,0:T(8,128)(2,1)S(1)}, bf16[256,1024]{1,0:T(8,128)(2,1)S(1)}, bf16[256,1024]{1,0:T(8,128)(2,1)S(1)}, bf16[256,1024]{1,0:T(8,128)(2,1)S(1)}) custom-call(s32[4]{0:T(128)S(1)} %pad_add_fusion.place, f32[256,2048]{1,0:T(8,128)S(1)} %pad_maximum_fusion.refs_0_.e_ref, ...), custom_call_target="tpu_custom_call" | custom-call | flops 1 | bytes 1 | tf_op jit(solution)/shard_map/pallas_call | solution.py:84
  74.6 0.9 collective-permute-start.20
  75.5 1.5 collective-permute-start.21
  77.0 3.1 %collective-permute-done.14 = f32[224,256]{1,0:T(8,128)S(1)} collective-permute-done((f32[224,256]{1,0:T(8,128)S(1)}, f32[224,256]{1,0:T(8,128)S(1)}, u32[]{:S(2)}, u32[]{:S(2)}) %collective-permute-start.14) | collective-permute-done | bytes 229408 | tf_op jit(solution)/shard_map/ppermute | solution.py:260
  80.1 1.5 collective-permute-start.22
  81.8 5.8 %collective-permute-done.21 = f32[192,256]{1,0:T(8,128)S(1)} collective-permute-done((f32[192,256]{1,0:T(8,128)S(1)}, f32[192,256]{1,0:T(8,128)S(1)}, u32[]{:S(2)}, u32[]{:S(2)}) %collective-permute-start.21) | collective-permute-done | bytes 196640 | tf_op jit(solution)/shard_map/ppermute | solution.py:260
  87.7 1.3 collective-permute-start.23
  89.0 0.8 collective-permute-start.24
  89.8 1.4 collective-permute-start.25
  91.2 2.5 %collective-permute-done.23 = f32[192,256]{1,0:T(8,128)S(1)} collective-permute-done((f32[192,256]{1,0:T(8,128)S(1)}, f32[192,256]{1,0:T(8,128)S(1)}, u32[]{:S(2)}, u32[]{:S(2)}) %collective-permute-start.23) | collective-permute-done | bytes 196640 | tf_op jit(solution)/shard_map/ppermute | solution.py:260
  93.8 3.3 %collective-permute-start.26 = (f32[128,256]{1,0:T(8,128)S(1)}, f32[128,256]{1,0:T(8,128)S(1)}, u32[]{:S(2)}, u32[]{:S(2)}) collective-permute-start(f32[128,256]{1,0:T(8,128)S(1)} %slice.93), channel_id=1, source_target_pairs={{0,1},{1,0},{2,3},{3,2},{4,5},{5,4},{6,7},{7,6},{8,9},{9,8},{10,11... | collective-permute-start | bytes 393224 | tf_op jit(solution)/shard_map/ppermute | solution.py:266
  97.1 2.9 %collective-permute-done.26 = f32[128,256]{1,0:T(8,128)S(1)} collective-permute-done((f32[128,256]{1,0:T(8,128)S(1)}, f32[128,256]{1,0:T(8,128)S(1)}, u32[]{:S(2)}, u32[]{:S(2)}) %collective-permute-start.26) | collective-permute-done | bytes 131104 | tf_op jit(solution)/shard_map/ppermute | solution.py:266
  100.0 1.2 collective-permute-start.28
  101.2 1.1 collective-permute-start.29
  102.2 1.2 collective-permute-start.30
  103.5 2.6 %shard_map.30 = (f32[4,64,256]{2,1,0:T(8,128)S(1)}, bf16[256,1024]{1,0:T(8,128)(2,1)S(1)}, bf16[256,1024]{1,0:T(8,128)(2,1)S(1)}, bf16[256,1024]{1,0:T(8,128)(2,1)S(1)}, bf16[256,1024]{1,0:T(8,128)(2,1)S(1)}) custom-call(s32[4]{0:T(128)S(1)} %pad_add_fusion.place, f32[256,2048]{1,0:T(8,128)S(1)} %pad_maximum_fusion.refs_0_.e_ref, ...), custom_call_target="tpu_custom_call" | custom-call | flops 1 | bytes 1 | tf_op jit(solution)/shard_map/pallas_call | solution.py:84
  106.3 2.0 %collective-permute-done.29 = f32[128,256]{1,0:T(8,128)S(1)} collective-permute-done((f32[128,256]{1,0:T(8,128)S(1)}, f32[128,256]{1,0:T(8,128)S(1)}, u32[]{:S(2)}, u32[]{:S(2)}) %collective-permute-start.29) | collective-permute-done | bytes 131104 | tf_op jit(solution)/shard_map/ppermute | solution.py:260
  108.2 1.4 collective-permute-done.30
  110.3 0.9 collective-permute-start.33
  111.2 1.4 collective-permute-start.34
  112.7 1.2 collective-permute-start.35
  113.9 4.5 %shard_map.31 = (f32[4,256,256]{2,1,0:T(8,128)S(1)}, f32[7,256,256]{2,1,0:T(8,128)S(1)}, bf16[256,768]{1,0:T(8,128)(2,1)S(1)}, bf16[256,768]{1,0:T(8,128)(2,1)S(1)}) custom-call(s32[4]{0:T(128)S(1)} %pad_add_fusion.place, f32[4,224,256]{2,1,0:T(8,128)S(1)} %pad_maximum_fusion.1.f01, f32[4,192,256]{2,1,0:T(8,128)S(1)} %pad_maximum_fusion.2.f2, ...), custom_call_target="tpu_custom_call" | custom-call | flops 1 | bytes 1 | tf_op jit(solution)/shard_map/pallas_call | solution.py:84
  118.5 1.2 copy-done
  121.9 1.4 collective-permute-start.37
  123.4 1.2 collective-permute-start.38
  124.6 1.5 copy-done.1
  126.1 3.0 %shard_map.32 = (bf16[1024,1024]{1,0:T(8,128)(2,1)S(1)}, bf16[1024,1024]{1,0:T(8,128)(2,1)S(1)}) custom-call(s32[4]{0:T(128)S(1)} %pad_add_fusion.place, f32[4,256,256]{2,1,0:T(8,128)S(1)} %get-tuple-element.84.t_ref, f32[7,256,256]{2,1,0:T(8,128)S(1)} %copy-done.1), custom_call_target="tpu_custom_call" | custom-call | flops 1 | bytes 1 | tf_op jit(solution)/shard_map/pallas_call | solution.py:84
  129.2 3.1 %shard_map.33 = (bf16[256,1024]{1,0:T(8,128)(2,1)S(1)}, bf16[256,1024]{1,0:T(8,128)(2,1)S(1)}) custom-call(s32[4]{0:T(128)S(1)} %pad_add_fusion.place, bf16[256,768]{1,0:T(8,128)(2,1)S(1)} %get-tuple-element.78.p_high, bf16[256,768]{1,0:T(8,128)(2,1)S(1)} %copy-done.27, bf16[1024,1024]{1,0:T(8,128)(2,1)S(1)} %get-tuple-element.88.m_high, ...), custom_call_target="tpu_custom_call" | custom-call | flops 1 | bytes 1 | tf_op jit(solution)/shard_map/pallas_call | solution.py:84
  132.5 2.4 %shard_map.34 = f32[4,64,1024]{2,1,0:T(8,128)S(1)} custom-call(s32[4]{0:T(128)S(1)} %pad_add_fusion.place, f32[256,2048]{1,0:T(8,128)S(1)} %pad_maximum_fusion.refs_0_.e_ref, bf16[256,1024]{1,0:T(8,128)(2,1)S(1)} %get-tuple-element.93.s_high, bf16[256,1024]{1,0:T(8,128)(2,1)S(1)} %get-tuple-element.94.s_low, bf16[512,1024]{1,0:T(8,128)(2,1)S(1)} %copy-done.7, ...), custom_call_target="tpu_custom_call" | custom-call | flops 1 | bytes 1 | tf_op jit(solution)/shard_map/pallas_call | solution.py:84
  134.9 0.9 collective-permute-start.39
  135.8 1.4 collective-permute-start.40
  137.3 1.2 collective-permute-start.41
  138.5 2.4 %shard_map.35 = f32[4,64,1024]{2,1,0:T(8,128)S(1)} custom-call(s32[4]{0:T(128)S(1)} %pad_add_fusion.place, f32[256,2048]{1,0:T(8,128)S(1)} %pad_maximum_fusion.refs_0_.e_ref, bf16[256,1024]{1,0:T(8,128)(2,1)S(1)} %get-tuple-element.93.s_high, bf16[256,1024]{1,0:T(8,128)(2,1)S(1)} %get-tuple-element.94.s_low, bf16[512,1024]{1,0:T(8,128)(2,1)S(1)} %copy-done.3, ...), custom_call_target="tpu_custom_call" | custom-call | flops 1 | bytes 1 | tf_op jit(solution)/shard_map/pallas_call | solution.py:84
  141.0 0.9 collective-permute-start.42
  141.9 1.4 collective-permute-start.43
  144.2 1.7 %collective-permute-start.44 = (f32[64,1024]{1,0:T(8,128)S(1)}, f32[64,1024]{1,0:T(8,128)S(1)}, u32[]{:S(2)}, u32[]{:S(2)}) collective-permute-start(f32[64,1024]{1,0:T(8,128)S(1)} %get-tuple-element.111), channel_id=1, source_target_pairs={{0,24},{4,28},{8,16},{12,20},{16,8},{20,12},{24,0},{28,4},{1,25},{... | collective-permute-start | bytes 786440 | tf_op jit(solution)/shard_map/ppermute | solution.py:260
  146.0 2.5 %collective-permute-done.40 = f32[64,1024]{1,0:T(8,128)S(1)} collective-permute-done((f32[64,1024]{1,0:T(8,128)S(1)}, f32[64,1024]{1,0:T(8,128)S(1)}, u32[]{:S(2)}, u32[]{:S(2)}) %collective-permute-start.40) | collective-permute-done | bytes 262176 | tf_op jit(solution)/shard_map/ppermute | solution.py:260
  148.5 1.9 %collective-permute-done.41 = f32[64,1024]{1,0:T(8,128)S(1)} collective-permute-done((f32[64,1024]{1,0:T(8,128)S(1)}, f32[64,1024]{1,0:T(8,128)S(1)}, u32[]{:S(2)}, u32[]{:S(2)}) %collective-permute-start.41) | collective-permute-done | bytes 262176 | tf_op jit(solution)/shard_map/ppermute | solution.py:260
  150.4 5.0 %collective-permute-done.42 = f32[64,1024]{1,0:T(8,128)S(1)} collective-permute-done((f32[64,1024]{1,0:T(8,128)S(1)}, f32[64,1024]{1,0:T(8,128)S(1)}, u32[]{:S(2)}, u32[]{:S(2)}) %collective-permute-start.42) | collective-permute-done | bytes 262176 | tf_op jit(solution)/shard_map/ppermute | solution.py:260
  155.5 3.5 %collective-permute-done.43 = f32[64,1024]{1,0:T(8,128)S(1)} collective-permute-done((f32[64,1024]{1,0:T(8,128)S(1)}, f32[64,1024]{1,0:T(8,128)S(1)}, u32[]{:S(2)}, u32[]{:S(2)}) %collective-permute-start.43) | collective-permute-done | bytes 262176 | tf_op jit(solution)/shard_map/ppermute | solution.py:260
  159.1 1.3 copy-done.28
  (123 shorter events, 9.0 us)
Async XLA Ops:
  0.0 6.3 %copy-start.29 = (f32[64,8192]{1,0:T(8,128)S(1)}, f32[64,8192]{1,0:T(8,128)}, u32[]{:S(2)}) copy-start(f32[64,8192]{1,0:T(8,128)} %param.2) | copy-start | bytes 6291460
  1.6 30.9 %collective-permute-start.3 = (f32[256,1024]{1,0:T(8,128)S(1)}, f32[256,1024]{1,0:T(8,128)}, u32[]{:S(2)}, u32[]{:S(2)}) collective-permute-start(f32[256,1024]{1,0:T(8,128)S(1)} %select_select_fusion.refs_1_), channel_id=1, source_target_pairs={{0,1},{1,0},{2,3},{3,2},{4,5},{5,4},{6,7},{7,6},{8,9},{9,8},{10,11... | collective-permute-start | bytes 3145736 | tf_op jit(solution)/shard_map/ppermute | solution.py:266
  4.7 27.9 %collective-permute-start.4 = (f32[256,1024]{1,0:T(8,128)S(1)}, f32[256,1024]{1,0:T(8,128)}, u32[]{:S(2)}, u32[]{:S(2)}) collective-permute-start(f32[256,1024]{1,0:T(8,128)S(1)} %select_select_fusion.refs_1_), channel_id=1, source_target_pairs={{1,2},{2,1},{5,6},{6,5},{9,10},{10,9},{13,14},{14,13},{17,18},{18,... | collective-permute-start | bytes 3145736 | tf_op jit(solution)/shard_map/ppermute | solution.py:266
  6.5 14.9 %collective-permute-start = (f32[64,2048]{1,0:T(8,128)S(1)}, f32[64,2048]{1,0:T(8,128)S(1)}, u32[]{:S(2)}, u32[]{:S(2)}) collective-permute-start(f32[64,2048]{1,0:T(8,128)S(1)} %get-tuple-element.110), channel_id=1, source_target_pairs={{0,8},{4,12},{8,0},{12,4},{16,24},{20,28},{24,16},{28,20},{1,9},{5... | collective-permute-start | bytes 1572872 | tf_op jit(solution)/shard_map/ppermute | solution.py:260
  8.0 24.3 %collective-permute-start.1 = (f32[64,2048]{1,0:T(8,128)S(1)}, f32[64,2048]{1,0:T(8,128)S(1)}, u32[]{:S(2)}, u32[]{:S(2)}) collective-permute-start(f32[64,2048]{1,0:T(8,128)S(1)} %get-tuple-element.109), channel_id=1, source_target_pairs={{0,16},{4,20},{8,24},{12,28},{16,0},{20,4},{24,8},{28,12},{1,17},{... | collective-permute-start | bytes 1572872 | tf_op jit(solution)/shard_map/ppermute | solution.py:260
  9.6 22.8 %collective-permute-start.2 = (f32[64,2048]{1,0:T(8,128)S(1)}, f32[64,2048]{1,0:T(8,128)S(1)}, u32[]{:S(2)}, u32[]{:S(2)}) collective-permute-start(f32[64,2048]{1,0:T(8,128)S(1)} %get-tuple-element.108), channel_id=1, source_target_pairs={{0,24},{4,28},{8,16},{12,20},{16,8},{20,12},{24,0},{28,4},{1,25},{... | collective-permute-start | bytes 1572872 | tf_op jit(solution)/shard_map/ppermute | solution.py:260
  32.6 3.6 %collective-permute-start.7 = (f32[256,1024]{1,0:T(8,128)S(1)}, f32[256,1024]{1,0:T(8,128)}, u32[]{:S(2)}, u32[]{:S(2)}) collective-permute-start(f32[256,1024]{1,0:T(8,128)S(1)} %select_select_fusion.refs_1_), channel_id=1, source_target_pairs={{0,4},{4,0},{8,12},{12,8},{16,20},{20,16},{24,28},{28,24},{1,5},{5... | collective-permute-start | bytes 3145736 | tf_op jit(solution)/shard_map/ppermute | solution.py:263
  32.6 4.5 %collective-permute-start.8 = (f32[256,1024]{1,0:T(8,128)}, f32[256,1024]{1,0:T(8,128)}, u32[]{:S(2)}, u32[]{:S(2)}) collective-permute-start(f32[256,1024]{1,0:T(8,128)} %collective-permute-done.3.refs_3_), channel_id=1, source_target_pairs={{0,4},{4,0},{8,12},{12,8},{16,20},{20,16},{24,28},{28,24},{1,5},{5... | collective-permute-start | bytes 3145736 | tf_op jit(solution)/shard_map/ppermute | solution.py:263
  33.1 30.0 %collective-permute-start.6 = (f32[256,1024]{1,0:T(8,128)}, f32[256,1024]{1,0:T(8,128)S(1)}, u32[]{:S(2)}, u32[]{:S(2)}) collective-permute-start(f32[256,1024]{1,0:T(8,128)} %collective-permute-done.3.refs_3_), channel_id=1, source_target_pairs={{1,2},{2,1},{5,6},{6,5},{9,10},{10,9},{13,14},{14,13},{17,18},{18,... | collective-permute-start | bytes 3145736 | tf_op jit(solution)/shard_map/ppermute | solution.py:266
  33.9 29.3 %collective-permute-start.5 = (f32[256,1024]{1,0:T(8,128)}, f32[256,1024]{1,0:T(8,128)S(1)}, u32[]{:S(2)}, u32[]{:S(2)}) collective-permute-start(f32[256,1024]{1,0:T(8,128)} %collective-permute-done.4.refs_9_.refs_3_), channel_id=1, source_target_pairs={{1,0},{2,3},{5,4},{6,7},{9,8},{10,11},{13,12},{14,15},{17,16},{18,... | collective-permute-start | bytes 3145736 | tf_op jit(solution)/shard_map/ppermute | solution.py:266
  44.1 24.1 %copy-start.2 = (bf16[512,1024]{1,0:T(8,128)(2,1)}, bf16[512,1024]{1,0:T(8,128)(2,1)S(1)}, u32[]{:S(2)}) copy-start(bf16[512,1024]{1,0:T(8,128)(2,1)S(1)} %get-tuple-element.101.refs_0_) | copy-start | bytes 3145732
  44.1 30.4 %copy-start.4 = (bf16[512,1024]{1,0:T(8,128)(2,1)}, bf16[512,1024]{1,0:T(8,128)(2,1)S(1)}, u32[]{:S(2)}) copy-start(bf16[512,1024]{1,0:T(8,128)(2,1)S(1)} %get-tuple-element.102.refs_1_) | copy-start | bytes 3145732
  44.1 12.6 %collective-permute-start.10 = (f32[224,256]{1,0:T(8,128)S(1)}, f32[224,256]{1,0:T(8,128)S(1)}, u32[]{:S(2)}, u32[]{:S(2)}) collective-permute-start(f32[224,256]{1,0:T(8,128)S(1)} %get-tuple-element.119), channel_id=1, source_target_pairs={{0,16},{4,20},{8,24},{12,28},{16,0},{20,4},{24,8},{28,12},{1,17},{... | collective-permute-start | bytes 688136 | tf_op jit(solution)/shard_map/ppermute | solution.py:260
  45.7 11.0 %collective-permute-start.11 = (f32[224,256]{1,0:T(8,128)S(1)}, f32[224,256]{1,0:T(8,128)S(1)}, u32[]{:S(2)}, u32[]{:S(2)}) collective-permute-start(f32[224,256]{1,0:T(8,128)S(1)} %get-tuple-element.118), channel_id=1, source_target_pairs={{0,24},{4,28},{8,16},{12,20},{16,8},{20,12},{24,0},{28,4},{1,25},{... | collective-permute-start | bytes 688136 | tf_op jit(solution)/shard_map/ppermute | solution.py:260
  46.9 11.1 %collective-permute-start.9 = (f32[224,256]{1,0:T(8,128)S(1)}, f32[224,256]{1,0:T(8,128)S(1)}, u32[]{:S(2)}, u32[]{:S(2)}) collective-permute-start(f32[224,256]{1,0:T(8,128)S(1)} %get-tuple-element.117), channel_id=1, source_target_pairs={{0,8},{4,12},{8,0},{12,4},{16,24},{20,28},{24,16},{28,20},{1,9},{5... | collective-permute-start | bytes 688136 | tf_op jit(solution)/shard_map/ppermute | solution.py:260
  58.1 6.6 %collective-permute-start.12 = (f32[224,256]{1,0:T(8,128)S(1)}, f32[224,256]{1,0:T(8,128)S(1)}, u32[]{:S(2)}, u32[]{:S(2)}) collective-permute-start(f32[224,256]{1,0:T(8,128)S(1)} %fusion.3), channel_id=1, source_target_pairs={{0,8},{4,12},{8,0},{12,4},{16,24},{20,28},{24,16},{28,20},{1,9},{5... | collective-permute-start | bytes 688136 | tf_op jit(solution)/shard_map/ppermute | solution.py:260
  59.4 8.9 %collective-permute-start.19 = (f32[256,1024]{1,0:T(8,128)}, f32[256,1024]{1,0:T(8,128)S(1)}, u32[]{:S(2)}, u32[]{:S(2)}) collective-permute-start(f32[256,1024]{1,0:T(8,128)} %collective-permute-done.4.refs_9_.refs_3_), channel_id=1, source_target_pairs={{0,4},{4,0},{8,12},{12,8},{16,20},{20,16},{24,28},{28,24},{1,5},{5... | collective-permute-start | bytes 3145736 | tf_op jit(solution)/shard_map/ppermute | solution.py:263
  64.7 4.7 %collective-permute-start.17 = (f32[256,1024]{1,0:T(8,128)S(1)}, f32[256,1024]{1,0:T(8,128)S(1)}, u32[]{:S(2)}, u32[]{:S(2)}) collective-permute-start(f32[256,1024]{1,0:T(8,128)S(1)} %collective-permute-done.5.refs_5_), channel_id=1, source_target_pairs={{0,4},{4,0},{8,12},{12,8},{16,20},{20,16},{24,28},{28,24},{1,5},{5... | collective-permute-start | bytes 3145736 | tf_op jit(solution)/shard_map/ppermute | solution.py:263
  64.7 4.7 %collective-permute-start.18 = (f32[256,1024]{1,0:T(8,128)S(1)}, f32[256,1024]{1,0:T(8,128)S(1)}, u32[]{:S(2)}, u32[]{:S(2)}) collective-permute-start(f32[256,1024]{1,0:T(8,128)S(1)} %collective-permute-done.6.refs_7_), channel_id=1, source_target_pairs={{0,4},{4,0},{8,12},{12,8},{16,20},{20,16},{24,28},{28,24},{1,5},{5... | collective-permute-start | bytes 3145736 | tf_op jit(solution)/shard_map/ppermute | solution.py:263
  65.2 31.9 %collective-permute-start.13 = (f32[256,1024]{1,0:T(8,128)S(1)}, f32[256,1024]{1,0:T(8,128)S(1)}, u32[]{:S(2)}, u32[]{:S(2)}) collective-permute-start(f32[256,1024]{1,0:T(8,128)S(1)} %collective-permute-done.6.refs_7_), channel_id=1, source_target_pairs={{1,0},{2,3},{5,4},{6,7},{9,8},{10,11},{13,12},{14,15},{17,16},{18,... | collective-permute-start | bytes 3145736 | tf_op jit(solution)/shard_map/ppermute | solution.py:266
  66.7 13.5 %collective-permute-start.14 = (f32[224,256]{1,0:T(8,128)S(1)}, f32[224,256]{1,0:T(8,128)S(1)}, u32[]{:S(2)}, u32[]{:S(2)}) collective-permute-start(f32[224,256]{1,0:T(8,128)S(1)} %fusion.3), channel_id=1, source_target_pairs={{0,16},{4,20},{8,24},{12,28},{16,0},{20,4},{24,8},{28,12},{1,17},{... | collective-permute-start | bytes 688136 | tf_op jit(solution)/shard_map/ppermute | solution.py:260
  68.2 13.4 %collective-permute-start.15 = (f32[224,256]{1,0:T(8,128)S(1)}, f32[224,256]{1,0:T(8,128)S(1)}, u32[]{:S(2)}, u32[]{:S(2)}) collective-permute-start(f32[224,256]{1,0:T(8,128)S(1)} %fusion.3), channel_id=1, source_target_pairs={{0,24},{4,28},{8,16},{12,20},{16,8},{20,12},{24,0},{28,4},{1,25},{... | collective-permute-start | bytes 688136 | tf_op jit(solution)/shard_map/ppermute | solution.py:260
  74.5 13.1 %copy-start.10 = (bf16[256,1024]{1,0:T(8,128)(2,1)}, bf16[256,1024]{1,0:T(8,128)(2,1)S(1)}, u32[]{:S(2)}) copy-start(bf16[256,1024]{1,0:T(8,128)(2,1)S(1)} %get-tuple-element.103.refs_2_) | copy-start | bytes 1572868
  74.5 13.1 %copy-start.12 = (bf16[256,1024]{1,0:T(8,128)(2,1)}, bf16[256,1024]{1,0:T(8,128)(2,1)S(1)}, u32[]{:S(2)}) copy-start(bf16[256,1024]{1,0:T(8,128)(2,1)S(1)} %get-tuple-element.104.refs_3_) | copy-start | bytes 1572868
  74.5 13.1 %copy-start.14 = (bf16[256,1024]{1,0:T(8,128)(2,1)}, bf16[256,1024]{1,0:T(8,128)(2,1)S(1)}, u32[]{:S(2)}) copy-start(bf16[256,1024]{1,0:T(8,128)(2,1)S(1)} %get-tuple-element.97.refs_2_) | copy-start | bytes 1572868
  74.6 13.1 %copy-start.16 = (bf16[256,1024]{1,0:T(8,128)(2,1)}, bf16[256,1024]{1,0:T(8,128)(2,1)S(1)}, u32[]{:S(2)}) copy-start(bf16[256,1024]{1,0:T(8,128)(2,1)S(1)} %get-tuple-element.98.refs_3_) | copy-start | bytes 1572868
  74.6 7.2 %collective-permute-start.20 = (f32[192,256]{1,0:T(8,128)S(1)}, f32[192,256]{1,0:T(8,128)S(1)}, u32[]{:S(2)}, u32[]{:S(2)}) collective-permute-start(f32[192,256]{1,0:T(8,128)S(1)} %get-tuple-element.120), channel_id=1, source_target_pairs={{0,8},{4,12},{8,0},{12,4},{16,24},{20,28},{24,16},{28,20},{1,9},{5... | collective-permute-start | bytes 589832 | tf_op jit(solution)/shard_map/ppermute | solution.py:260
  75.5 12.1 %collective-permute-start.21 = (f32[192,256]{1,0:T(8,128)S(1)}, f32[192,256]{1,0:T(8,128)S(1)}, u32[]{:S(2)}, u32[]{:S(2)}) collective-permute-start(f32[192,256]{1,0:T(8,128)S(1)} %get-tuple-element.122), channel_id=1, source_target_pairs={{0,16},{4,20},{8,24},{12,28},{16,0},{20,4},{24,8},{28,12},{1,17},{... | collective-permute-start | bytes 589832 | tf_op jit(solution)/shard_map/ppermute | solution.py:260
  80.1 7.5 %collective-permute-start.22 = (f32[192,256]{1,0:T(8,128)S(1)}, f32[192,256]{1,0:T(8,128)S(1)}, u32[]{:S(2)}, u32[]{:S(2)}) collective-permute-start(f32[192,256]{1,0:T(8,128)S(1)} %get-tuple-element.121), channel_id=1, source_target_pairs={{0,24},{4,28},{8,16},{12,20},{16,8},{20,12},{24,0},{28,4},{1,25},{... | collective-permute-start | bytes 589832 | tf_op jit(solution)/shard_map/ppermute | solution.py:260
  81.7 15.4 %collective-permute-start.16 = (f32[4,96,256]{2,1,0:T(8,128)S(1)}, f32[4,96,256]{2,1,0:T(8,128)S(1)}, u32[]{:S(2)}, u32[]{:S(2)}) collective-permute-start(f32[4,96,256]{2,1,0:T(8,128)S(1)} %slice.92), channel_id=1, source_target_pairs={{0,4},{4,0},{8,12},{12,8},{16,20},{20,16},{24,28},{28,24},{1,5},{5... | collective-permute-start | bytes 1179656 | tf_op jit(solution)/shard_map/ppermute | solution.py:263
  87.7 6.1 %collective-permute-start.23 = (f32[192,256]{1,0:T(8,128)S(1)}, f32[192,256]{1,0:T(8,128)S(1)}, u32[]{:S(2)}, u32[]{:S(2)}) collective-permute-start(f32[192,256]{1,0:T(8,128)S(1)} %fusion.5), channel_id=1, source_target_pairs={{0,8},{4,12},{8,0},{12,4},{16,24},{20,28},{24,16},{28,20},{1,9},{5... | collective-permute-start | bytes 589832 | tf_op jit(solution)/shard_map/ppermute | solution.py:260
  89.0 8.1 %collective-permute-start.24 = (f32[192,256]{1,0:T(8,128)S(1)}, f32[192,256]{1,0:T(8,128)S(1)}, u32[]{:S(2)}, u32[]{:S(2)}) collective-permute-start(f32[192,256]{1,0:T(8,128)S(1)} %fusion.5), channel_id=1, source_target_pairs={{0,16},{4,20},{8,24},{12,28},{16,0},{20,4},{24,8},{28,12},{1,17},{... | collective-permute-start | bytes 589832 | tf_op jit(solution)/shard_map/ppermute | solution.py:260
  89.8 7.2 %collective-permute-start.25 = (f32[192,256]{1,0:T(8,128)S(1)}, f32[192,256]{1,0:T(8,128)S(1)}, u32[]{:S(2)}, u32[]{:S(2)}) collective-permute-start(f32[192,256]{1,0:T(8,128)S(1)} %fusion.5), channel_id=1, source_target_pairs={{0,24},{4,28},{8,16},{12,20},{16,8},{20,12},{24,0},{28,4},{1,25},{... | collective-permute-start | bytes 589832 | tf_op jit(solution)/shard_map/ppermute | solution.py:260
  93.8 6.2 %collective-permute-start.26 = (f32[128,256]{1,0:T(8,128)S(1)}, f32[128,256]{1,0:T(8,128)S(1)}, u32[]{:S(2)}, u32[]{:S(2)}) collective-permute-start(f32[128,256]{1,0:T(8,128)S(1)} %slice.93), channel_id=1, source_target_pairs={{0,1},{1,0},{2,3},{3,2},{4,5},{5,4},{6,7},{7,6},{8,9},{9,8},{10,11... | collective-permute-start | bytes 393224 | tf_op jit(solution)/shard_map/ppermute | solution.py:266
  100.0 3.5 %collective-permute-start.27 = (f32[256,1024]{1,0:T(8,128)S(1)}, f32[256,1024]{1,0:T(8,128)S(1)}, u32[]{:S(2)}, u32[]{:S(2)}) collective-permute-start(f32[256,1024]{1,0:T(8,128)S(1)} %collective-permute-done.13.refs_1_), channel_id=1, source_target_pairs={{0,4},{4,0},{8,12},{12,8},{16,20},{20,16},{24,28},{28,24},{1,5},{5... | collective-permute-start | bytes 3145736 | tf_op jit(solution)/shard_map/ppermute | solution.py:263
  100.0 6.3 %collective-permute-start.28 = (f32[128,256]{1,0:T(8,128)S(1)}, f32[128,256]{1,0:T(8,128)S(1)}, u32[]{:S(2)}, u32[]{:S(2)}) collective-permute-start(f32[128,256]{1,0:T(8,128)S(1)} %collective-permute-done.26), channel_id=1, source_target_pairs={{0,8},{4,12},{8,0},{12,4},{16,24},{20,28},{24,16},{28,20},{1,9},{5... | collective-permute-start | bytes 393224 | tf_op jit(solution)/shard_map/ppermute | solution.py:260
  101.2 7.0 %collective-permute-start.29 = (f32[128,256]{1,0:T(8,128)S(1)}, f32[128,256]{1,0:T(8,128)S(1)}, u32[]{:S(2)}, u32[]{:S(2)}) collective-permute-start(f32[128,256]{1,0:T(8,128)S(1)} %collective-permute-done.26), channel_id=1, source_target_pairs={{0,16},{4,20},{8,24},{12,28},{16,0},{20,4},{24,8},{28,12},{1,17},{... | collective-permute-start | bytes 393224 | tf_op jit(solution)/shard_map/ppermute | solution.py:260
  102.2 7.4 %collective-permute-start.30 = (f32[128,256]{1,0:T(8,128)S(1)}, f32[128,256]{1,0:T(8,128)S(1)}, u32[]{:S(2)}, u32[]{:S(2)}) collective-permute-start(f32[128,256]{1,0:T(8,128)S(1)} %collective-permute-done.26), channel_id=1, source_target_pairs={{0,24},{4,28},{8,16},{12,20},{16,8},{20,12},{24,0},{28,4},{1,25},{... | collective-permute-start | bytes 393224 | tf_op jit(solution)/shard_map/ppermute | solution.py:260
  106.0 12.4 %copy-start.18 = (bf16[256,1024]{1,0:T(8,128)(2,1)}, bf16[256,1024]{1,0:T(8,128)(2,1)S(1)}, u32[]{:S(2)}) copy-start(bf16[256,1024]{1,0:T(8,128)(2,1)S(1)} %get-tuple-element.105.refs_4_) | copy-start | bytes 1572868
  106.1 12.4 %copy-start.20 = (bf16[256,1024]{1,0:T(8,128)(2,1)}, bf16[256,1024]{1,0:T(8,128)(2,1)S(1)}, u32[]{:S(2)}) copy-start(bf16[256,1024]{1,0:T(8,128)(2,1)S(1)} %get-tuple-element.106.refs_5_) | copy-start | bytes 1572868
  106.1 12.4 %copy-start.22 = (bf16[256,1024]{1,0:T(8,128)(2,1)}, bf16[256,1024]{1,0:T(8,128)(2,1)S(1)}, u32[]{:S(2)}) copy-start(bf16[256,1024]{1,0:T(8,128)(2,1)S(1)} %get-tuple-element.99.refs_4_) | copy-start | bytes 1572868
  106.1 12.4 %copy-start.24 = (bf16[256,1024]{1,0:T(8,128)(2,1)}, bf16[256,1024]{1,0:T(8,128)(2,1)S(1)}, u32[]{:S(2)}) copy-start(bf16[256,1024]{1,0:T(8,128)(2,1)S(1)} %get-tuple-element.100.refs_5_) | copy-start | bytes 1572868
  109.6 4.3 %collective-permute-start.32 = (f32[4,128,256]{2,1,0:T(8,128)S(1)}, f32[4,128,256]{2,1,0:T(8,128)S(1)}, u32[]{:S(2)}, u32[]{:S(2)}) collective-permute-start(f32[4,128,256]{2,1,0:T(8,128)S(1)} %pad_maximum_fusion.3.fb), channel_id=1, source_target_pairs={{0,4},{4,0},{8,12},{12,8},{16,20},{20,16},{24,28},{28,24},{1,5},{5... | collective-permute-start | bytes 1572872 | tf_op jit(solution)/shard_map/ppermute | solution.py:263
  109.8 4.1 %collective-permute-start.31 = (f32[4,128,256]{2,1,0:T(8,128)S(1)}, f32[4,128,256]{2,1,0:T(8,128)S(1)}, u32[]{:S(2)}, u32[]{:S(2)}) collective-permute-start(f32[4,128,256]{2,1,0:T(8,128)S(1)} %slice.79), channel_id=1, source_target_pairs={{0,4},{4,0},{8,12},{12,8},{16,20},{20,16},{24,28},{28,24},{1,5},{5... | collective-permute-start | bytes 1572872 | tf_op jit(solution)/shard_map/ppermute | solution.py:263
  110.3 10.1 %collective-permute-start.33 = (f32[64,256]{1,0:T(8,128)S(1)}, f32[64,256]{1,0:T(8,128)S(1)}, u32[]{:S(2)}, u32[]{:S(2)}) collective-permute-start(f32[64,256]{1,0:T(8,128)S(1)} %get-tuple-element.125), channel_id=1, source_target_pairs={{0,8},{4,12},{8,0},{12,4},{16,24},{20,28},{24,16},{28,20},{1,9},{5... | collective-permute-start | bytes 196616 | tf_op jit(solution)/shard_map/ppermute | solution.py:260
  111.2 9.2 %collective-permute-start.34 = (f32[64,256]{1,0:T(8,128)S(1)}, f32[64,256]{1,0:T(8,128)S(1)}, u32[]{:S(2)}, u32[]{:S(2)}) collective-permute-start(f32[64,256]{1,0:T(8,128)S(1)} %get-tuple-element.124), channel_id=1, source_target_pairs={{0,16},{4,20},{8,24},{12,28},{16,0},{20,4},{24,8},{28,12},{1,17},{... | collective-permute-start | bytes 196616 | tf_op jit(solution)/shard_map/ppermute | solution.py:260
  112.7 7.8 %collective-permute-start.35 = (f32[64,256]{1,0:T(8,128)S(1)}, f32[64,256]{1,0:T(8,128)S(1)}, u32[]{:S(2)}, u32[]{:S(2)}) collective-permute-start(f32[64,256]{1,0:T(8,128)S(1)} %get-tuple-element.123), channel_id=1, source_target_pairs={{0,24},{4,28},{8,16},{12,20},{16,8},{20,12},{24,0},{28,4},{1,25},{... | collective-permute-start | bytes 196616 | tf_op jit(solution)/shard_map/ppermute | solution.py:260
  121.1 8.0 %collective-permute-start.36 = (f32[64,256]{1,0:T(8,128)}, f32[64,256]{1,0:T(8,128)}, u32[]{:S(2)}, u32[]{:S(2)}) collective-permute-start(f32[64,256]{1,0:T(8,128)} %fusion.7.refs_0_), channel_id=1, source_target_pairs={{0,8},{4,12},{8,0},{12,4},{16,24},{20,28},{24,16},{28,20},{1,9},{5... | collective-permute-start | bytes 196616 | tf_op jit(solution)/shard_map/ppermute | solution.py:260
  121.9 7.2 %collective-permute-start.37 = (f32[64,256]{1,0:T(8,128)}, f32[64,256]{1,0:T(8,128)}, u32[]{:S(2)}, u32[]{:S(2)}) collective-permute-start(f32[64,256]{1,0:T(8,128)} %fusion.7.refs_0_), channel_id=1, source_target_pairs={{0,16},{4,20},{8,24},{12,28},{16,0},{20,4},{24,8},{28,12},{1,17},{... | collective-permute-start | bytes 196616 | tf_op jit(solution)/shard_map/ppermute | solution.py:260
  123.4 5.8 %collective-permute-start.38 = (f32[64,256]{1,0:T(8,128)}, f32[64,256]{1,0:T(8,128)}, u32[]{:S(2)}, u32[]{:S(2)}) collective-permute-start(f32[64,256]{1,0:T(8,128)} %fusion.7.refs_0_), channel_id=1, source_target_pairs={{0,24},{4,28},{8,16},{12,20},{16,8},{20,12},{24,0},{28,4},{1,25},{... | collective-permute-start | bytes 196616 | tf_op jit(solution)/shard_map/ppermute | solution.py:260
  129.2 3.2 %copy-start.7 = (bf16[512,1024]{1,0:T(8,128)(2,1)S(1)}, bf16[512,1024]{1,0:T(8,128)(2,1)}, u32[]{:S(2)}) copy-start(bf16[512,1024]{1,0:T(8,128)(2,1)} %copy-done.6) | copy-start | bytes 3145732
  129.2 3.2 %copy-start.9 = (bf16[512,1024]{1,0:T(8,128)(2,1)S(1)}, bf16[512,1024]{1,0:T(8,128)(2,1)}, u32[]{:S(2)}) copy-start(bf16[512,1024]{1,0:T(8,128)(2,1)} %copy-done.8) | copy-start | bytes 3145732
  132.4 6.1 %copy-start.5 = (bf16[512,1024]{1,0:T(8,128)(2,1)S(1)}, bf16[512,1024]{1,0:T(8,128)(2,1)}, u32[]{:S(2)}) copy-start(bf16[512,1024]{1,0:T(8,128)(2,1)} %copy-done.4) | copy-start | bytes 3145732
  132.4 6.1 %copy-start.11 = (bf16[256,1024]{1,0:T(8,128)(2,1)S(1)}, bf16[256,1024]{1,0:T(8,128)(2,1)}, u32[]{:S(2)}) copy-start(bf16[256,1024]{1,0:T(8,128)(2,1)} %copy-done.10) | copy-start | bytes 1572868
  132.4 6.1 %copy-start.13 = (bf16[256,1024]{1,0:T(8,128)(2,1)S(1)}, bf16[256,1024]{1,0:T(8,128)(2,1)}, u32[]{:S(2)}) copy-start(bf16[256,1024]{1,0:T(8,128)(2,1)} %copy-done.12) | copy-start | bytes 1572868
  132.5 6.0 %copy-start.19 = (bf16[256,1024]{1,0:T(8,128)(2,1)S(1)}, bf16[256,1024]{1,0:T(8,128)(2,1)}, u32[]{:S(2)}) copy-start(bf16[256,1024]{1,0:T(8,128)(2,1)} %copy-done.18) | copy-start | bytes 1572868
  132.5 6.0 %copy-start.21 = (bf16[256,1024]{1,0:T(8,128)(2,1)S(1)}, bf16[256,1024]{1,0:T(8,128)(2,1)}, u32[]{:S(2)}) copy-start(bf16[256,1024]{1,0:T(8,128)(2,1)} %copy-done.20) | copy-start | bytes 1572868
  134.9 3.7 %copy-start.3 = (bf16[512,1024]{1,0:T(8,128)(2,1)S(1)}, bf16[512,1024]{1,0:T(8,128)(2,1)}, u32[]{:S(2)}) copy-start(bf16[512,1024]{1,0:T(8,128)(2,1)} %copy-done.2) | copy-start | bytes 3145732
  134.9 9.3 %collective-permute-start.39 = (f32[64,1024]{1,0:T(8,128)S(1)}, f32[64,1024]{1,0:T(8,128)S(1)}, u32[]{:S(2)}, u32[]{:S(2)}) collective-permute-start(f32[64,1024]{1,0:T(8,128)S(1)} %get-tuple-element.116), channel_id=1, source_target_pairs={{0,8},{4,12},{8,0},{12,4},{16,24},{20,28},{24,16},{28,20},{1,9},{5... | collective-permute-start | bytes 786440 | tf_op jit(solution)/shard_map/ppermute | solution.py:260
  135.8 12.6 %collective-permute-start.40 = (f32[64,1024]{1,0:T(8,128)S(1)}, f32[64,1024]{1,0:T(8,128)S(1)}, u32[]{:S(2)}, u32[]{:S(2)}) collective-permute-start(f32[64,1024]{1,0:T(8,128)S(1)} %get-tuple-element.115), channel_id=1, source_target_pairs={{0,16},{4,20},{8,24},{12,28},{16,0},{20,4},{24,8},{28,12},{1,17},{... | collective-permute-start | bytes 786440 | tf_op jit(solution)/shard_map/ppermute | solution.py:260
  137.3 13.1 %collective-permute-start.41 = (f32[64,1024]{1,0:T(8,128)S(1)}, f32[64,1024]{1,0:T(8,128)S(1)}, u32[]{:S(2)}, u32[]{:S(2)}) collective-permute-start(f32[64,1024]{1,0:T(8,128)S(1)} %get-tuple-element.114), channel_id=1, source_target_pairs={{0,24},{4,28},{8,16},{12,20},{16,8},{20,12},{24,0},{28,4},{1,25},{... | collective-permute-start | bytes 786440 | tf_op jit(solution)/shard_map/ppermute | solution.py:260
  141.0 14.5 %collective-permute-start.42 = (f32[64,1024]{1,0:T(8,128)S(1)}, f32[64,1024]{1,0:T(8,128)S(1)}, u32[]{:S(2)}, u32[]{:S(2)}) collective-permute-start(f32[64,1024]{1,0:T(8,128)S(1)} %get-tuple-element.113), channel_id=1, source_target_pairs={{0,8},{4,12},{8,0},{12,4},{16,24},{20,28},{24,16},{28,20},{1,9},{5... | collective-permute-start | bytes 786440 | tf_op jit(solution)/shard_map/ppermute | solution.py:260
  141.9 17.2 %collective-permute-start.43 = (f32[64,1024]{1,0:T(8,128)S(1)}, f32[64,1024]{1,0:T(8,128)S(1)}, u32[]{:S(2)}, u32[]{:S(2)}) collective-permute-start(f32[64,1024]{1,0:T(8,128)S(1)} %get-tuple-element.112), channel_id=1, source_target_pairs={{0,16},{4,20},{8,24},{12,28},{16,0},{20,4},{24,8},{28,12},{1,17},{... | collective-permute-start | bytes 786440 | tf_op jit(solution)/shard_map/ppermute | solution.py:260
  144.2 14.8 %collective-permute-start.44 = (f32[64,1024]{1,0:T(8,128)S(1)}, f32[64,1024]{1,0:T(8,128)S(1)}, u32[]{:S(2)}, u32[]{:S(2)}) collective-permute-start(f32[64,1024]{1,0:T(8,128)S(1)} %get-tuple-element.111), channel_id=1, source_target_pairs={{0,24},{4,28},{8,16},{12,20},{16,8},{20,12},{24,0},{28,4},{1,25},{... | collective-permute-start | bytes 786440 | tf_op jit(solution)/shard_map/ppermute | solution.py:260
  (11 other events, 22.6 us)

commit v5 on v4

--- a/solution.py
+++ b/solution.py
@@ -245,6 +245,12 @@
         out_ref[:, :, k : k + step] = value.reshape(chips, mine, step)
 
 
+def first_kernel(chips, place, *refs):
+    ins, (high_ref, low_ref, out_ref) = refs[:-3], refs[-3:]
+    apply_kernel(place, *ins[: 4 + chips], high_ref, low_ref)
+    update_kernel(chips, 0, place, ins[4 + chips], high_ref, low_ref, *ins[5 + chips :], out_ref)
+
+
 def panels_on_cols(eigvecs, reflectors, chips):
     width = reflectors.shape[1]
     r, c = lax.axis_index("row"), lax.axis_index("col")
@@ -330,19 +336,18 @@
     from_3 = [across(held_3, x) for x in range(1, chips)]
     from_3, inverse = lax.optimization_barrier((from_3, inverse))
     solved = b16(chips * mine, PANELS * B)
-    solved = call(
-        apply_kernel, (solved, solved), place, *p_early, *inverse, held_3, *from_3, limit=16
+    dones = f32(chips, mine, width)
+    kept = [kept_01[2 * h : 2 * h + 2] + kept_2[2 * h : 2 * h + 2] + kept_3[2 * h : 2 * h + 2] for h in range(2)]
+    *solved, first = call(
+        functools.partial(first_kernel, chips),
+        (solved, solved, dones),
+        place,
+        *(*p_early, *inverse, held_3, *from_3, grid, *kept[0]),
+        limit=24,
     )
+    second = call(functools.partial(update_kernel, chips, 1), dones, place, grid, *solved, *kept[1], limit=20)
     result = jnp.zeros_like(eigvecs)
-    for half in range(2):
-        done = call(
-            functools.partial(update_kernel, chips, half),
-            f32(chips, mine, width),
-            place,
-            *(grid, *solved),
-            *(kept_01[2 * half : 2 * half + 2] + kept_2[2 * half : 2 * half + 2] + kept_3[2 * half : 2 * half + 2]),
-            limit=20,
-        )
+    for half, done in enumerate((first, second)):
         for x in range(chips):
             piece = across(done[x], x) if x else done[x]
             start = (chip ^ x) * 2 * width + (core ^ half) * width

time: 161 us -> 165 us (1.025)
  local copies, waits for them, and re-layouts: 8.29 us -> 12.5 us
    unnamed x60 -> x64, local copies, waits for them, and re-layouts: 6.83 us -> 11.1 us
    pallas_call x8 -> x7, Pallas kernels: 28.1 us -> 27.4 us  [call(): pl.pallas_call(kernel, out_shape=out_shape, in_specs=[pl.BlockSpec(memory...]
where the time goes in v5:
time: 165 us
  waiting for transfers between devices  71.4 us (43%)
  starting transfers between devices  49.9 us (30%)
  Pallas kernels  27.4 us (17%)
  local copies, waits for them, and re-layouts  12.5 us (8%)
  other arithmetic  2.68 us (2%)
    ppermute x30, waiting for transfers between devices, across(): lax.ppermute(value, 'row', [(i, i ^ 2 * x) for i in range(2 * chips)])  62.9 us
    ppermute x30, starting transfers between devices, across(): lax.ppermute(value, 'row', [(i, i ^ 2 * x) for i in range(2 * chips)])  36.7 us
    pallas_call x7, Pallas kernels, call(): pl.pallas_call(kernel, out_shape=out_shape, in_specs=[pl.BlockSpec(memory...  27.4 us
    ppermute x6, starting transfers between devices, zmove(): return lax.ppermute(value, 'col', pairs)  11.5 us
    unnamed x64, local copies, waits for them, and re-layouts  11.1 us
    ppermute x6, waiting for transfers between devices, zmove(): return lax.ppermute(value, 'col', pairs)  6.61 us
  transfers between devices with their start and end apart: 45, of which 20 were waited for; matrix products, arithmetic and copies ran while one was open for 1% of the time, Pallas kernels for 14%

profile of v5, /device:TPU:0, one launch (start us, length us, event | category | flops | bytes accessed | tf_op | source)
XLA Modules:
  0.0 164.6 jit_solution(7736584830555365737)
XLA Ops:
  0.0 1.6 select_select_fusion.refs_1_
  1.6 3.1 %collective-permute-start.3 = (f32[256,1024]{1,0:T(8,128)S(1)}, f32[256,1024]{1,0:T(8,128)}, u32[]{:S(2)}, u32[]{:S(2)}) collective-permute-start(f32[256,1024]{1,0:T(8,128)S(1)} %select_select_fusion.refs_1_), channel_id=1, source_target_pairs={{0,1},{1,0},{2,3},{3,2},{4,5},{5,4},{6,7},{7,6},{8,9},{9,8},{10,11... | collective-permute-start | bytes 3145736 | tf_op jit(solution)/shard_map/ppermute | solution.py:272
  4.7 1.6 collective-permute-start.4
  6.5 1.6 collective-permute-start
  8.0 1.5 collective-permute-start.1
  10.0 11.4 %collective-permute-done = f32[64,2048]{1,0:T(8,128)S(1)} collective-permute-done((f32[64,2048]{1,0:T(8,128)S(1)}, f32[64,2048]{1,0:T(8,128)S(1)}, u32[]{:S(2)}, u32[]{:S(2)}) %collective-permute-start) | collective-permute-done | bytes 524320 | tf_op jit(solution)/shard_map/ppermute | solution.py:266
  21.4 11.0 %collective-permute-done.1 = f32[64,2048]{1,0:T(8,128)S(1)} collective-permute-done((f32[64,2048]{1,0:T(8,128)S(1)}, f32[64,2048]{1,0:T(8,128)S(1)}, u32[]{:S(2)}, u32[]{:S(2)}) %collective-permute-start.1) | collective-permute-done | bytes 524320 | tf_op jit(solution)/shard_map/ppermute | solution.py:266
  33.8 1.3 collective-permute-start.5
  36.1 1.0 collective-permute-done.8.refs_4_
  37.1 5.0 %shard_map.28 = (f32[4,224,256]{2,1,0:T(8,128)S(1)}, bf16[512,1024]{1,0:T(8,128)(2,1)S(1)}, bf16[512,1024]{1,0:T(8,128)(2,1)S(1)}, bf16[512,1024]{1,0:T(8,128)(2,1)S(1)}, bf16[512,1024]{1,0:T(8,128)(2,1)S(1)}) custom-call(s32[4]{0:T(128)S(1)} %pad_add_fusion.place, f32[256,2048]{1,0:T(8,128)S(1)} %pad_maximum_fusion.refs_0_.refs_8_.e_ref, ...), custom_call_target="tpu_custom_call" | custom-call | flops 1 | bytes 1 | tf_op jit(solution)/shard_map/pallas_call | solution.py:84
  42.1 1.0 copy-done.6
  43.1 1.0 copy-done.8
  44.2 1.6 collective-permute-start.10
  45.7 1.2 collective-permute-start.11
  47.7 9.1 %collective-permute-done.10 = f32[224,256]{1,0:T(8,128)S(1)} collective-permute-done((f32[224,256]{1,0:T(8,128)S(1)}, f32[224,256]{1,0:T(8,128)S(1)}, u32[]{:S(2)}, u32[]{:S(2)}) %collective-permute-start.10) | collective-permute-done | bytes 229408 | tf_op jit(solution)/shard_map/ppermute | solution.py:266
  56.8 1.2 collective-permute-done.9
  58.1 1.3 collective-permute-start.12
  59.4 3.7 %collective-permute-done.5.refs_5_ = f32[256,1024]{1,0:T(8,128)S(1)} collective-permute-done((f32[256,1024]{1,0:T(8,128)}, f32[256,1024]{1,0:T(8,128)S(1)}, u32[]{:S(2)}, u32[]{:S(2)}) %collective-permute-start.5) | collective-permute-done | bytes 1048608 | tf_op jit(solution)/shard_map/ppermute | solution.py:272
  63.1 1.6 collective-permute-done.12
  65.2 1.5 collective-permute-start.13
  66.7 1.6 collective-permute-start.14
  68.2 1.2 collective-permute-start.15
  69.4 5.1 %shard_map.29 = (f32[4,192,256]{2,1,0:T(8,128)S(1)}, bf16[256,1024]{1,0:T(8,128)(2,1)S(1)}, bf16[256,1024]{1,0:T(8,128)(2,1)S(1)}, bf16[256,1024]{1,0:T(8,128)(2,1)S(1)}, bf16[256,1024]{1,0:T(8,128)(2,1)S(1)}) custom-call(s32[4]{0:T(128)S(1)} %pad_add_fusion.place, f32[256,2048]{1,0:T(8,128)S(1)} %pad_maximum_fusion.refs_0_.refs_8_.e_ref, ...), custom_call_target="tpu_custom_call" | custom-call | flops 1 | bytes 1 | tf_op jit(solution)/shard_map/pallas_call | solution.py:84
  75.5 1.5 collective-permute-start.21
  77.0 3.1 %collective-permute-done.14 = f32[224,256]{1,0:T(8,128)S(1)} collective-permute-done((f32[224,256]{1,0:T(8,128)S(1)}, f32[224,256]{1,0:T(8,128)S(1)}, u32[]{:S(2)}, u32[]{:S(2)}) %collective-permute-start.14) | collective-permute-done | bytes 229408 | tf_op jit(solution)/shard_map/ppermute | solution.py:266
  80.1 1.5 collective-permute-start.22
  81.8 5.8 %collective-permute-done.21 = f32[192,256]{1,0:T(8,128)S(1)} collective-permute-done((f32[192,256]{1,0:T(8,128)S(1)}, f32[192,256]{1,0:T(8,128)S(1)}, u32[]{:S(2)}, u32[]{:S(2)}) %collective-permute-start.21) | collective-permute-done | bytes 196640 | tf_op jit(solution)/shard_map/ppermute | solution.py:266
  87.7 1.3 collective-permute-start.23
  89.8 1.4 collective-permute-start.25
  91.2 2.5 %collective-permute-done.23 = f32[192,256]{1,0:T(8,128)S(1)} collective-permute-done((f32[192,256]{1,0:T(8,128)S(1)}, f32[192,256]{1,0:T(8,128)S(1)}, u32[]{:S(2)}, u32[]{:S(2)}) %collective-permute-start.23) | collective-permute-done | bytes 196640 | tf_op jit(solution)/shard_map/ppermute | solution.py:266
  93.8 3.3 %collective-permute-start.26 = (f32[128,256]{1,0:T(8,128)S(1)}, f32[128,256]{1,0:T(8,128)S(1)}, u32[]{:S(2)}, u32[]{:S(2)}) collective-permute-start(f32[128,256]{1,0:T(8,128)S(1)} %slice.93), channel_id=1, source_target_pairs={{0,1},{1,0},{2,3},{3,2},{4,5},{5,4},{6,7},{7,6},{8,9},{9,8},{10,11... | collective-permute-start | bytes 393224 | tf_op jit(solution)/shard_map/ppermute | solution.py:272
  97.1 2.9 %collective-permute-done.26 = f32[128,256]{1,0:T(8,128)S(1)} collective-permute-done((f32[128,256]{1,0:T(8,128)S(1)}, f32[128,256]{1,0:T(8,128)S(1)}, u32[]{:S(2)}, u32[]{:S(2)}) %collective-permute-start.26) | collective-permute-done | bytes 131104 | tf_op jit(solution)/shard_map/ppermute | solution.py:272
  100.0 1.2 collective-permute-start.28
  101.2 1.1 collective-permute-start.29
  102.2 1.2 collective-permute-start.30
  103.5 2.6 %shard_map.30 = (f32[4,64,256]{2,1,0:T(8,128)S(1)}, bf16[256,1024]{1,0:T(8,128)(2,1)S(1)}, bf16[256,1024]{1,0:T(8,128)(2,1)S(1)}, bf16[256,1024]{1,0:T(8,128)(2,1)S(1)}, bf16[256,1024]{1,0:T(8,128)(2,1)S(1)}) custom-call(s32[4]{0:T(128)S(1)} %pad_add_fusion.place, f32[256,2048]{1,0:T(8,128)S(1)} %pad_maximum_fusion.refs_0_.refs_8_.e_ref, ...), custom_call_target="tpu_custom_call" | custom-call | flops 1 | bytes 1 | tf_op jit(solution)/shard_map/pallas_call | solution.py:84
  106.3 2.0 %collective-permute-done.29 = f32[128,256]{1,0:T(8,128)S(1)} collective-permute-done((f32[128,256]{1,0:T(8,128)S(1)}, f32[128,256]{1,0:T(8,128)S(1)}, u32[]{:S(2)}, u32[]{:S(2)}) %collective-permute-start.29) | collective-permute-done | bytes 131104 | tf_op jit(solution)/shard_map/ppermute | solution.py:266
  108.2 1.4 collective-permute-done.30
  110.4 0.9 collective-permute-start.33
  111.3 1.4 collective-permute-start.34
  112.7 1.2 collective-permute-start.35
  113.9 4.5 %shard_map.31 = (f32[4,256,256]{2,1,0:T(8,128)S(1)}, f32[7,256,256]{2,1,0:T(8,128)S(1)}, bf16[256,768]{1,0:T(8,128)(2,1)S(1)}, bf16[256,768]{1,0:T(8,128)(2,1)S(1)}) custom-call(s32[4]{0:T(128)S(1)} %pad_add_fusion.place, f32[4,224,256]{2,1,0:T(8,128)S(1)} %pad_maximum_fusion.1.f01, f32[4,192,256]{2,1,0:T(8,128)S(1)} %pad_maximum_fusion.2.f2, ...), custom_call_target="tpu_custom_call" | custom-call | flops 1 | bytes 1 | tf_op jit(solution)/shard_map/pallas_call | solution.py:84
  118.5 1.2 copy-done
  119.7 1.0 copy-done.10
  122.9 1.4 collective-permute-start.37
  124.4 1.2 collective-permute-start.38
  125.6 1.5 copy-done.1
  127.1 1.2 copy-done.11
  128.3 3.0 %shard_map.32 = (bf16[1024,1024]{1,0:T(8,128)(2,1)S(1)}, bf16[1024,1024]{1,0:T(8,128)(2,1)S(1)}) custom-call(s32[4]{0:T(128)S(1)} %pad_add_fusion.place, f32[4,256,256]{2,1,0:T(8,128)S(1)} %copy-done.11, f32[7,256,256]{2,1,0:T(8,128)S(1)} %copy-done.1), custom_call_target="tpu_custom_call" | custom-call | flops 1 | bytes 1 | tf_op jit(solution)/shard_map/pallas_call | solution.py:84
  131.5 1.0 copy-done.27
  132.5 1.0 copy-done.29
  133.5 4.8 %shard_map.33 = (bf16[256,1024]{1,0:T(8,128)(2,1)S(1)}, bf16[256,1024]{1,0:T(8,128)(2,1)S(1)}, f32[4,64,1024]{2,1,0:T(8,128)S(1)}) custom-call(s32[4]{0:T(128)S(1)} %pad_add_fusion.place, bf16[256,768]{1,0:T(8,128)(2,1)S(1)} %get-tuple-element.79.refs_0_, bf16[256,768]{1,0:T(8,128)(2,1)S(1)} %copy-done.29, bf16[1024,1024]{1,0:T(8,128)(2,1)S(1)} %get-tuple-element.89.refs_2_, ...), custom_call_target="tpu_custom_call" | custom-call | flops 1 | bytes 1 | tf_op jit(solution)/shard_map/pallas_call | solution.py:84
  138.4 0.9 collective-permute-start.39
  139.3 1.4 collective-permute-start.40
  140.7 1.2 collective-permute-start.41
  142.0 2.4 %shard_map.34 = f32[4,64,1024]{2,1,0:T(8,128)S(1)} custom-call(s32[4]{0:T(128)S(1)} %pad_add_fusion.place, f32[256,2048]{1,0:T(8,128)S(1)} %pad_maximum_fusion.refs_0_.refs_8_.e_ref, bf16[256,1024]{1,0:T(8,128)(2,1)S(1)} %get-tuple-element.101.s_high, bf16[256,1024]{1,0:T(8,128)(2,1)S(1)} %get-tuple-element.102.s_low, bf16[512,1024]{1,0:T(8,128)(2,1)S(1)} %copy-done.3, ...), custom_call_target="tpu_custom_call" | custom-call | flops 1 | bytes 1 | tf_op jit(solution)/shard_map/pallas_call | solution.py:84
  144.5 0.9 collective-permute-start.42
  145.3 1.4 collective-permute-start.43
  147.7 1.7 %collective-permute-start.44 = (f32[64,1024]{1,0:T(8,128)S(1)}, f32[64,1024]{1,0:T(8,128)S(1)}, u32[]{:S(2)}, u32[]{:S(2)}) collective-permute-start(f32[64,1024]{1,0:T(8,128)S(1)} %get-tuple-element.113), channel_id=1, source_target_pairs={{0,24},{4,28},{8,16},{12,20},{16,8},{20,12},{24,0},{28,4},{1,25},{... | collective-permute-start | bytes 786440 | tf_op jit(solution)/shard_map/ppermute | solution.py:266
  149.4 2.4 %collective-permute-done.40 = f32[64,1024]{1,0:T(8,128)S(1)} collective-permute-done((f32[64,1024]{1,0:T(8,128)S(1)}, f32[64,1024]{1,0:T(8,128)S(1)}, u32[]{:S(2)}, u32[]{:S(2)}) %collective-permute-start.40) | collective-permute-done | bytes 262176 | tf_op jit(solution)/shard_map/ppermute | solution.py:266
  151.9 1.9 %collective-permute-done.41 = f32[64,1024]{1,0:T(8,128)S(1)} collective-permute-done((f32[64,1024]{1,0:T(8,128)S(1)}, f32[64,1024]{1,0:T(8,128)S(1)}, u32[]{:S(2)}, u32[]{:S(2)}) %collective-permute-start.41) | collective-permute-done | bytes 262176 | tf_op jit(solution)/shard_map/ppermute | solution.py:266
  153.9 5.1 %collective-permute-done.42 = f32[64,1024]{1,0:T(8,128)S(1)} collective-permute-done((f32[64,1024]{1,0:T(8,128)S(1)}, f32[64,1024]{1,0:T(8,128)S(1)}, u32[]{:S(2)}, u32[]{:S(2)}) %collective-permute-start.42) | collective-permute-done | bytes 262176 | tf_op jit(solution)/shard_map/ppermute | solution.py:266
  159.0 3.5 %collective-permute-done.43 = f32[64,1024]{1,0:T(8,128)S(1)} collective-permute-done((f32[64,1024]{1,0:T(8,128)S(1)}, f32[64,1024]{1,0:T(8,128)S(1)}, u32[]{:S(2)}, u32[]{:S(2)}) %collective-permute-start.43) | collective-permute-done | bytes 262176 | tf_op jit(solution)/shard_map/ppermute | solution.py:266
  162.6 1.3 copy-done.30
  (126 shorter events, 11.6 us)
Async XLA Ops:
  0.0 6.3 %copy-start.31 = (f32[64,8192]{1,0:T(8,128)S(1)}, f32[64,8192]{1,0:T(8,128)}, u32[]{:S(2)}) copy-start(f32[64,8192]{1,0:T(8,128)} %param.2) | copy-start | bytes 6291460
  1.6 30.9 %collective-permute-start.3 = (f32[256,1024]{1,0:T(8,128)S(1)}, f32[256,1024]{1,0:T(8,128)}, u32[]{:S(2)}, u32[]{:S(2)}) collective-permute-start(f32[256,1024]{1,0:T(8,128)S(1)} %select_select_fusion.refs_1_), channel_id=1, source_target_pairs={{0,1},{1,0},{2,3},{3,2},{4,5},{5,4},{6,7},{7,6},{8,9},{9,8},{10,11... | collective-permute-start | bytes 3145736 | tf_op jit(solution)/shard_map/ppermute | solution.py:272
  4.7 27.9 %collective-permute-start.4 = (f32[256,1024]{1,0:T(8,128)S(1)}, f32[256,1024]{1,0:T(8,128)}, u32[]{:S(2)}, u32[]{:S(2)}) collective-permute-start(f32[256,1024]{1,0:T(8,128)S(1)} %select_select_fusion.refs_1_), channel_id=1, source_target_pairs={{1,2},{2,1},{5,6},{6,5},{9,10},{10,9},{13,14},{14,13},{17,18},{18,... | collective-permute-start | bytes 3145736 | tf_op jit(solution)/shard_map/ppermute | solution.py:272
  6.5 14.9 %collective-permute-start = (f32[64,2048]{1,0:T(8,128)S(1)}, f32[64,2048]{1,0:T(8,128)S(1)}, u32[]{:S(2)}, u32[]{:S(2)}) collective-permute-start(f32[64,2048]{1,0:T(8,128)S(1)} %get-tuple-element.112), channel_id=1, source_target_pairs={{0,8},{4,12},{8,0},{12,4},{16,24},{20,28},{24,16},{28,20},{1,9},{5... | collective-permute-start | bytes 1572872 | tf_op jit(solution)/shard_map/ppermute | solution.py:266
  8.0 24.3 %collective-permute-start.1 = (f32[64,2048]{1,0:T(8,128)S(1)}, f32[64,2048]{1,0:T(8,128)S(1)}, u32[]{:S(2)}, u32[]{:S(2)}) collective-permute-start(f32[64,2048]{1,0:T(8,128)S(1)} %get-tuple-element.111), channel_id=1, source_target_pairs={{0,16},{4,20},{8,24},{12,28},{16,0},{20,4},{24,8},{28,12},{1,17},{... | collective-permute-start | bytes 1572872 | tf_op jit(solution)/shard_map/ppermute | solution.py:266
  9.6 22.8 %collective-permute-start.2 = (f32[64,2048]{1,0:T(8,128)S(1)}, f32[64,2048]{1,0:T(8,128)S(1)}, u32[]{:S(2)}, u32[]{:S(2)}) collective-permute-start(f32[64,2048]{1,0:T(8,128)S(1)} %get-tuple-element.110), channel_id=1, source_target_pairs={{0,24},{4,28},{8,16},{12,20},{16,8},{20,12},{24,0},{28,4},{1,25},{... | collective-permute-start | bytes 1572872 | tf_op jit(solution)/shard_map/ppermute | solution.py:266
  32.5 3.6 %collective-permute-start.7 = (f32[256,1024]{1,0:T(8,128)S(1)}, f32[256,1024]{1,0:T(8,128)}, u32[]{:S(2)}, u32[]{:S(2)}) collective-permute-start(f32[256,1024]{1,0:T(8,128)S(1)} %select_select_fusion.refs_1_), channel_id=1, source_target_pairs={{0,4},{4,0},{8,12},{12,8},{16,20},{20,16},{24,28},{28,24},{1,5},{5... | collective-permute-start | bytes 3145736 | tf_op jit(solution)/shard_map/ppermute | solution.py:269
  32.6 4.5 %collective-permute-start.8 = (f32[256,1024]{1,0:T(8,128)}, f32[256,1024]{1,0:T(8,128)}, u32[]{:S(2)}, u32[]{:S(2)}) collective-permute-start(f32[256,1024]{1,0:T(8,128)} %collective-permute-done.3.refs_3_), channel_id=1, source_target_pairs={{0,4},{4,0},{8,12},{12,8},{16,20},{20,16},{24,28},{28,24},{1,5},{5... | collective-permute-start | bytes 3145736 | tf_op jit(solution)/shard_map/ppermute | solution.py:269
  33.1 30.0 %collective-permute-start.6 = (f32[256,1024]{1,0:T(8,128)}, f32[256,1024]{1,0:T(8,128)S(1)}, u32[]{:S(2)}, u32[]{:S(2)}) collective-permute-start(f32[256,1024]{1,0:T(8,128)} %collective-permute-done.3.refs_3_), channel_id=1, source_target_pairs={{1,2},{2,1},{5,6},{6,5},{9,10},{10,9},{13,14},{14,13},{17,18},{18,... | collective-permute-start | bytes 3145736 | tf_op jit(solution)/shard_map/ppermute | solution.py:272
  33.8 29.3 %collective-permute-start.5 = (f32[256,1024]{1,0:T(8,128)}, f32[256,1024]{1,0:T(8,128)S(1)}, u32[]{:S(2)}, u32[]{:S(2)}) collective-permute-start(f32[256,1024]{1,0:T(8,128)} %collective-permute-done.4.refs_9_.refs_3_), channel_id=1, source_target_pairs={{1,0},{2,3},{5,4},{6,7},{9,8},{10,11},{13,12},{14,15},{17,16},{18,... | collective-permute-start | bytes 3145736 | tf_op jit(solution)/shard_map/ppermute | solution.py:272
  44.1 24.1 %copy-start.2 = (bf16[512,1024]{1,0:T(8,128)(2,1)}, bf16[512,1024]{1,0:T(8,128)(2,1)S(1)}, u32[]{:S(2)}) copy-start(bf16[512,1024]{1,0:T(8,128)(2,1)S(1)} %get-tuple-element.103.refs_0_) | copy-start | bytes 3145732
  44.1 30.4 %copy-start.4 = (bf16[512,1024]{1,0:T(8,128)(2,1)}, bf16[512,1024]{1,0:T(8,128)(2,1)S(1)}, u32[]{:S(2)}) copy-start(bf16[512,1024]{1,0:T(8,128)(2,1)S(1)} %get-tuple-element.104.refs_1_) | copy-start | bytes 3145732
  44.2 12.6 %collective-permute-start.10 = (f32[224,256]{1,0:T(8,128)S(1)}, f32[224,256]{1,0:T(8,128)S(1)}, u32[]{:S(2)}, u32[]{:S(2)}) collective-permute-start(f32[224,256]{1,0:T(8,128)S(1)} %get-tuple-element.121), channel_id=1, source_target_pairs={{0,16},{4,20},{8,24},{12,28},{16,0},{20,4},{24,8},{28,12},{1,17},{... | collective-permute-start | bytes 688136 | tf_op jit(solution)/shard_map/ppermute | solution.py:266
  45.7 11.0 %collective-permute-start.11 = (f32[224,256]{1,0:T(8,128)S(1)}, f32[224,256]{1,0:T(8,128)S(1)}, u32[]{:S(2)}, u32[]{:S(2)}) collective-permute-start(f32[224,256]{1,0:T(8,128)S(1)} %get-tuple-element.120), channel_id=1, source_target_pairs={{0,24},{4,28},{8,16},{12,20},{16,8},{20,12},{24,0},{28,4},{1,25},{... | collective-permute-start | bytes 688136 | tf_op jit(solution)/shard_map/ppermute | solution.py:266
  46.9 11.1 %collective-permute-start.9 = (f32[224,256]{1,0:T(8,128)S(1)}, f32[224,256]{1,0:T(8,128)S(1)}, u32[]{:S(2)}, u32[]{:S(2)}) collective-permute-start(f32[224,256]{1,0:T(8,128)S(1)} %get-tuple-element.119), channel_id=1, source_target_pairs={{0,8},{4,12},{8,0},{12,4},{16,24},{20,28},{24,16},{28,20},{1,9},{5... | collective-permute-start | bytes 688136 | tf_op jit(solution)/shard_map/ppermute | solution.py:266
  58.1 6.6 %collective-permute-start.12 = (f32[224,256]{1,0:T(8,128)S(1)}, f32[224,256]{1,0:T(8,128)S(1)}, u32[]{:S(2)}, u32[]{:S(2)}) collective-permute-start(f32[224,256]{1,0:T(8,128)S(1)} %fusion.2), channel_id=1, source_target_pairs={{0,8},{4,12},{8,0},{12,4},{16,24},{20,28},{24,16},{28,20},{1,9},{5... | collective-permute-start | bytes 688136 | tf_op jit(solution)/shard_map/ppermute | solution.py:266
  59.4 8.9 %collective-permute-start.19 = (f32[256,1024]{1,0:T(8,128)}, f32[256,1024]{1,0:T(8,128)S(1)}, u32[]{:S(2)}, u32[]{:S(2)}) collective-permute-start(f32[256,1024]{1,0:T(8,128)} %collective-permute-done.4.refs_9_.refs_3_), channel_id=1, source_target_pairs={{0,4},{4,0},{8,12},{12,8},{16,20},{20,16},{24,28},{28,24},{1,5},{5... | collective-permute-start | bytes 3145736 | tf_op jit(solution)/shard_map/ppermute | solution.py:269
  64.7 4.8 %collective-permute-start.17 = (f32[256,1024]{1,0:T(8,128)S(1)}, f32[256,1024]{1,0:T(8,128)S(1)}, u32[]{:S(2)}, u32[]{:S(2)}) collective-permute-start(f32[256,1024]{1,0:T(8,128)S(1)} %collective-permute-done.5.refs_5_), channel_id=1, source_target_pairs={{0,4},{4,0},{8,12},{12,8},{16,20},{20,16},{24,28},{28,24},{1,5},{5... | collective-permute-start | bytes 3145736 | tf_op jit(solution)/shard_map/ppermute | solution.py:269
  64.7 4.8 %collective-permute-start.18 = (f32[256,1024]{1,0:T(8,128)S(1)}, f32[256,1024]{1,0:T(8,128)S(1)}, u32[]{:S(2)}, u32[]{:S(2)}) collective-permute-start(f32[256,1024]{1,0:T(8,128)S(1)} %collective-permute-done.6.refs_7_), channel_id=1, source_target_pairs={{0,4},{4,0},{8,12},{12,8},{16,20},{20,16},{24,28},{28,24},{1,5},{5... | collective-permute-start | bytes 3145736 | tf_op jit(solution)/shard_map/ppermute | solution.py:269
  65.2 31.9 %collective-permute-start.13 = (f32[256,1024]{1,0:T(8,128)S(1)}, f32[256,1024]{1,0:T(8,128)S(1)}, u32[]{:S(2)}, u32[]{:S(2)}) collective-permute-start(f32[256,1024]{1,0:T(8,128)S(1)} %collective-permute-done.6.refs_7_), channel_id=1, source_target_pairs={{1,0},{2,3},{5,4},{6,7},{9,8},{10,11},{13,12},{14,15},{17,16},{18,... | collective-permute-start | bytes 3145736 | tf_op jit(solution)/shard_map/ppermute | solution.py:272
  66.7 13.5 %collective-permute-start.14 = (f32[224,256]{1,0:T(8,128)S(1)}, f32[224,256]{1,0:T(8,128)S(1)}, u32[]{:S(2)}, u32[]{:S(2)}) collective-permute-start(f32[224,256]{1,0:T(8,128)S(1)} %fusion.2), channel_id=1, source_target_pairs={{0,16},{4,20},{8,24},{12,28},{16,0},{20,4},{24,8},{28,12},{1,17},{... | collective-permute-start | bytes 688136 | tf_op jit(solution)/shard_map/ppermute | solution.py:266
  68.2 13.4 %collective-permute-start.15 = (f32[224,256]{1,0:T(8,128)S(1)}, f32[224,256]{1,0:T(8,128)S(1)}, u32[]{:S(2)}, u32[]{:S(2)}) collective-permute-start(f32[224,256]{1,0:T(8,128)S(1)} %fusion.2), channel_id=1, source_target_pairs={{0,24},{4,28},{8,16},{12,20},{16,8},{20,12},{24,0},{28,4},{1,25},{... | collective-permute-start | bytes 688136 | tf_op jit(solution)/shard_map/ppermute | solution.py:266
  74.6 13.1 %copy-start.12 = (bf16[256,1024]{1,0:T(8,128)(2,1)}, bf16[256,1024]{1,0:T(8,128)(2,1)S(1)}, u32[]{:S(2)}) copy-start(bf16[256,1024]{1,0:T(8,128)(2,1)S(1)} %get-tuple-element.105.refs_2_) | copy-start | bytes 1572868
  74.6 13.1 %copy-start.14 = (bf16[256,1024]{1,0:T(8,128)(2,1)}, bf16[256,1024]{1,0:T(8,128)(2,1)S(1)}, u32[]{:S(2)}) copy-start(bf16[256,1024]{1,0:T(8,128)(2,1)S(1)} %get-tuple-element.106.refs_3_) | copy-start | bytes 1572868
  74.6 13.1 %copy-start.16 = (bf16[256,1024]{1,0:T(8,128)(2,1)}, bf16[256,1024]{1,0:T(8,128)(2,1)S(1)}, u32[]{:S(2)}) copy-start(bf16[256,1024]{1,0:T(8,128)(2,1)S(1)} %get-tuple-element.96.refs_11_) | copy-start | bytes 1572868
  74.6 13.1 %copy-start.18 = (bf16[256,1024]{1,0:T(8,128)(2,1)}, bf16[256,1024]{1,0:T(8,128)(2,1)S(1)}, u32[]{:S(2)}) copy-start(bf16[256,1024]{1,0:T(8,128)(2,1)S(1)} %get-tuple-element.97.refs_12_) | copy-start | bytes 1572868
  74.6 7.2 %collective-permute-start.20 = (f32[192,256]{1,0:T(8,128)S(1)}, f32[192,256]{1,0:T(8,128)S(1)}, u32[]{:S(2)}, u32[]{:S(2)}) collective-permute-start(f32[192,256]{1,0:T(8,128)S(1)} %get-tuple-element.122), channel_id=1, source_target_pairs={{0,8},{4,12},{8,0},{12,4},{16,24},{20,28},{24,16},{28,20},{1,9},{5... | collective-permute-start | bytes 589832 | tf_op jit(solution)/shard_map/ppermute | solution.py:266
  75.5 12.1 %collective-permute-start.21 = (f32[192,256]{1,0:T(8,128)S(1)}, f32[192,256]{1,0:T(8,128)S(1)}, u32[]{:S(2)}, u32[]{:S(2)}) collective-permute-start(f32[192,256]{1,0:T(8,128)S(1)} %get-tuple-element.124), channel_id=1, source_target_pairs={{0,16},{4,20},{8,24},{12,28},{16,0},{20,4},{24,8},{28,12},{1,17},{... | collective-permute-start | bytes 589832 | tf_op jit(solution)/shard_map/ppermute | solution.py:266
  80.1 7.5 %collective-permute-start.22 = (f32[192,256]{1,0:T(8,128)S(1)}, f32[192,256]{1,0:T(8,128)S(1)}, u32[]{:S(2)}, u32[]{:S(2)}) collective-permute-start(f32[192,256]{1,0:T(8,128)S(1)} %get-tuple-element.123), channel_id=1, source_target_pairs={{0,24},{4,28},{8,16},{12,20},{16,8},{20,12},{24,0},{28,4},{1,25},{... | collective-permute-start | bytes 589832 | tf_op jit(solution)/shard_map/ppermute | solution.py:266
  81.7 15.4 %collective-permute-start.16 = (f32[4,96,256]{2,1,0:T(8,128)S(1)}, f32[4,96,256]{2,1,0:T(8,128)S(1)}, u32[]{:S(2)}, u32[]{:S(2)}) collective-permute-start(f32[4,96,256]{2,1,0:T(8,128)S(1)} %slice.92), channel_id=1, source_target_pairs={{0,4},{4,0},{8,12},{12,8},{16,20},{20,16},{24,28},{28,24},{1,5},{5... | collective-permute-start | bytes 1179656 | tf_op jit(solution)/shard_map/ppermute | solution.py:269
  87.7 6.1 %collective-permute-start.23 = (f32[192,256]{1,0:T(8,128)S(1)}, f32[192,256]{1,0:T(8,128)S(1)}, u32[]{:S(2)}, u32[]{:S(2)}) collective-permute-start(f32[192,256]{1,0:T(8,128)S(1)} %fusion.4), channel_id=1, source_target_pairs={{0,8},{4,12},{8,0},{12,4},{16,24},{20,28},{24,16},{28,20},{1,9},{5... | collective-permute-start | bytes 589832 | tf_op jit(solution)/shard_map/ppermute | solution.py:266
  89.0 8.1 %collective-permute-start.24 = (f32[192,256]{1,0:T(8,128)S(1)}, f32[192,256]{1,0:T(8,128)S(1)}, u32[]{:S(2)}, u32[]{:S(2)}) collective-permute-start(f32[192,256]{1,0:T(8,128)S(1)} %fusion.4), channel_id=1, source_target_pairs={{0,16},{4,20},{8,24},{12,28},{16,0},{20,4},{24,8},{28,12},{1,17},{... | collective-permute-start | bytes 589832 | tf_op jit(solution)/shard_map/ppermute | solution.py:266
  89.8 7.2 %collective-permute-start.25 = (f32[192,256]{1,0:T(8,128)S(1)}, f32[192,256]{1,0:T(8,128)S(1)}, u32[]{:S(2)}, u32[]{:S(2)}) collective-permute-start(f32[192,256]{1,0:T(8,128)S(1)} %fusion.4), channel_id=1, source_target_pairs={{0,24},{4,28},{8,16},{12,20},{16,8},{20,12},{24,0},{28,4},{1,25},{... | collective-permute-start | bytes 589832 | tf_op jit(solution)/shard_map/ppermute | solution.py:266
  93.8 6.2 %collective-permute-start.26 = (f32[128,256]{1,0:T(8,128)S(1)}, f32[128,256]{1,0:T(8,128)S(1)}, u32[]{:S(2)}, u32[]{:S(2)}) collective-permute-start(f32[128,256]{1,0:T(8,128)S(1)} %slice.93), channel_id=1, source_target_pairs={{0,1},{1,0},{2,3},{3,2},{4,5},{5,4},{6,7},{7,6},{8,9},{9,8},{10,11... | collective-permute-start | bytes 393224 | tf_op jit(solution)/shard_map/ppermute | solution.py:272
  100.0 3.5 %collective-permute-start.27 = (f32[256,1024]{1,0:T(8,128)S(1)}, f32[256,1024]{1,0:T(8,128)S(1)}, u32[]{:S(2)}, u32[]{:S(2)}) collective-permute-start(f32[256,1024]{1,0:T(8,128)S(1)} %collective-permute-done.13.refs_1_), channel_id=1, source_target_pairs={{0,4},{4,0},{8,12},{12,8},{16,20},{20,16},{24,28},{28,24},{1,5},{5... | collective-permute-start | bytes 3145736 | tf_op jit(solution)/shard_map/ppermute | solution.py:269
  100.0 6.3 %collective-permute-start.28 = (f32[128,256]{1,0:T(8,128)S(1)}, f32[128,256]{1,0:T(8,128)S(1)}, u32[]{:S(2)}, u32[]{:S(2)}) collective-permute-start(f32[128,256]{1,0:T(8,128)S(1)} %collective-permute-done.26), channel_id=1, source_target_pairs={{0,8},{4,12},{8,0},{12,4},{16,24},{20,28},{24,16},{28,20},{1,9},{5... | collective-permute-start | bytes 393224 | tf_op jit(solution)/shard_map/ppermute | solution.py:266
  101.2 7.0 %collective-permute-start.29 = (f32[128,256]{1,0:T(8,128)S(1)}, f32[128,256]{1,0:T(8,128)S(1)}, u32[]{:S(2)}, u32[]{:S(2)}) collective-permute-start(f32[128,256]{1,0:T(8,128)S(1)} %collective-permute-done.26), channel_id=1, source_target_pairs={{0,16},{4,20},{8,24},{12,28},{16,0},{20,4},{24,8},{28,12},{1,17},{... | collective-permute-start | bytes 393224 | tf_op jit(solution)/shard_map/ppermute | solution.py:266
  102.2 7.4 %collective-permute-start.30 = (f32[128,256]{1,0:T(8,128)S(1)}, f32[128,256]{1,0:T(8,128)S(1)}, u32[]{:S(2)}, u32[]{:S(2)}) collective-permute-start(f32[128,256]{1,0:T(8,128)S(1)} %collective-permute-done.26), channel_id=1, source_target_pairs={{0,24},{4,28},{8,16},{12,20},{16,8},{20,12},{24,0},{28,4},{1,25},{... | collective-permute-start | bytes 393224 | tf_op jit(solution)/shard_map/ppermute | solution.py:266
  106.1 12.4 %copy-start.20 = (bf16[256,1024]{1,0:T(8,128)(2,1)}, bf16[256,1024]{1,0:T(8,128)(2,1)S(1)}, u32[]{:S(2)}) copy-start(bf16[256,1024]{1,0:T(8,128)(2,1)S(1)} %get-tuple-element.107.refs_4_) | copy-start | bytes 1572868
  106.1 12.4 %copy-start.22 = (bf16[256,1024]{1,0:T(8,128)(2,1)}, bf16[256,1024]{1,0:T(8,128)(2,1)S(1)}, u32[]{:S(2)}) copy-start(bf16[256,1024]{1,0:T(8,128)(2,1)S(1)} %get-tuple-element.108.refs_5_) | copy-start | bytes 1572868
  106.1 12.4 %copy-start.24 = (bf16[256,1024]{1,0:T(8,128)(2,1)}, bf16[256,1024]{1,0:T(8,128)(2,1)S(1)}, u32[]{:S(2)}) copy-start(bf16[256,1024]{1,0:T(8,128)(2,1)S(1)} %get-tuple-element.98.refs_13_) | copy-start | bytes 1572868
  106.1 12.4 %copy-start.26 = (bf16[256,1024]{1,0:T(8,128)(2,1)}, bf16[256,1024]{1,0:T(8,128)(2,1)S(1)}, u32[]{:S(2)}) copy-start(bf16[256,1024]{1,0:T(8,128)(2,1)S(1)} %get-tuple-element.99.refs_14_) | copy-start | bytes 1572868
  109.7 4.3 %collective-permute-start.32 = (f32[4,128,256]{2,1,0:T(8,128)S(1)}, f32[4,128,256]{2,1,0:T(8,128)S(1)}, u32[]{:S(2)}, u32[]{:S(2)}) collective-permute-start(f32[4,128,256]{2,1,0:T(8,128)S(1)} %pad_maximum_fusion.3.fb), channel_id=1, source_target_pairs={{0,4},{4,0},{8,12},{12,8},{16,20},{20,16},{24,28},{28,24},{1,5},{5... | collective-permute-start | bytes 1572872 | tf_op jit(solution)/shard_map/ppermute | solution.py:269
  109.8 4.1 %collective-permute-start.31 = (f32[4,128,256]{2,1,0:T(8,128)S(1)}, f32[4,128,256]{2,1,0:T(8,128)S(1)}, u32[]{:S(2)}, u32[]{:S(2)}) collective-permute-start(f32[4,128,256]{2,1,0:T(8,128)S(1)} %slice.79), channel_id=1, source_target_pairs={{0,4},{4,0},{8,12},{12,8},{16,20},{20,16},{24,28},{28,24},{1,5},{5... | collective-permute-start | bytes 1572872 | tf_op jit(solution)/shard_map/ppermute | solution.py:269
  110.4 11.1 %collective-permute-start.33 = (f32[64,256]{1,0:T(8,128)S(1)}, f32[64,256]{1,0:T(8,128)S(1)}, u32[]{:S(2)}, u32[]{:S(2)}) collective-permute-start(f32[64,256]{1,0:T(8,128)S(1)} %get-tuple-element.127), channel_id=1, source_target_pairs={{0,8},{4,12},{8,0},{12,4},{16,24},{20,28},{24,16},{28,20},{1,9},{5... | collective-permute-start | bytes 196616 | tf_op jit(solution)/shard_map/ppermute | solution.py:266
  111.3 10.2 %collective-permute-start.34 = (f32[64,256]{1,0:T(8,128)S(1)}, f32[64,256]{1,0:T(8,128)S(1)}, u32[]{:S(2)}, u32[]{:S(2)}) collective-permute-start(f32[64,256]{1,0:T(8,128)S(1)} %get-tuple-element.126), channel_id=1, source_target_pairs={{0,16},{4,20},{8,24},{12,28},{16,0},{20,4},{24,8},{28,12},{1,17},{... | collective-permute-start | bytes 196616 | tf_op jit(solution)/shard_map/ppermute | solution.py:266
  112.7 8.8 %collective-permute-start.35 = (f32[64,256]{1,0:T(8,128)S(1)}, f32[64,256]{1,0:T(8,128)S(1)}, u32[]{:S(2)}, u32[]{:S(2)}) collective-permute-start(f32[64,256]{1,0:T(8,128)S(1)} %get-tuple-element.125), channel_id=1, source_target_pairs={{0,24},{4,28},{8,16},{12,20},{16,8},{20,12},{24,0},{28,4},{1,25},{... | collective-permute-start | bytes 196616 | tf_op jit(solution)/shard_map/ppermute | solution.py:266
  113.9 17.5 %copy-start.7 = (bf16[512,1024]{1,0:T(8,128)(2,1)S(1)}, bf16[512,1024]{1,0:T(8,128)(2,1)}, u32[]{:S(2)}) copy-start(bf16[512,1024]{1,0:T(8,128)(2,1)} %copy-done.6) | copy-start | bytes 3145732
  122.1 9.3 %collective-permute-start.36 = (f32[64,256]{1,0:T(8,128)}, f32[64,256]{1,0:T(8,128)}, u32[]{:S(2)}, u32[]{:S(2)}) collective-permute-start(f32[64,256]{1,0:T(8,128)} %fusion.6.refs_4_), channel_id=1, source_target_pairs={{0,8},{4,12},{8,0},{12,4},{16,24},{20,28},{24,16},{28,20},{1,9},{5... | collective-permute-start | bytes 196616 | tf_op jit(solution)/shard_map/ppermute | solution.py:266
  122.9 8.5 %collective-permute-start.37 = (f32[64,256]{1,0:T(8,128)}, f32[64,256]{1,0:T(8,128)}, u32[]{:S(2)}, u32[]{:S(2)}) collective-permute-start(f32[64,256]{1,0:T(8,128)} %fusion.6.refs_4_), channel_id=1, source_target_pairs={{0,16},{4,20},{8,24},{12,28},{16,0},{20,4},{24,8},{28,12},{1,17},{... | collective-permute-start | bytes 196616 | tf_op jit(solution)/shard_map/ppermute | solution.py:266
  124.4 7.0 %collective-permute-start.38 = (f32[64,256]{1,0:T(8,128)}, f32[64,256]{1,0:T(8,128)}, u32[]{:S(2)}, u32[]{:S(2)}) collective-permute-start(f32[64,256]{1,0:T(8,128)} %fusion.6.refs_4_), channel_id=1, source_target_pairs={{0,24},{4,28},{8,16},{12,20},{16,8},{20,12},{24,0},{28,4},{1,25},{... | collective-permute-start | bytes 196616 | tf_op jit(solution)/shard_map/ppermute | solution.py:266
  128.3 3.1 %copy-start.25 = (bf16[256,1024]{1,0:T(8,128)(2,1)S(1)}, bf16[256,1024]{1,0:T(8,128)(2,1)}, u32[]{:S(2)}) copy-start(bf16[256,1024]{1,0:T(8,128)(2,1)} %copy-done.24) | copy-start | bytes 1572868
  133.5 8.5 %copy-start.5 = (bf16[512,1024]{1,0:T(8,128)(2,1)S(1)}, bf16[512,1024]{1,0:T(8,128)(2,1)}, u32[]{:S(2)}) copy-start(bf16[512,1024]{1,0:T(8,128)(2,1)} %copy-done.4) | copy-start | bytes 3145732
  133.5 8.5 %copy-start.13 = (bf16[256,1024]{1,0:T(8,128)(2,1)S(1)}, bf16[256,1024]{1,0:T(8,128)(2,1)}, u32[]{:S(2)}) copy-start(bf16[256,1024]{1,0:T(8,128)(2,1)} %copy-done.12) | copy-start | bytes 1572868
  133.5 8.5 %copy-start.15 = (bf16[256,1024]{1,0:T(8,128)(2,1)S(1)}, bf16[256,1024]{1,0:T(8,128)(2,1)}, u32[]{:S(2)}) copy-start(bf16[256,1024]{1,0:T(8,128)(2,1)} %copy-done.14) | copy-start | bytes 1572868
  133.5 8.5 %copy-start.21 = (bf16[256,1024]{1,0:T(8,128)(2,1)S(1)}, bf16[256,1024]{1,0:T(8,128)(2,1)}, u32[]{:S(2)}) copy-start(bf16[256,1024]{1,0:T(8,128)(2,1)} %copy-done.20) | copy-start | bytes 1572868
  133.5 8.5 %copy-start.23 = (bf16[256,1024]{1,0:T(8,128)(2,1)S(1)}, bf16[256,1024]{1,0:T(8,128)(2,1)}, u32[]{:S(2)}) copy-start(bf16[256,1024]{1,0:T(8,128)(2,1)} %copy-done.22) | copy-start | bytes 1572868
  138.3 3.7 %copy-start.3 = (bf16[512,1024]{1,0:T(8,128)(2,1)S(1)}, bf16[512,1024]{1,0:T(8,128)(2,1)}, u32[]{:S(2)}) copy-start(bf16[512,1024]{1,0:T(8,128)(2,1)} %copy-done.2) | copy-start | bytes 3145732
  138.4 9.3 %collective-permute-start.39 = (f32[64,1024]{1,0:T(8,128)S(1)}, f32[64,1024]{1,0:T(8,128)S(1)}, u32[]{:S(2)}, u32[]{:S(2)}) collective-permute-start(f32[64,1024]{1,0:T(8,128)S(1)} %get-tuple-element.118), channel_id=1, source_target_pairs={{0,8},{4,12},{8,0},{12,4},{16,24},{20,28},{24,16},{28,20},{1,9},{5... | collective-permute-start | bytes 786440 | tf_op jit(solution)/shard_map/ppermute | solution.py:266
  139.3 12.6 %collective-permute-start.40 = (f32[64,1024]{1,0:T(8,128)S(1)}, f32[64,1024]{1,0:T(8,128)S(1)}, u32[]{:S(2)}, u32[]{:S(2)}) collective-permute-start(f32[64,1024]{1,0:T(8,128)S(1)} %get-tuple-element.117), channel_id=1, source_target_pairs={{0,16},{4,20},{8,24},{12,28},{16,0},{20,4},{24,8},{28,12},{1,17},{... | collective-permute-start | bytes 786440 | tf_op jit(solution)/shard_map/ppermute | solution.py:266
  140.7 13.1 %collective-permute-start.41 = (f32[64,1024]{1,0:T(8,128)S(1)}, f32[64,1024]{1,0:T(8,128)S(1)}, u32[]{:S(2)}, u32[]{:S(2)}) collective-permute-start(f32[64,1024]{1,0:T(8,128)S(1)} %get-tuple-element.116), channel_id=1, source_target_pairs={{0,24},{4,28},{8,16},{12,20},{16,8},{20,12},{24,0},{28,4},{1,25},{... | collective-permute-start | bytes 786440 | tf_op jit(solution)/shard_map/ppermute | solution.py:266
  144.5 14.5 %collective-permute-start.42 = (f32[64,1024]{1,0:T(8,128)S(1)}, f32[64,1024]{1,0:T(8,128)S(1)}, u32[]{:S(2)}, u32[]{:S(2)}) collective-permute-start(f32[64,1024]{1,0:T(8,128)S(1)} %get-tuple-element.115), channel_id=1, source_target_pairs={{0,8},{4,12},{8,0},{12,4},{16,24},{20,28},{24,16},{28,20},{1,9},{5... | collective-permute-start | bytes 786440 | tf_op jit(solution)/shard_map/ppermute | solution.py:266
  145.3 17.2 %collective-permute-start.43 = (f32[64,1024]{1,0:T(8,128)S(1)}, f32[64,1024]{1,0:T(8,128)S(1)}, u32[]{:S(2)}, u32[]{:S(2)}) collective-permute-start(f32[64,1024]{1,0:T(8,128)S(1)} %get-tuple-element.114), channel_id=1, source_target_pairs={{0,16},{4,20},{8,24},{12,28},{16,0},{20,4},{24,8},{28,12},{1,17},{... | collective-permute-start | bytes 786440 | tf_op jit(solution)/shard_map/ppermute | solution.py:266
  147.7 14.8 %collective-permute-start.44 = (f32[64,1024]{1,0:T(8,128)S(1)}, f32[64,1024]{1,0:T(8,128)S(1)}, u32[]{:S(2)}, u32[]{:S(2)}) collective-permute-start(f32[64,1024]{1,0:T(8,128)S(1)} %get-tuple-element.113), channel_id=1, source_target_pairs={{0,24},{4,28},{8,16},{12,20},{16,8},{20,12},{24,0},{28,4},{1,25},{... | collective-permute-start | bytes 786440 | tf_op jit(solution)/shard_map/ppermute | solution.py:266
  (13 other events, 20.4 us)
